TPU v7x, 32 devices: a whole 2x2x4 slice. The times are simulated.
32 devices in a mesh: dp: 8 (over y, x, core), mp: 4 (over z).
Axes of the slice: x: 2, y: 2, z: 4, core: 2. Of those that a mesh axis runs over, the one named last changes fastest.
Arguments:
- tokens: bfloat16 [3, 8192, 1024], P(None, ('dp', 'mp')), may hold values from -6 to 6
- first_values: bfloat16 [3, 8192, 1024], P(None, ('dp', 'mp')), may hold values from -6 to 6
- sequences: int32 [3, 8], P(None, 'dp'), may hold values from 1 to 2
- w_query: bfloat16 [1024, 1024], P('dp', 'mp'), may hold values from -0.1875 to 0.1875
- w_key: bfloat16 [1024, 1024], P('dp', 'mp'), may hold values from -0.1875 to 0.1875
- w_value: bfloat16 [1024, 1024], P('dp', 'mp'), may hold values from -0.1875 to 0.1875
- w_out: bfloat16 [1024, 1024], P('dp', 'mp'), may hold values from -4 to 4
- w_gate: bfloat16 [1024, 2816], P('dp', 'mp'), may hold values from -0.1875 to 0.1875
- w_up: bfloat16 [1024, 2816], P('dp', 'mp'), may hold values from -0.1875 to 0.1875
- w_down: bfloat16 [1024, 2816], P('dp', 'mp'), may hold values from -0.109375 to 0.109375
- gain_attn: bfloat16 [1024], P('dp'), may hold values from 0.5 to 1.5
- gain_mlp: bfloat16 [1024], P('dp'), may hold values from 0.5 to 1.5
- cotangent: bfloat16 [3, 8192, 1024], P(None, ('dp', 'mp')), may hold values from -6 to 6
Outputs:
- layer_out: bfloat16 [3, 8192, 1024], P(None, ('dp', 'mp'))
- grad_tokens: float32 [3, 8192, 1024], P(None, ('dp', 'mp'))
- grad_first_values: float32 [3, 8192, 1024], P(None, ('dp', 'mp'))
- grad_w_query: float32 [1024, 1024], P('dp', 'mp')
- grad_w_key: float32 [1024, 1024], P('dp', 'mp')
- grad_w_value: float32 [1024, 1024], P('dp', 'mp')
- grad_w_out: float32 [1024, 1024], P('dp', 'mp')
- grad_w_gate: float32 [1024, 2816], P('dp', 'mp')
- grad_w_up: float32 [1024, 2816], P('dp', 'mp')
- grad_w_down: float32 [1024, 2816], P('dp', 'mp')
- grad_gain_attn: float32 [1024], P(('dp', 'mp'))
- grad_gain_mlp: float32 [1024], P(('dp', 'mp'))
Inputs may be any that keep to these rules, and one draw needn't show every extreme that they name: A block with 1 holds one sequence of 1024 tokens; a block with 2 holds two sequences of 512 tokens, the second starting at the block's middle.
All inputs are finite; a program needn't handle non-finite values.
Results may differ from a plain program's by a relative error of at most 0.023.
Values may be sent and summed in bfloat16 or wider, within the bound.
A program may use at most 320 MiB of HBM per device.

v0:
```python
import jax
import jax.numpy as jnp
from jax import lax
from jax.sharding import PartitionSpec as P

HEAD_DIM = 64


EPSILON = 1e-06
THETA = 10000.0


def normalize(rows):
    factor = lax.rsqrt(jnp.mean(rows * rows, axis=-1, keepdims=True) + EPSILON)
    return (rows * factor, factor)


def norm_back(grad_normed, normed, factor):
    return factor * (grad_normed - normed * jnp.mean(grad_normed * normed, axis=-1, keepdims=True))


def rotary_tables(position, head_size):
    halfway = head_size // 2
    inverse = THETA ** (-2.0 * jnp.arange(halfway, dtype=jnp.float32) / head_size)
    angles = position.astype(jnp.float32)[:, None] * inverse[None, :]
    return (jnp.cos(angles), jnp.sin(angles))


def rotate(values, cosine, sine, direction):
    halfway = values.shape[-1] // 2
    former = values[..., :halfway]
    latter = values[..., halfway:]
    cos_rows = cosine[:, None, :]
    sin_rows = direction * sine[:, None, :]
    return jnp.concatenate(
        [former * cos_rows - latter * sin_rows, latter * cos_rows + former * sin_rows], axis=-1
    )


def layout(packed, length):
    index_rows = jnp.arange(length, dtype=jnp.int32)
    second = jnp.where((packed == 2) & (index_rows >= length // 2), 1, 0).astype(jnp.int32)
    return (second, index_rows - second * (length // 2))


def block_scores(query, key_rows, second, offset, block_rows, key_end, scale):
    raw = (
        jnp.einsum(
            "qhd,khd->hqk",
            query[offset : offset + block_rows],
            key_rows,
            preferred_element_type=jnp.float32,
        )
        * scale
    )
    row_ids = offset + jnp.arange(block_rows, dtype=jnp.int32)
    col_ids = jnp.arange(key_end, dtype=jnp.int32)
    allowed = (col_ids[None, :] <= row_ids[:, None]) & (
        second[offset : offset + block_rows][:, None] == second[None, :]
    )
    return jnp.where(allowed[None], raw, -1e30)


def whole_rows(part):
    return lax.all_gather(part, "mp", axis=0, tiled=True)


def summed_rows(term, local_rows):
    return lax.psum_scatter(
        term(jnp.int32(0), local_rows * lax.axis_size("mp")).astype(jnp.bfloat16),
        "mp",
        scatter_dimension=0,
        tiled=True,
    ).astype(jnp.float32)


def fetch(w_query, w_key, w_value, w_out, w_gate, w_up, w_down, gain_attn, gain_mlp):
    return (
        lax.all_gather(w_query, "dp", axis=0, tiled=True),
        lax.all_gather(w_key, "dp", axis=0, tiled=True),
        lax.all_gather(w_value, "dp", axis=0, tiled=True),
        lax.all_gather(w_out, "dp", axis=0, tiled=True),
        lax.all_gather(w_gate, "dp", axis=0, tiled=True),
        lax.all_gather(w_up, "dp", axis=0, tiled=True),
        lax.all_gather(w_down, "dp", axis=0, tiled=True),
        lax.all_gather(gain_attn, "dp", axis=0, tiled=True),
        lax.all_gather(gain_mlp, "dp", axis=0, tiled=True),
    )


def project_back(left, right):
    return jnp.einsum("rc,dc->rd", left, right, preferred_element_type=jnp.float32)


def outer_sum(left, right):
    return jnp.einsum("td,tc->dc", left, right, preferred_element_type=jnp.float32)


def body(
    tokens,
    first_values,
    sequences,
    w_query,
    w_key,
    w_value,
    w_out,
    w_gate,
    w_up,
    w_down,
    gain_attn,
    gain_mlp,
    cotangent,
):
    micro = tokens.shape[0]
    local_rows = tokens.shape[1]
    length = local_rows * lax.axis_size("mp")
    heads_here = w_query.shape[1] // HEAD_DIM
    block_rows = min(512, length)
    scale = HEAD_DIM ** (-0.5)
    saved = []
    outputs = []
    for batch in range(micro):
        full = fetch(w_query, w_key, w_value, w_out, w_gate, w_up, w_down, gain_attn, gain_mlp)
        q_full, k_full, v_full, o_full, gate_full, up_full, down_full, gain_one, gain_two = full
        gain_one = gain_one.astype(jnp.float32)
        gain_two = gain_two.astype(jnp.float32)
        x_rows = tokens[batch].astype(jnp.float32)
        normed_one, factor_one = normalize(x_rows)
        input_one = whole_rows((normed_one * gain_one[None, :]).astype(jnp.bfloat16))
        second, position = layout(sequences[batch, 0], length)
        cosine, sine = rotary_tables(position, HEAD_DIM)
        query = jnp.dot(input_one, q_full, preferred_element_type=jnp.float32).reshape(
            length, heads_here, HEAD_DIM
        )
        query = rotate(query, cosine, sine, 1.0).astype(jnp.bfloat16)
        key_rows = jnp.dot(input_one, k_full, preferred_element_type=jnp.float32).reshape(
            length, heads_here, HEAD_DIM
        )
        key_rows = rotate(key_rows, cosine, sine, 1.0).astype(jnp.bfloat16)
        first_here = lax.all_to_all(
            first_values[batch], "mp", split_axis=1, concat_axis=0, tiled=True
        )
        mixed = 0.5 * (
            jnp.dot(input_one, v_full, preferred_element_type=jnp.float32)
            + first_here.astype(jnp.float32)
        )
        mixed = mixed.astype(jnp.bfloat16).reshape(length, heads_here, HEAD_DIM)
        pieces = []
        logsums = []
        for offset in range(0, length, block_rows):
            key_end = length
            scores = block_scores(query, key_rows, second, offset, block_rows, key_end, scale)
            highest = jnp.max(scores, axis=-1, keepdims=True)
            powers = jnp.exp(scores - highest)
            denominator = jnp.sum(powers, axis=-1, keepdims=True)
            probs_low = (powers / denominator).astype(jnp.bfloat16)
            logsums.append(highest + jnp.log(denominator))
            pieces.append(
                jnp.einsum("hqk,khd->qhd", probs_low, mixed, preferred_element_type=jnp.float32)
            )
        attended = (
            jnp.concatenate(pieces, axis=0)
            .reshape(length, heads_here * HEAD_DIM)
            .astype(jnp.bfloat16)
        )

        def attn_term(offset, amount):
            return project_back(attended, o_full)

        mid_rows = x_rows + summed_rows(attn_term, local_rows)
        normed_two, factor_two = normalize(mid_rows)
        input_two = whole_rows((normed_two * gain_two[None, :]).astype(jnp.bfloat16))
        gate = jnp.dot(input_two, gate_full, preferred_element_type=jnp.float32)
        upward = jnp.dot(input_two, up_full, preferred_element_type=jnp.float32)
        sigma = jax.nn.sigmoid(gate)
        hidden = (gate * sigma * upward).astype(jnp.bfloat16)

        def mlp_term(offset, amount):
            return project_back(hidden, down_full)

        mlp_rows = summed_rows(mlp_term, local_rows)
        outputs.append((mid_rows + mlp_rows).astype(jnp.bfloat16))
        saved.append(
            (
                normed_one,
                factor_one,
                input_one,
                second,
                cosine,
                sine,
                query,
                key_rows,
                mixed,
                logsums,
                attended,
                normed_two,
                factor_two,
                input_two,
                gate,
                sigma,
                upward,
                hidden,
            )
        )
    grad_sum = None
    gain_grad_one = jnp.zeros((tokens.shape[2],), jnp.float32)
    gain_grad_two = jnp.zeros((tokens.shape[2],), jnp.float32)
    grad_tokens = []
    grad_first = []
    for batch in range(micro):
        (
            normed_one,
            factor_one,
            input_one,
            second,
            cosine,
            sine,
            query,
            key_rows,
            mixed,
            logsums,
            attended,
            normed_two,
            factor_two,
            input_two,
            gate,
            sigma,
            upward,
            hidden,
        ) = saved[batch]
        full = fetch(w_query, w_key, w_value, w_out, w_gate, w_up, w_down, gain_attn, gain_mlp)
        q_full, k_full, v_full, o_full, gate_full, up_full, down_full, gain_one, gain_two = full
        gain_one = gain_one.astype(jnp.float32)
        gain_two = gain_two.astype(jnp.float32)
        grad_rows = cotangent[batch]
        grad_full = whole_rows(grad_rows)
        grad_down = outer_sum(grad_full, hidden)
        grad_hidden = jnp.dot(grad_full, down_full, preferred_element_type=jnp.float32)
        grad_gate = (grad_hidden * upward * sigma * (1.0 + gate * (1.0 - sigma))).astype(
            jnp.bfloat16
        )
        grad_up = (grad_hidden * gate * sigma).astype(jnp.bfloat16)
        grad_gate_w = outer_sum(input_two, grad_gate)
        grad_up_w = outer_sum(input_two, grad_up)

        def mlp_back(offset, amount):
            return project_back(grad_gate, gate_full) + project_back(grad_up, up_full)

        grad_input_two = summed_rows(mlp_back, local_rows)
        gain_grad_two = gain_grad_two + jnp.sum(grad_input_two * normed_two, axis=0)
        grad_mid = grad_rows.astype(jnp.float32) + norm_back(
            grad_input_two * gain_two[None, :], normed_two, factor_two
        )
        grad_attn = whole_rows(grad_mid.astype(jnp.bfloat16))
        grad_out_w = outer_sum(grad_attn, attended)
        grad_attended = jnp.dot(grad_attn, o_full, preferred_element_type=jnp.float32)
        grad_attended = grad_attended.astype(jnp.bfloat16).reshape(length, heads_here, HEAD_DIM)
        grad_mixed = jnp.zeros((length, heads_here, HEAD_DIM), jnp.float32)
        grad_key = jnp.zeros((length, heads_here, HEAD_DIM), jnp.float32)
        query_parts = []
        for turn, offset in enumerate(range(0, length, block_rows)):
            key_end = length
            scores = block_scores(query, key_rows, second, offset, block_rows, key_end, scale)
            probs = jnp.exp(scores - logsums[turn])
            grad_block = grad_attended[offset : offset + block_rows]
            grad_probs = jnp.einsum(
                "qhd,khd->hqk", grad_block, mixed, preferred_element_type=jnp.float32
            )
            grad_mixed = grad_mixed.at[:key_end].add(
                jnp.einsum(
                    "hqk,qhd->khd",
                    probs.astype(jnp.bfloat16),
                    grad_block,
                    preferred_element_type=jnp.float32,
                )
            )
            grad_scores = probs * (grad_probs - jnp.sum(probs * grad_probs, axis=-1, keepdims=True))
            grad_scores = grad_scores.astype(jnp.bfloat16)
            query_parts.append(
                jnp.einsum(
                    "hqk,khd->qhd", grad_scores, key_rows, preferred_element_type=jnp.float32
                )
                * scale
            )
            grad_key = grad_key.at[:key_end].add(
                jnp.einsum(
                    "hqk,qhd->khd",
                    grad_scores,
                    query[offset : offset + block_rows],
                    preferred_element_type=jnp.float32,
                )
                * scale
            )
        grad_mixed_low = grad_mixed.reshape(length, heads_here * HEAD_DIM).astype(jnp.bfloat16)
        grad_value = (0.5 * grad_mixed_low.astype(jnp.float32)).astype(jnp.bfloat16)
        grad_query = rotate(jnp.concatenate(query_parts, axis=0), cosine, sine, -1.0)
        grad_query = grad_query.reshape(length, heads_here * HEAD_DIM).astype(jnp.bfloat16)
        grad_key_low = (
            rotate(grad_key, cosine, sine, -1.0)
            .reshape(length, heads_here * HEAD_DIM)
            .astype(jnp.bfloat16)
        )
        grad_query_w = outer_sum(input_one, grad_query)
        grad_key_w = outer_sum(input_one, grad_key_low)
        grad_value_w = outer_sum(input_one, grad_value)

        def attn_back(offset, amount):
            return (
                project_back(grad_query, q_full)
                + project_back(grad_key_low, k_full)
                + project_back(grad_value, v_full)
            )

        grad_input_one = summed_rows(attn_back, local_rows)
        gain_grad_one = gain_grad_one + jnp.sum(grad_input_one * normed_one, axis=0)
        grad_tokens.append(
            grad_mid + norm_back(grad_input_one * gain_one[None, :], normed_one, factor_one)
        )
        returned = lax.all_to_all(grad_mixed_low, "mp", split_axis=0, concat_axis=1, tiled=True)
        grad_first.append(0.5 * returned.astype(jnp.float32))
        shared = (
            lax.psum_scatter(
                grad_query_w.astype(jnp.bfloat16), "dp", scatter_dimension=0, tiled=True
            ).astype(jnp.float32),
            lax.psum_scatter(
                grad_key_w.astype(jnp.bfloat16), "dp", scatter_dimension=0, tiled=True
            ).astype(jnp.float32),
            lax.psum_scatter(
                grad_value_w.astype(jnp.bfloat16), "dp", scatter_dimension=0, tiled=True
            ).astype(jnp.float32),
            lax.psum_scatter(
                grad_out_w.astype(jnp.bfloat16), "dp", scatter_dimension=0, tiled=True
            ).astype(jnp.float32),
            lax.psum_scatter(
                grad_gate_w.astype(jnp.bfloat16), "dp", scatter_dimension=0, tiled=True
            ).astype(jnp.float32),
            lax.psum_scatter(
                grad_up_w.astype(jnp.bfloat16), "dp", scatter_dimension=0, tiled=True
            ).astype(jnp.float32),
            lax.psum_scatter(
                grad_down.astype(jnp.bfloat16), "dp", scatter_dimension=0, tiled=True
            ).astype(jnp.float32),
        )
        grad_sum = shared if grad_sum is None else jax.tree.map(jnp.add, grad_sum, shared)
    gain_parts = (
        lax.psum_scatter(gain_grad_one, ("dp", "mp"), scatter_dimension=0, tiled=True),
        lax.psum_scatter(gain_grad_two, ("dp", "mp"), scatter_dimension=0, tiled=True),
    )
    return (
        jnp.stack(outputs),
        jnp.stack(grad_tokens),
        jnp.stack(grad_first),
        grad_sum[0],
        grad_sum[1],
        grad_sum[2],
        grad_sum[3],
        grad_sum[4],
        grad_sum[5],
        grad_sum[6],
        gain_parts[0],
        gain_parts[1],
    )


def solution(mesh):
    return jax.shard_map(
        body,
        mesh=mesh,
        in_specs=(
            P(None, ("dp", "mp"), None),
            P(None, ("dp", "mp"), None),
            P(None, "dp"),
            P("dp", "mp"),
            P("dp", "mp"),
            P("dp", "mp"),
            P("dp", "mp"),
            P("dp", "mp"),
            P("dp", "mp"),
            P("dp", "mp"),
            P("dp"),
            P("dp"),
            P(None, ("dp", "mp"), None),
        ),
        out_specs=(
            P(None, ("dp", "mp"), None),
            P(None, ("dp", "mp"), None),
            P(None, ("dp", "mp"), None),
            P("dp", "mp"),
            P("dp", "mp"),
            P("dp", "mp"),
            P("dp", "mp"),
            P("dp", "mp"),
            P("dp", "mp"),
            P("dp", "mp"),
            P(("dp", "mp")),
            P(("dp", "mp")),
        ),
        check_vma=False,
    )
```

profile of v0, /device:TPU:0, one launch (start us, length us, event | category | flops | bytes accessed | tf_op | source)
XLA Modules:
  0.0 2012.4 jit_solution(3197105828252842754)
XLA Ops:
  9.9 10.3 all-gather.3
  33.9 9.9 all_gather.45
  43.8 9.0 all_gather.46
  52.7 9.7 all_gather.44
  71.4 9.0 all_gather.47
  84.1 6.6 all-to-all-done
  98.9 25.1 %all-to-all-done.2 = bf16[256,4,256]{0,2,1:T(8,128)(2,1)} async-done(((bf16[256,4,256]{0,2,1:T(8,128)(2,1)}), bf16[256,4,256]{0,2,1:T(8,128)(2,1)}, u32[]{:S(2)}, u32[]{:S(2)}) %all-to-all-start.2) | async-done | bytes 524320 | tf_op jit(solution)/shard_map/all_to_all | solution.py:140
  166.4 23.4 %all-gather.21.cloned.1.call-done = bf16[1024,1024]{1,0:T(8,128)(2,1)} async-done(((bf16[256,1024]{1,0:T(8,128)(2,1)}), bf16[1024,1024]{1,0:T(8,128)(2,1)}) %all-gather.21.cloned.1.call-update) | async-done | bytes 2097168 | tf_op jit(solution)/shard_map/all_gather | solution.py:65
  210.2 8.7 all-gather.4
  218.9 16.2 reduce-scatter.56.cloned.1.call-done
  235.1 45.5 %reduce-scatter.60.cloned.1.call-done = bf16[256,1024]{1,0:T(8,128)(2,1)} async-done(((bf16[1024,1024]{1,0:T(8,128)(2,1)}), bf16[256,1024]{1,0:T(8,128)(2,1)}) %reduce-scatter.60.cloned.1.call-update) | async-done | bytes 524304 | tf_op jit(solution)/shard_map/reduce_scatter | solution.py:69
  280.6 45.9 %reduce-scatter.52.cloned.1.call-done = bf16[256,1024]{1,0:T(8,128)(2,1)} async-done(((bf16[1024,1024]{1,0:T(8,128)(2,1)}), bf16[256,1024]{1,0:T(8,128)(2,1)}) %reduce-scatter.52.cloned.1.call-update) | async-done | bytes 524304 | tf_op jit(solution)/shard_map/reduce_scatter | solution.py:69
  335.6 39.7 %all-gather.37.cloned.1.call-done = bf16[1024,1024]{1,0:T(8,128)(2,1)} async-done(((bf16[256,1024]{1,0:T(8,128)(2,1)}), bf16[1024,1024]{1,0:T(8,128)(2,1)}) %all-gather.37.cloned.1.call-update) | async-done | bytes 2097168 | tf_op jit(solution)/shard_map/all_gather | solution.py:65
  380.6 20.6 %all-gather.25.cloned.1.call-done = bf16[1024,704]{0,1:T(8,128)(2,1)} async-done(((bf16[128,704]{0,1:T(8,128)(2,1)}), bf16[1024,704]{0,1:T(8,128)(2,1)}) %all-gather.25.cloned.1.call-update) | async-done | bytes 1441808 | tf_op jit(solution)/shard_map/all_gather | solution.py:83
  406.4 21.9 %all-gather.29.cloned.1.call-done = bf16[1024,704]{0,1:T(8,128)(2,1)} async-done(((bf16[128,704]{0,1:T(8,128)(2,1)}), bf16[1024,704]{0,1:T(8,128)(2,1)}) %all-gather.29.cloned.1.call-update) | async-done | bytes 1441808 | tf_op jit(solution)/shard_map/all_gather | solution.py:85
  428.4 47.3 %all-gather.49.cloned.1.call-done = bf16[1,1024,1024]{2,1,0:T(8,128)(2,1)} async-done(((bf16[1,256,1024]{2,1,0:T(8,128)(2,1)}), bf16[1,1024,1024]{2,1,0:T(8,128)(2,1)}) %all-gather.49.cloned.1.call-update) | async-done | bytes 2097168 | tf_op jit(solution)/shard_map/all_gather | solution.py:65
  475.6 7.7 multiply_convert_fusion.6
  489.4 55.0 %all-gather.33.cloned.1.call-done = bf16[1024,1024]{1,0:T(8,128)(2,1)} async-done(((bf16[256,1024]{1,0:T(8,128)(2,1)}), bf16[1024,1024]{1,0:T(8,128)(2,1)}) %all-gather.33.cloned.1.call-update) | async-done | bytes 2097168 | tf_op jit(solution)/shard_map/all_gather | solution.py:65
  544.5 5.4 fusion.241
  553.2 37.3 %all-gather.47.cloned.1.call-done = bf16[1,1024,1024]{2,1,0:T(8,128)(2,1)} async-done(((bf16[1,256,1024]{2,1,0:T(8,128)(2,1)}), bf16[1,1024,1024]{2,1,0:T(8,128)(2,1)}) %all-gather.47.cloned.1.call-update) | async-done | bytes 2097168 | tf_op jit(solution)/shard_map/all_gather | solution.py:65
  590.5 7.7 multiply_convert_fusion.8
  604.0 55.2 %all-gather.23.cloned.1.call-done = bf16[1024,1024]{1,0:T(8,128)(2,1)} async-done(((bf16[256,1024]{1,0:T(8,128)(2,1)}), bf16[1024,1024]{1,0:T(8,128)(2,1)}) %all-gather.23.cloned.1.call-update) | async-done | bytes 2097168 | tf_op jit(solution)/shard_map/all_gather | solution.py:65
  667.9 37.3 %all-gather.45.cloned.1.call-done = bf16[1,1024,1024]{2,1,0:T(8,128)(2,1)} async-done(((bf16[1,256,1024]{2,1,0:T(8,128)(2,1)}), bf16[1,1024,1024]{2,1,0:T(8,128)(2,1)}) %all-gather.45.cloned.1.call-update) | async-done | bytes 2097168 | tf_op jit(solution)/shard_map/all_gather | solution.py:65
  705.2 7.7 multiply_convert_fusion.10
  718.6 42.7 %reduce-scatter.64.cloned.1.call-done = bf16[256,1024]{1,0:T(8,128)(2,1)} async-done(((bf16[1024,1024]{1,0:T(8,128)(2,1)}), bf16[256,1024]{1,0:T(8,128)(2,1)}) %reduce-scatter.64.cloned.1.call-update) | async-done | bytes 524304 | tf_op jit(solution)/shard_map/reduce_scatter | solution.py:69
  818.0 40.3 %all-gather.43.cloned.1.call-done = bf16[1024,1024]{1,0:T(8,128)(2,1)} async-done(((bf16[256,1024]{1,0:T(8,128)(2,1)}), bf16[1024,1024]{1,0:T(8,128)(2,1)}) %all-gather.43.cloned.1.call-update) | async-done | bytes 2097168 | tf_op jit(solution)/shard_map/all_gather | solution.py:65
  861.6 5.6 multiply_reduce_fusion.5
  877.9 5.4 fusion.133
  887.8 5.4 fusion.136
  906.8 7.4 multiply_convert_fusion
  919.3 5.9 fusion.12
  925.3 5.5 multiply_reduce_fusion.3
  938.9 6.0 fusion.20
  944.9 6.0 fusion.16
  952.5 6.6 multiply_convert_fusion.16
  961.9 6.2 multiply_convert_fusion.15
  971.7 6.2 multiply_convert_fusion.17
  1004.6 6.9 multiply_reduce_fusion.2
  1011.8 6.9 multiply_convert_fusion.2
  1067.6 13.3 all-to-all-done.4
  1094.1 18.5 reduce-scatter.102.cloned.1.call-done
  1113.7 40.6 %reduce-scatter.108.cloned.1.call-done = bf16[128,704]{1,0:T(8,128)(2,1)} async-done(((bf16[1024,704]{1,0:T(8,128)(2,1)}), bf16[128,704]{1,0:T(8,128)(2,1)}) %reduce-scatter.108.cloned.1.call-update) | async-done | bytes 180240
  1155.4 40.4 %reduce-scatter.112.cloned.1.call-done = bf16[128,704]{1,0:T(8,128)(2,1)} async-done(((bf16[1024,704]{1,0:T(8,128)(2,1)}), bf16[128,704]{1,0:T(8,128)(2,1)}) %reduce-scatter.112.cloned.1.call-update) | async-done | bytes 180240
  1196.9 40.6 %reduce-scatter.100.cloned.1.call-done = bf16[128,704]{1,0:T(8,128)(2,1)} async-done(((bf16[1024,704]{1,0:T(8,128)(2,1)}), bf16[128,704]{1,0:T(8,128)(2,1)}) %reduce-scatter.100.cloned.1.call-update) | async-done | bytes 180240
  1238.5 40.4 %reduce-scatter.106.cloned.1.call-done = bf16[128,704]{1,0:T(8,128)(2,1)} async-done(((bf16[1024,704]{1,0:T(8,128)(2,1)}), bf16[128,704]{1,0:T(8,128)(2,1)}) %reduce-scatter.106.cloned.1.call-update) | async-done | bytes 180240
  1290.4 11.8 all-to-all-done.3
  1308.3 7.7 reduce-scatter.94.cloned.1.call-done
  1316.1 37.4 %reduce-scatter.98.cloned.1.call-done = bf16[128,256]{1,0:T(8,128)(2,1)} async-done(((bf16[1024,256]{1,0:T(8,128)(2,1)}), bf16[128,256]{1,0:T(8,128)(2,1)}) %reduce-scatter.98.cloned.1.call-update) | async-done | bytes 65552 | tf_op jit(solution)/shard_map/reduce_scatter | solution.py:331
  1353.5 37.2 %reduce-scatter.96.cloned.1.call-done = bf16[128,256]{1,0:T(8,128)(2,1)} async-done(((bf16[1024,256]{1,0:T(8,128)(2,1)}), bf16[128,256]{1,0:T(8,128)(2,1)}) %reduce-scatter.96.cloned.1.call-update) | async-done | bytes 65552 | tf_op jit(solution)/shard_map/reduce_scatter | solution.py:331
  1392.3 35.8 %reduce-scatter.90.cloned.1.call-done = bf16[128,256]{1,0:T(8,128)(2,1)} async-done(((bf16[1024,256]{1,0:T(8,128)(2,1)}), bf16[128,256]{1,0:T(8,128)(2,1)}) %reduce-scatter.90.cloned.1.call-update) | async-done | bytes 65552 | tf_op jit(solution)/shard_map/reduce_scatter | solution.py:328
  1428.1 37.3 %reduce-scatter.92.cloned.1.call-done = bf16[128,256]{1,0:T(8,128)(2,1)} async-done(((bf16[1024,256]{1,0:T(8,128)(2,1)}), bf16[128,256]{1,0:T(8,128)(2,1)}) %reduce-scatter.92.cloned.1.call-update) | async-done | bytes 65552 | tf_op jit(solution)/shard_map/reduce_scatter | solution.py:328
  1465.4 37.5 %reduce-scatter.88.cloned.1.call-done = bf16[128,256]{1,0:T(8,128)(2,1)} async-done(((bf16[1024,256]{1,0:T(8,128)(2,1)}), bf16[128,256]{1,0:T(8,128)(2,1)}) %reduce-scatter.88.cloned.1.call-update) | async-done | bytes 65552 | tf_op jit(solution)/shard_map/reduce_scatter | solution.py:328
  1504.5 35.5 %reduce-scatter.82.cloned.1.call-done = bf16[128,256]{1,0:T(8,128)(2,1)} async-done(((bf16[1024,256]{1,0:T(8,128)(2,1)}), bf16[128,256]{1,0:T(8,128)(2,1)}) %reduce-scatter.82.cloned.1.call-update) | async-done | bytes 65552 | tf_op jit(solution)/shard_map/reduce_scatter | solution.py:325
  1540.0 37.4 %reduce-scatter.86.cloned.1.call-done = bf16[128,256]{1,0:T(8,128)(2,1)} async-done(((bf16[1024,256]{1,0:T(8,128)(2,1)}), bf16[128,256]{1,0:T(8,128)(2,1)}) %reduce-scatter.86.cloned.1.call-update) | async-done | bytes 65552 | tf_op jit(solution)/shard_map/reduce_scatter | solution.py:325
  1577.4 37.3 %reduce-scatter.84.cloned.1.call-done = bf16[128,256]{1,0:T(8,128)(2,1)} async-done(((bf16[1024,256]{1,0:T(8,128)(2,1)}), bf16[128,256]{1,0:T(8,128)(2,1)}) %reduce-scatter.84.cloned.1.call-update) | async-done | bytes 65552 | tf_op jit(solution)/shard_map/reduce_scatter | solution.py:325
  1616.3 35.8 %reduce-scatter.76.cloned.1.call-done = bf16[128,256]{1,0:T(8,128)(2,1)} async-done(((bf16[1024,256]{1,0:T(8,128)(2,1)}), bf16[128,256]{1,0:T(8,128)(2,1)}) %reduce-scatter.76.cloned.1.call-update) | async-done | bytes 65552 | tf_op jit(solution)/shard_map/reduce_scatter | solution.py:322
  1652.1 37.1 %reduce-scatter.80.cloned.1.call-done = bf16[128,256]{1,0:T(8,128)(2,1)} async-done(((bf16[1024,256]{1,0:T(8,128)(2,1)}), bf16[128,256]{1,0:T(8,128)(2,1)}) %reduce-scatter.80.cloned.1.call-update) | async-done | bytes 65552 | tf_op jit(solution)/shard_map/reduce_scatter | solution.py:322
  1689.2 37.5 %reduce-scatter.78.cloned.1.call-done = bf16[128,256]{1,0:T(8,128)(2,1)} async-done(((bf16[1024,256]{1,0:T(8,128)(2,1)}), bf16[128,256]{1,0:T(8,128)(2,1)}) %reduce-scatter.78.cloned.1.call-update) | async-done | bytes 65552 | tf_op jit(solution)/shard_map/reduce_scatter | solution.py:322
  1728.3 44.1 %reduce-scatter.66.cloned.1.call-done = bf16[256,1024]{1,0:T(8,128)(2,1)} async-done(((bf16[1024,1024]{1,0:T(8,128)(2,1)}), bf16[256,1024]{1,0:T(8,128)(2,1)}) %reduce-scatter.66.cloned.1.call-update) | async-done | bytes 524304 | tf_op jit(solution)/shard_map/reduce_scatter | solution.py:69
  1772.4 45.6 %reduce-scatter.74.cloned.1.call-done = bf16[256,1024]{1,0:T(8,128)(2,1)} async-done(((bf16[1024,1024]{1,0:T(8,128)(2,1)}), bf16[256,1024]{1,0:T(8,128)(2,1)}) %reduce-scatter.74.cloned.1.call-update) | async-done | bytes 524304 | tf_op jit(solution)/shard_map/reduce_scatter | solution.py:69
  1818.0 45.1 %reduce-scatter.70.cloned.1.call-done = bf16[256,1024]{1,0:T(8,128)(2,1)} async-done(((bf16[1024,1024]{1,0:T(8,128)(2,1)}), bf16[256,1024]{1,0:T(8,128)(2,1)}) %reduce-scatter.70.cloned.1.call-update) | async-done | bytes 524304 | tf_op jit(solution)/shard_map/reduce_scatter | solution.py:69
  1865.6 43.4 %all-reduce.2 = (f32[1024]{0:T(1024)S(1)}, f32[1024]{0:T(1024)S(1)}) all-reduce(f32[1024]{0:T(1024)S(1)} %add_add_fusion.1, f32[1024]{0:T(1024)S(1)} %add_add_fusion), channel_id=38, replica_groups=mesh['dp'=8,'mp'=4] {'dp','mp'}, use_global_device_ids=true, to_apply=%region_66.67.clone | all-reduce | flops 2048 | bytes 16384
  1913.6 40.6 %reduce-scatter.58.cloned.1.call-done = bf16[256,1024]{1,0:T(8,128)(2,1)} async-done(((bf16[1024,1024]{1,0:T(8,128)(2,1)}), bf16[256,1024]{1,0:T(8,128)(2,1)}) %reduce-scatter.58.cloned.1.call-update) | async-done | bytes 524304 | tf_op jit(solution)/shard_map/reduce_scatter | solution.py:69
  1957.6 41.7 %reduce-scatter.54.cloned.1.call-done = bf16[256,1024]{1,0:T(8,128)(2,1)} async-done(((bf16[1024,1024]{1,0:T(8,128)(2,1)}), bf16[256,1024]{1,0:T(8,128)(2,1)}) %reduce-scatter.54.cloned.1.call-update) | async-done | bytes 524304 | tf_op jit(solution)/shard_map/reduce_scatter | solution.py:69
  (764 shorter events, 386.7 us)
Async XLA Ops:
  8.0 118.2 %all-gather.31.cloned.1.call-start = ((), (), s32[]{:S(2)}) async-start(), calls=%async_computation.46 | async-start | bytes 2621440 | tf_op jit(solution)/shard_map/all_gather | solution.py:65
  23.7 122.6 %all-gather.35.cloned.1.call-start = ((), (), s32[]{:S(2)}) async-start(), calls=%async_computation.50 | async-start | bytes 2621440 | tf_op jit(solution)/shard_map/all_gather | solution.py:65
  25.6 40.7 %all-to-all-start.1 = ((bf16[256,4,256]{0,2,1:T(8,128)(2,1)}), bf16[256,4,256]{0,2,1:T(8,128)(2,1)S(1)}, u32[]{:S(2)}, u32[]{:S(2)}) async-start(bf16[256,4,256]{0,2,1:T(8,128)(2,1)} %bitcast.18), calls=%async_computation.3 | async-start | bytes 1048576 | tf_op jit(solution)/shard_map/all_to_all | solution.py:140
  30.5 159.3 %all-gather.21.cloned.1.call-start = ((), (), s32[]{:S(2)}) async-start(), calls=%async_computation.39 | async-start | bytes 2621440 | tf_op jit(solution)/shard_map/all_gather | solution.py:65
  66.3 24.4 %all-to-all-start = ((bf16[256,4,256]{0,2,1:T(8,128)(2,1)}), bf16[256,4,256]{0,2,1:T(8,128)(2,1)S(1)}, u32[]{:S(2)}, u32[]{:S(2)}) async-start(bf16[256,4,256]{0,2,1:T(8,128)(2,1)} %bitcast.4), calls=%async_computation | async-start | bytes 1048576 | tf_op jit(solution)/shard_map/all_to_all | solution.py:140
  90.7 33.3 %all-to-all-start.2 = ((bf16[256,4,256]{0,2,1:T(8,128)(2,1)}), bf16[256,4,256]{0,2,1:T(8,128)(2,1)}, u32[]{:S(2)}, u32[]{:S(2)}) async-start(bf16[256,4,256]{0,2,1:T(8,128)(2,1)} %bitcast.452), calls=%async_computation.6 | async-start | bytes 1048576 | tf_op jit(solution)/shard_map/all_to_all | solution.py:140
  94.8 140.3 %reduce-scatter.56.cloned.1.call-start = ((), (), s32[]{:S(2)}) async-start(), calls=%async_computation.47 | async-start | bytes 2621440 | tf_op jit(solution)/shard_map/reduce_scatter | solution.py:69
  145.7 134.9 %reduce-scatter.60.cloned.1.call-start = ((), (), s32[]{:S(2)}) async-start(), calls=%async_computation.51 | async-start | bytes 2621440 | tf_op jit(solution)/shard_map/reduce_scatter | solution.py:69
  166.2 160.3 %reduce-scatter.52.cloned.1.call-start = ((), (), s32[]{:S(2)}) async-start(), calls=%async_computation.40 | async-start | bytes 2621440 | tf_op jit(solution)/shard_map/reduce_scatter | solution.py:69
  209.6 126.0 %all-gather.27.cloned.1.call-start = ((), (), s32[]{:S(2)}) async-start(), calls=%async_computation.43 | async-start | bytes 1622016 | tf_op jit(solution)/shard_map/all_gather | solution.py:84
  210.1 165.2 %all-gather.37.cloned.1.call-start = ((), (), s32[]{:S(2)}) async-start(), calls=%async_computation.52 | async-start | bytes 2621440 | tf_op jit(solution)/shard_map/all_gather | solution.py:65
  218.9 546.2 %copy-start.132 = (f32[8,1,128]{2,1,0:T(1,128)}, f32[8,1,128]{2,1,0:T(1,128)S(1)}, u32[]{:S(2)}) copy-start(f32[8,1,128]{2,1,0:T(1,128)S(1)} %convert_element_type.739) | copy-start | bytes 12292
  330.3 70.9 %all-gather.25.cloned.1.call-start = ((), (), s32[]{:S(2)}) async-start(), calls=%async_computation.42 | async-start | bytes 1622016 | tf_op jit(solution)/shard_map/all_gather | solution.py:83
  330.9 97.5 %all-gather.29.cloned.1.call-start = ((), (), s32[]{:S(2)}) async-start(), calls=%async_computation.44 | async-start | bytes 1622016 | tf_op jit(solution)/shard_map/all_gather | solution.py:85
  331.6 144.0 %all-gather.49.cloned.1.call-start = ((), (), s32[]{:S(2)}) async-start(), calls=%async_computation.77 | async-start | bytes 2621440 | tf_op jit(solution)/shard_map/all_gather | solution.py:65
  333.0 211.5 %all-gather.33.cloned.1.call-start = ((), (), s32[]{:S(2)}) async-start(), calls=%async_computation.48 | async-start | bytes 2621440 | tf_op jit(solution)/shard_map/all_gather | solution.py:65
  333.7 256.8 %all-gather.47.cloned.1.call-start = ((), (), s32[]{:S(2)}) async-start(), calls=%async_computation.76 | async-start | bytes 2621440 | tf_op jit(solution)/shard_map/all_gather | solution.py:65
  334.3 324.9 %all-gather.23.cloned.1.call-start = ((), (), s32[]{:S(2)}) async-start(), calls=%async_computation.41 | async-start | bytes 2621440 | tf_op jit(solution)/shard_map/all_gather | solution.py:65
  334.9 370.3 %all-gather.45.cloned.1.call-start = ((), (), s32[]{:S(2)}) async-start(), calls=%async_computation.75 | async-start | bytes 2621440 | tf_op jit(solution)/shard_map/all_gather | solution.py:65
  335.5 383.1 %reduce-scatter.72.cloned.1.call-start = ((), (), s32[]{:S(2)}) async-start(), calls=%async_computation.60 | async-start | bytes 2621440 | tf_op jit(solution)/shard_map/reduce_scatter | solution.py:69
  489.0 229.6 %reduce-scatter.68.cloned.1.call-start = ((), (), s32[]{:S(2)}) async-start(), calls=%async_computation.57 | async-start | bytes 2621440 | tf_op jit(solution)/shard_map/reduce_scatter | solution.py:69
  603.8 157.5 %reduce-scatter.64.cloned.1.call-start = ((), (), s32[]{:S(2)}) async-start(), calls=%async_computation.54 | async-start | bytes 2621440 | tf_op jit(solution)/shard_map/reduce_scatter | solution.py:69
  718.5 96.4 %all-gather.39.cloned.1.call-start = ((), (), s32[]{:S(2)}) async-start(), calls=%async_computation.55 | async-start | bytes 2621440 | tf_op jit(solution)/shard_map/all_gather | solution.py:65
  767.5 90.8 %all-gather.43.cloned.1.call-start = ((), (), s32[]{:S(2)}) async-start(), calls=%async_computation.61 | async-start | bytes 2621440 | tf_op jit(solution)/shard_map/all_gather | solution.py:65
  768.1 136.3 %all-gather.41.cloned.1.call-start = ((), (), s32[]{:S(2)}) async-start(), calls=%async_computation.58 | async-start | bytes 2621440 | tf_op jit(solution)/shard_map/all_gather | solution.py:65
  768.9 320.8 %reduce-scatter.116.cloned.1.call-start = ((), (), s32[]{:S(2)}) async-start(), calls=%async_computation.86 | async-start | bytes 1769472
  774.6 316.2 %reduce-scatter.104.cloned.1.call-start = ((), (), s32[]{:S(2)}) async-start(), calls=%async_computation.80 | async-start | bytes 1769472
  779.7 312.2 %reduce-scatter.110.cloned.1.call-start = ((), (), s32[]{:S(2)}) async-start(), calls=%async_computation.83 | async-start | bytes 1769472
  784.7 308.4 %reduce-scatter.114.cloned.1.call-start = ((), (), s32[]{:S(2)}) async-start(), calls=%async_computation.85 | async-start | bytes 1769472
  789.6 323.0 %reduce-scatter.102.cloned.1.call-start = ((), (), s32[]{:S(2)}) async-start(), calls=%async_computation.79 | async-start | bytes 1769472
  794.5 359.8 %reduce-scatter.108.cloned.1.call-start = ((), (), s32[]{:S(2)}) async-start(), calls=%async_computation.82 | async-start | bytes 1769472
  799.5 396.3 %reduce-scatter.112.cloned.1.call-start = ((), (), s32[]{:S(2)}) async-start(), calls=%async_computation.84 | async-start | bytes 1769472
  804.5 433.0 %reduce-scatter.100.cloned.1.call-start = ((), (), s32[]{:S(2)}) async-start(), calls=%async_computation.78 | async-start | bytes 1769472
  809.7 469.3 %reduce-scatter.106.cloned.1.call-start = ((), (), s32[]{:S(2)}) async-start(), calls=%async_computation.81 | async-start | bytes 1769472
  814.8 501.3 %reduce-scatter.94.cloned.1.call-start = ((), (), s32[]{:S(2)}) async-start(), calls=%async_computation.72 | async-start | bytes 589824 | tf_op jit(solution)/shard_map/reduce_scatter | solution.py:331
  925.2 428.3 %reduce-scatter.98.cloned.1.call-start = ((), (), s32[]{:S(2)}) async-start(), calls=%async_computation.74 | async-start | bytes 589824 | tf_op jit(solution)/shard_map/reduce_scatter | solution.py:331
  944.8 445.9 %reduce-scatter.96.cloned.1.call-start = ((), (), s32[]{:S(2)}) async-start(), calls=%async_computation.73 | async-start | bytes 589824 | tf_op jit(solution)/shard_map/reduce_scatter | solution.py:331
  959.1 469.0 %reduce-scatter.90.cloned.1.call-start = ((), (), s32[]{:S(2)}) async-start(), calls=%async_computation.70 | async-start | bytes 589824 | tf_op jit(solution)/shard_map/reduce_scatter | solution.py:328
  968.2 497.2 %reduce-scatter.92.cloned.1.call-start = ((), (), s32[]{:S(2)}) async-start(), calls=%async_computation.71 | async-start | bytes 589824 | tf_op jit(solution)/shard_map/reduce_scatter | solution.py:328
  978.0 524.9 %reduce-scatter.88.cloned.1.call-start = ((), (), s32[]{:S(2)}) async-start(), calls=%async_computation.69 | async-start | bytes 589824 | tf_op jit(solution)/shard_map/reduce_scatter | solution.py:328
  987.5 552.5 %reduce-scatter.82.cloned.1.call-start = ((), (), s32[]{:S(2)}) async-start(), calls=%async_computation.66 | async-start | bytes 589824 | tf_op jit(solution)/shard_map/reduce_scatter | solution.py:325
  999.0 578.4 %reduce-scatter.86.cloned.1.call-start = ((), (), s32[]{:S(2)}) async-start(), calls=%async_computation.68 | async-start | bytes 589824 | tf_op jit(solution)/shard_map/reduce_scatter | solution.py:325
  1011.5 603.2 %reduce-scatter.84.cloned.1.call-start = ((), (), s32[]{:S(2)}) async-start(), calls=%async_computation.67 | async-start | bytes 589824 | tf_op jit(solution)/shard_map/reduce_scatter | solution.py:325
  1023.9 628.1 %reduce-scatter.76.cloned.1.call-start = ((), (), s32[]{:S(2)}) async-start(), calls=%async_computation.63 | async-start | bytes 589824 | tf_op jit(solution)/shard_map/reduce_scatter | solution.py:322
  1028.2 661.1 %reduce-scatter.80.cloned.1.call-start = ((), (), s32[]{:S(2)}) async-start(), calls=%async_computation.65 | async-start | bytes 589824 | tf_op jit(solution)/shard_map/reduce_scatter | solution.py:322
  1032.2 694.5 %reduce-scatter.78.cloned.1.call-start = ((), (), s32[]{:S(2)}) async-start(), calls=%async_computation.64 | async-start | bytes 589824 | tf_op jit(solution)/shard_map/reduce_scatter | solution.py:322
  1038.7 733.8 %reduce-scatter.66.cloned.1.call-start = ((), (), s32[]{:S(2)}) async-start(), calls=%async_computation.56 | async-start | bytes 2621440 | tf_op jit(solution)/shard_map/reduce_scatter | solution.py:69
  1043.6 774.4 %reduce-scatter.74.cloned.1.call-start = ((), (), s32[]{:S(2)}) async-start(), calls=%async_computation.62 | async-start | bytes 2621440 | tf_op jit(solution)/shard_map/reduce_scatter | solution.py:69
  1047.8 815.2 %reduce-scatter.70.cloned.1.call-start = ((), (), s32[]{:S(2)}) async-start(), calls=%async_computation.59 | async-start | bytes 2621440 | tf_op jit(solution)/shard_map/reduce_scatter | solution.py:69
  1052.3 857.8 %reduce-scatter.62.cloned.1.call-start = ((), (), s32[]{:S(2)}) async-start(), calls=%async_computation.53 | async-start | bytes 2621440 | tf_op jit(solution)/shard_map/reduce_scatter | solution.py:69
  1056.9 897.3 %reduce-scatter.58.cloned.1.call-start = ((), (), s32[]{:S(2)}) async-start(), calls=%async_computation.49 | async-start | bytes 2621440 | tf_op jit(solution)/shard_map/reduce_scatter | solution.py:69
  1062.9 18.1 all-to-all-start.4
  1081.0 202.0 %all-to-all-start.5 = ((bf16[4,256,256]{1,2,0:T(8,128)(2,1)}), bf16[4,256,256]{1,2,0:T(8,128)(2,1)S(1)}, u32[]{:S(2)}, u32[]{:S(2)}) async-start(bf16[4,256,256]{1,2,0:T(8,128)(2,1)} %copy.39), calls=%async_computation.17 | async-start | bytes 1048576 | tf_op jit(solution)/shard_map/all_to_all | solution.py:319
  1084.4 914.9 %reduce-scatter.54.cloned.1.call-start = ((), (), s32[]{:S(2)}) async-start(), calls=%async_computation.45 | async-start | bytes 2621440 | tf_op jit(solution)/shard_map/reduce_scatter | solution.py:69
  1282.9 19.2 all-to-all-start.3
  1304.6 558.5 %copy-start.7 = (bf16[3,256,1024]{2,1,0:T(8,128)(2,1)S(1)}, bf16[3,256,1024]{2,1,0:T(8,128)(2,1)}, u32[]{:S(2)}) copy-start(bf16[3,256,1024]{2,1,0:T(8,128)(2,1)} %param.61) | copy-start | bytes 4718596
  1304.6 558.5 %copy-start.135 = (f32[8,1,128]{2,1,0:T(1,128)S(1)}, f32[8,1,128]{2,1,0:T(1,128)}, u32[]{:S(2)}) copy-start(f32[8,1,128]{2,1,0:T(1,128)} %copy-done.134) | copy-start | bytes 12292
  1304.6 558.5 %copy-start.166 = (f32[256]{0:T(256)S(1)}, f32[256]{0:T(256)}, u32[]{:S(2)}) copy-start(f32[256]{0:T(256)} %copy-done.165) | copy-start | bytes 3076
  1304.6 558.5 %copy-start.168 = (f32[256]{0:T(256)S(1)}, f32[256]{0:T(256)}, u32[]{:S(2)}) copy-start(f32[256]{0:T(256)} %copy-done.167) | copy-start | bytes 3076
  1304.6 558.5 %copy-start.170 = (f32[256]{0:T(256)S(1)}, f32[256]{0:T(256)}, u32[]{:S(2)}) copy-start(f32[256]{0:T(256)} %copy-done.169) | copy-start | bytes 3076
  1308.3 601.8 %copy-start.30 = (bf16[3,256,1024]{2,1,0:T(8,128)(2,1)S(1)}, bf16[3,256,1024]{2,1,0:T(8,128)(2,1)}, u32[]{:S(2)}) copy-start(bf16[3,256,1024]{2,1,0:T(8,128)(2,1)} %param.73) | copy-start | bytes 4718596
  1308.3 601.8 %copy-start.133 = (f32[8,1,128]{2,1,0:T(1,128)S(1)}, f32[8,1,128]{2,1,0:T(1,128)}, u32[]{:S(2)}) copy-start(f32[8,1,128]{2,1,0:T(1,128)} %copy-done.132) | copy-start | bytes 12292
  1308.3 601.8 %copy-start.161 = (f32[256]{0:T(256)S(1)}, f32[256]{0:T(256)}, u32[]{:S(2)}) copy-start(f32[256]{0:T(256)} %copy-done.160) | copy-start | bytes 3076
  1308.3 601.9 %copy-start.176 = (f32[256]{0:T(256)S(1)}, f32[256]{0:T(256)}, u32[]{:S(2)}) copy-start(f32[256]{0:T(256)} %copy-done.175) | copy-start | bytes 3076
  (207 other events, 3551.3 us)
Sparse Core Ops, SparseCore 0:
  23.8 64.7 all-gather.30
  90.2 53.9 all-gather.34
  145.8 43.9 all-gather.20
  192.5 42.5 reduce-scatter.55
  237.4 43.1 reduce-scatter.59
  283.3 43.1 reduce-scatter.51
  489.1 66.6 reduce-scatter.71
  603.9 66.5 reduce-scatter.67
  718.6 42.6 reduce-scatter.63
Sparse Core Ops, SparseCore 1:
  211.9 23.8 all-gather.26
  330.4 44.9 all-gather.36
  377.2 23.9 all-gather.24
  403.2 25.1 all-gather.28
  430.0 45.5 all-gather.48
  477.3 67.1 all-gather.32
  546.0 44.4 all-gather.46
  592.0 67.1 all-gather.22
  660.7 44.4 all-gather.44
  767.6 44.9 all-gather.38
  814.0 44.3 all-gather.42
  860.0 44.3 all-gather.40
  907.5 37.2 reduce-scatter.115
  948.7 38.3 reduce-scatter.103
  990.3 38.3 reduce-scatter.109
  1032.0 38.3 reduce-scatter.113
  1074.3 38.3 reduce-scatter.101
  1115.9 38.3 reduce-scatter.107
  1157.4 38.3 reduce-scatter.111
  1199.1 38.3 reduce-scatter.99
  1240.6 38.3 reduce-scatter.105
  1281.9 34.1 reduce-scatter.93
  1319.3 34.1 reduce-scatter.97
  1356.6 34.1 reduce-scatter.95
  1393.9 34.1 reduce-scatter.89
  1431.2 34.1 reduce-scatter.91
  1468.8 34.1 reduce-scatter.87
  1505.9 34.1 reduce-scatter.81
  1543.3 34.1 reduce-scatter.85
  1580.5 34.1 reduce-scatter.83
  1617.9 34.1 reduce-scatter.75
  1655.0 34.1 reduce-scatter.79
  1692.6 34.1 reduce-scatter.77
  1728.9 43.5 reduce-scatter.65
  1775.3 42.7 reduce-scatter.73
  1820.3 42.7 reduce-scatter.69
  1865.5 43.7 reduce-scatter.61
  1911.4 42.7 reduce-scatter.57
  1956.6 42.7 reduce-scatter.53
where the time goes:
time: 2020 us; the launch traced here: 2010 us
  waiting for transfers between devices  1410 us (70%)
  matrix products  298 us (15%)
  blocking collectives  99.9 us (5%)
  other arithmetic  92.5 us (5%)
  local copies, waits for them, and re-layouts  61.2 us (3%)
  starting transfers between devices  31 us (2%)
  between operations  21.1 us (1%)
    reduce_scatter x12, waiting for transfers between devices, summed_rows(): lax.psum_scatter(term(jnp.int32(0), local_rows * lax.axis_size('mp')).ast...  367 us
    all_gather x12, waiting for transfers between devices, whole_rows(): return lax.all_gather(part, 'mp', axis=0, tiled=True)  341 us
    unnamed x57, waiting for transfers between devices  188 us
    reduce_scatter x3, waiting for transfers between devices, body(): lax.psum_scatter(grad_value_w.astype(jnp.bfloat16), 'dp', scatter_dimensi...  111 us
    reduce_scatter x3, waiting for transfers between devices, body(): lax.psum_scatter(grad_query_w.astype(jnp.bfloat16), 'dp', scatter_dimensi...  110 us
    reduce_scatter x3, waiting for transfers between devices, body(): lax.psum_scatter(grad_key_w.astype(jnp.bfloat16), 'dp', scatter_dimension...  110 us
    reduce_scatter x3, waiting for transfers between devices, body(): lax.psum_scatter(grad_out_w.astype(jnp.bfloat16), 'dp', scatter_dimension...  82.4 us
    dot_general x21, matrix products, outer_sum(): jnp.einsum('td,tc->dc', left, right, preferred_element_type=jnp.float32)  56.7 us
  transfers between devices with their start and end apart: 54, of which 41 were waited for; matrix products, arithmetic and copies ran while one was open for 21% of the time, Pallas kernels for 0%

commit v1 on v0

--- a/solution.py
+++ b/solution.py
@@ -1,6 +1,9 @@
 import jax
 import jax.numpy as jnp
+import numpy as np
 from jax import lax
+from jax.experimental import pallas as pl
+from jax.experimental.pallas import tpu as pltpu
 from jax.sharding import PartitionSpec as P
 
 HEAD_DIM = 64
@@ -362,9 +365,866 @@
     )
 
 
+def rope_tables():
+    half = HEAD_DIM // 2
+    inverse = THETA ** (-2.0 * jnp.arange(half, dtype=jnp.float32) / HEAD_DIM)
+    angles = jnp.arange(1024, dtype=jnp.int32).astype(jnp.float32)[:, None] * inverse[None, :]
+    cosine, sine = jnp.cos(angles), jnp.sin(angles)
+    return (
+        jnp.concatenate([cosine] * 4, axis=1),
+        jnp.concatenate([-sine, sine, -sine, sine], axis=1),
+    )
+
+
+BF = jnp.bfloat16
+F32 = jnp.float32
+MESH = pl.DeviceIdType.MESH
+CHUNK = 256
+HP = 768
+PADW = 2560
+QROWS = 400
+
+
+def remote(src, dst, send, recv, device):
+    return pltpu.make_async_remote_copy(
+        src_ref=src, dst_ref=dst, send_sem=send, recv_sem=recv, device_id=device, device_id_type=MESH
+    )
+
+
+class Place:
+    def __init__(self):
+        self.d = d = lax.axis_index("dp")
+        self.z = z = lax.axis_index("mp")
+        core = lax.rem(d, 2)
+        along_x = lax.rem(lax.div(d, 2), 2)
+        along_y = lax.div(d, 4)
+        self.dc = d + 1 - 2 * core
+        self.dx = d + 2 - 4 * along_x
+        self.dy = d + 4 - 8 * along_y
+        self.dxy = self.dx + 4 - 8 * along_y
+        self.core = (self.dc, z)
+        self.x = (self.dx, z)
+        self.y = (self.dy, z)
+        self.quads = (d, self.dx, self.dy, self.dxy)
+        self.core_quads = tuple(q + 1 - 2 * core for q in self.quads)
+
+    def peer(self, step):
+        return lax.rem(self.z + step, 4)
+
+    def greet(self):
+        barrier = pltpu.get_barrier_semaphore()
+        others = [self.core, self.x, self.y] + [(self.d, self.peer(s)) for s in (1, 2, 3)]
+        for other in others:
+            pl.semaphore_signal(barrier, inc=1, device_id=other, device_id_type=MESH)
+        pl.semaphore_wait(barrier, len(others))
+
+    def hop(self, step, visit):
+        for sign in (1, -1):
+            m = self.z + sign * step
+
+            @pl.when((m >= 0) & (m <= 3))
+            def _():
+                visit(m)
+
+
+class Gather:
+    def __init__(self, place, at, own, sems):
+        self.p, self.at, self.own = place, at, own
+        self.right, self.left, self.sx, self.sy, self.sc, self.arrived = sems
+
+    def send(self, src, m, d, sem, device):
+        remote(src, self.at(m, d), sem, self.arrived.at[m, d], device).start()
+
+    def along_z(self, m, src=None):
+        p = self.p
+        src = self.at(m, p.d) if src is None else src
+
+        @pl.when((m <= p.z) & (p.z < 3))
+        def _():
+            self.send(src, m, p.d, self.right.at[m], (p.d, p.z + 1))
+
+        @pl.when((m >= p.z) & (p.z > 0))
+        def _():
+            self.send(src, m, p.d, self.left.at[m], (p.d, p.z - 1))
+
+    def spread(self, m, src=None):
+        p = self.p
+        src = self.at(m, p.d) if src is None else src
+        self.send(src, m, p.d, self.sx.at[m], p.x)
+        self.send(src, m, p.d, self.sy.at[m], p.y)
+        self.send(src, m, p.d, self.sc.at[m], p.core)
+
+    def take(self, m, d):
+        remote(self.at(m, d), self.at(m, d), self.sc.at[0], self.arrived.at[m, d], self.p.core).wait_recv()
+
+    def z_in(self, m):
+        self.take(m, self.p.d)
+        self.along_z(m)
+
+    def x_in(self, m):
+        p = self.p
+        self.take(m, p.dx)
+        src = self.at(m, p.dx)
+
+        @pl.when(lax.rem(m, 2) == 0)
+        def _():
+            self.send(src, m, p.dx, self.sy.at[4 + m], p.y)
+
+        self.send(src, m, p.dx, self.sc.at[4 + m], p.core)
+
+    def y_in(self, m):
+        p = self.p
+        self.take(m, p.dy)
+        src = self.at(m, p.dy)
+
+        @pl.when(lax.rem(m, 2) == 1)
+        def _():
+            self.send(src, m, p.dy, self.sx.at[4 + m], p.x)
+
+        self.send(src, m, p.dy, self.sc.at[8 + m], p.core)
+
+    def diag_in(self, m):
+        p = self.p
+        self.take(m, p.dxy)
+        self.send(self.at(m, p.dxy), m, p.dxy, self.sc.at[12 + m], p.core)
+
+    def core_in(self, m):
+        for d in self.p.core_quads:
+            self.take(m, d)
+
+    def finish(self):
+        p = self.p
+
+        def sent(sem, device):
+            remote(self.own, self.own, sem, self.arrived.at[0, 0], device).wait_send()
+
+        for m in range(4):
+
+            @pl.when((m <= p.z) & (p.z < 3))
+            def _():
+                sent(self.right.at[m], p.core)
+
+            @pl.when((m >= p.z) & (p.z > 0))
+            def _():
+                sent(self.left.at[m], p.core)
+
+            sent(self.sx.at[m], p.core)
+            sent(self.sy.at[m], p.core)
+            sent((self.sx if m % 2 else self.sy).at[4 + m], p.core)
+            for q in range(4):
+                sent(self.sc.at[4 * q + m], p.core)
+
+
+def gather_sems():
+    dma = pltpu.SemaphoreType.DMA
+    return [dma((4,)), dma((4,)), dma((8,)), dma((8,)), dma((16,)), dma((4, 8))]
+
+
+def lanes(shape, width):
+    return lax.div(lax.broadcasted_iota(jnp.int32, shape, 1), width)
+
+
+def turned(x, cosine, sine):
+    first = lax.rem(lanes(x.shape, 32), 2) == 0
+    width = x.shape[1]
+    other = jnp.where(first, pltpu.roll(x, width - 32, 1), pltpu.roll(x, 32, 1))
+    return x * cosine + other * sine
+
+
+def wide(table):
+    return jnp.concatenate([table, table], axis=1)
+
+
+def dot(a, b):
+    return lax.dot_general(a, b, (((1,), (0,)), ((), ())), preferred_element_type=F32)
+
+
+def dot_nt(a, b):
+    return lax.dot_general(a, b, (((1,), (1,)), ((), ())), preferred_element_type=F32)
+
+
+def dot_tn(a, b):
+    return lax.dot_general(a, b, (((0,), (0,)), ((), ())), preferred_element_type=F32)
+
+
+def tile_scores(q_head, keys, tile, packed):
+    n = (tile + 1) * CHUNK
+    s = dot_nt(q_head, keys) * 0.125
+    rows = lax.broadcasted_iota(jnp.int32, (CHUNK, n), 0) + tile * CHUNK
+    cols = lax.broadcasted_iota(jnp.int32, (CHUNK, n), 1)
+    allowed = cols <= rows
+    if tile >= 2:
+        allowed = allowed & ((packed != 2) | (cols >= 2 * CHUNK))
+    return jnp.where(allowed, s, -1e30)
+
+
+def forward_kernel(
+    seq, tok, fv, wq, wk, wv, wo, wg, wu, wd, gains, cos_t, sin_t,
+    f1, f2, qkv, o_head, lse, o_rows, a1, gain_out,
+    stage, p2, *sems,
+):
+    p = Place()
+    sems = list(sems)
+    g1s, g2s = sems[:6], sems[6:12]
+    s_qkv, r_qkv, s_o, r_o, s_local = sems[12:]
+    z, d = p.z, p.d
+    p.greet()
+
+    f1[z, d, 0:128] = wq[...]
+    f1[z, d, 128:256] = wk[...]
+    f1[z, d, 256:384] = wv[...]
+    f1[z, d, 384:400] = gains[...]
+    g1 = Gather(p, lambda m, e: f1.at[m, e], f1.at[0, 0], g1s)
+    g2 = Gather(p, lambda m, e: f2.at[m, e], p2, g2s)
+    g1.along_z(z)
+    g1.spread(z)
+    p2[...] = jnp.zeros_like(p2)
+    p2[:, 0:256] = wo[...]
+    p2[:, 256:960] = wg[...]
+    p2[:, 1024:1728] = wu[...]
+    p2[:, 1792:2496] = wd[...]
+    own_copy = pltpu.make_async_copy(p2, f2.at[z, d], s_local)
+    own_copy.start()
+
+    def arrive(g):
+        def visit(m):
+            g.z_in(m)
+            g.spread(m)
+        return visit
+
+    def side(g):
+        def visit(m):
+            g.x_in(m)
+            g.y_in(m)
+        return visit
+
+    p.hop(1, arrive(g1))
+    side(g1)(z)
+    p.hop(2, arrive(g1))
+    p.hop(1, side(g1))
+    g1.diag_in(z)
+    p.hop(3, arrive(g1))
+    g2.along_z(z, p2)
+    p.hop(2, side(g1))
+    p.hop(1, g1.diag_in)
+    g1.core_in(z)
+
+    gain_row = jnp.concatenate([f1[z, e, 384:400, :].astype(F32)[0:8] for e in range(8)], axis=1)
+    for e in range(8):
+        gain_out[:, e * 128 : (e + 1) * 128] = gain_row[:, e * 256 + 128 : e * 256 + 256]
+
+    def norm_body(b, carry):
+        x = tok[b].astype(F32)
+        factor = lax.rsqrt(jnp.mean(x * x, axis=1, keepdims=True) + EPSILON)
+        for e in range(8):
+            cols = slice(e * 128, (e + 1) * 128)
+            a1[pl.ds(pl.multiple_of(b * CHUNK, CHUNK), CHUNK), cols] = (
+                x[:, cols] * factor * gain_row[0:1, e * 256 : e * 256 + 128]
+            ).astype(BF)
+        return carry
+
+    lax.fori_loop(0, 3, norm_body, 0)
+
+    p.hop(3, side(g1))
+    p.hop(2, g1.diag_in)
+    p.hop(1, g1.core_in)
+    p.hop(3, g1.diag_in)
+    p.hop(2, g1.core_in)
+    p.hop(3, g1.core_in)
+    g2.spread(z, p2)
+
+    def project(b):
+        pos_full = pl.ds(pl.multiple_of(z * CHUNK, CHUNK), CHUNK)
+        low = jnp.where(z >= 2, z - 2, z)
+        pos_half = pl.ds(pl.multiple_of(low * CHUNK, CHUNK), CHUNK)
+        second = seq[b] == 2
+        cosine = wide(jnp.where(second, cos_t[pos_half, :], cos_t[pos_full, :]))
+        sine = wide(jnp.where(second, sin_t[pos_half, :], sin_t[pos_full, :]))
+        rows = a1[b * CHUNK : (b + 1) * CHUNK, :]
+
+        def one(step, carry):
+            m = lax.rem(z + step, 4)
+            w = lambda i: f1[m, :, i * 128 : (i + 1) * 128, :].reshape(1024, CHUNK)
+            stage[b, m, 0] = turned(dot(rows, w(0)), cosine, sine).astype(BF)
+            stage[b, m, 1] = turned(dot(rows, w(1)), cosine, sine).astype(BF)
+            first = fv[b, :, pl.ds(pl.multiple_of(m * CHUNK, CHUNK), CHUNK)].astype(F32)
+            stage[b, m, 2] = (0.5 * (dot(rows, w(2)) + first)).astype(BF)
+            return carry
+
+        lax.fori_loop(0, 4, one, 0)
+        for i in range(3):
+            qkv[b, i, pl.ds(pl.multiple_of(z * CHUNK, CHUNK), CHUNK), :] = stage[b, z, i]
+
+    def qkv_copy(b, step):
+        m = p.peer(step)
+        dst = qkv.at[b, :, pl.ds(pl.multiple_of(z * CHUNK, CHUNK), CHUNK), :]
+        return remote(stage.at[b, m], dst, s_qkv.at[b, step - 1], r_qkv.at[b, z], (d, m))
+
+    def send_qkv(b):
+        for step in (1, 2, 3):
+            qkv_copy(b, step).start()
+
+    def sent_qkv(b):
+        for step in (1, 2, 3):
+            qkv_copy(b, step).wait_send()
+
+    def take_qkv(b):
+        for step in (1, 2, 3):
+            m = p.peer(step)
+            dst = qkv.at[b, :, pl.ds(pl.multiple_of(m * CHUNK, CHUNK), CHUNK), :]
+            remote(stage.at[b, m], dst, s_qkv.at[b, 0], r_qkv.at[b, m], (d, m)).wait_recv()
+
+    def o_copy(b, i):
+        rows = slice(i * CHUNK, (i + 1) * CHUNK)
+        return remote(o_head.at[b, rows, :], o_rows.at[b, z], s_o.at[b, i], r_o.at[b, z], (d, i))
+
+    def attend(b, i):
+        n = (i + 1) * CHUNK
+        rows = slice(i * CHUNK, n)
+        packed = seq[b]
+        q = qkv[b, 0, rows, :]
+        keys = qkv[b, 1, 0:n, :]
+        values = qkv[b, 2, 0:n, :]
+        head_of = lanes((CHUNK, CHUNK), 64)
+        lane = lax.broadcasted_iota(jnp.int32, (CHUNK, 128), 1)
+
+        def head(h, carry):
+            out, stats = carry
+            s = tile_scores(jnp.where(head_of == h, q, jnp.zeros_like(q)), keys, i, packed)
+            top = jnp.max(s, axis=1, keepdims=True)
+            e = jnp.exp(s - top)
+            total = jnp.sum(e, axis=1, keepdims=True)
+            part = dot(e.astype(BF), values) * (1.0 / total)
+            return (
+                jnp.where(head_of == h, part, out),
+                jnp.where(lane == h, top + jnp.log(total), stats),
+            )
+
+        out, stats = lax.fori_loop(
+            0, 4, head, (jnp.zeros((CHUNK, CHUNK), F32), jnp.zeros((CHUNK, 128), F32))
+        )
+        o_head[b, rows, :] = out.astype(BF)
+        lse[b, rows, :] = stats
+
+        @pl.when(z == i)
+        def _():
+            o_rows[b, z] = out.astype(BF)
+
+        @pl.when(z != i)
+        def _():
+            o_copy(b, i).start()
+
+    for b in range(3):
+        project(b)
+        if b == 0:
+            send_qkv(0)
+    p.hop(1, g2.z_in)
+    sent_qkv(0)
+    send_qkv(1)
+    p.hop(2, g2.z_in)
+    p.hop(3, g2.z_in)
+    p.hop(1, g2.spread)
+    side(g2)(z)
+    p.hop(2, g2.spread)
+    take_qkv(0)
+    attend(0, 0)
+    attend(0, 1)
+    p.hop(1, side(g2))
+    sent_qkv(1)
+    send_qkv(2)
+    attend(0, 2)
+    attend(0, 3)
+    p.hop(3, g2.spread)
+    p.hop(2, side(g2))
+    take_qkv(1)
+    attend(1, 0)
+    attend(1, 1)
+    g2.diag_in(z)
+    p.hop(1, g2.diag_in)
+    attend(1, 2)
+    attend(1, 3)
+    p.hop(3, side(g2))
+    p.hop(2, g2.diag_in)
+    take_qkv(2)
+    attend(2, 0)
+    attend(2, 1)
+    p.hop(3, g2.diag_in)
+    attend(2, 2)
+    attend(2, 3)
+    sent_qkv(2)
+    for m in range(4):
+        g2.core_in(m)
+    for b in range(3):
+        for step in (1, 2, 3):
+            m = p.peer(step)
+            remote(o_rows.at[b, m], o_rows.at[b, m], s_o.at[b, 0], r_o.at[b, m], (d, m)).wait_recv()
+        for i in range(4):
+
+            @pl.when(z != i)
+            def _():
+                o_copy(b, i).wait_send()
+
+    g1.finish()
+    g2.finish()
+    own_copy.wait()
+
+
+def run_forward(seq, tok, fv, wq, wk, wv, wo, wg, wu, wd, gains, cos_t, sin_t):
+    vmem = pl.BlockSpec(memory_space=pltpu.VMEM)
+    hbm = pl.BlockSpec(memory_space=pl.ANY)
+    dma = pltpu.SemaphoreType.DMA
+    shape = jax.ShapeDtypeStruct
+    return pl.pallas_call(
+        forward_kernel,
+        out_shape=(
+            shape((4, 8, QROWS, CHUNK), BF),
+            shape((4, 8, 128, PADW), BF),
+            shape((3, 3, 1024, CHUNK), BF),
+            shape((3, 1024, CHUNK), BF),
+            shape((3, 1024, 128), F32),
+            shape((3, 4, CHUNK, CHUNK), BF),
+            shape((768, 1024), BF),
+            shape((8, 1024), F32),
+        ),
+        in_specs=[pl.BlockSpec(memory_space=pltpu.SMEM)] + [vmem] * 12,
+        out_specs=(vmem, hbm, vmem, vmem, vmem, vmem, vmem, vmem),
+        scratch_shapes=[
+            pltpu.VMEM((3, 4, 3, CHUNK, CHUNK), BF),
+            pltpu.VMEM((128, PADW), BF),
+        ]
+        + gather_sems()
+        + gather_sems()
+        + [dma((3, 3)), dma((3, 4)), dma((3, 4)), dma((3, 4)), dma],
+        compiler_params=pltpu.CompilerParams(
+            collective_id=1, has_side_effects=True, vmem_limit_bytes=60 * 2**20
+        ),
+        cost_estimate=pl.CostEstimate(flops=2 * 10**10, bytes_accessed=6 * 10**7, transcendentals=8 * 10**6),
+        name="gather_attend",
+    )(seq, tok, fv, wq, wk, wv, wo, wg, wu, wd, gains, cos_t, sin_t)
+
+
+def backward_kernel(
+    seq, do_rows, qkv, o_head, lse, cos_t, sin_t,
+    d_rows,
+    do_head, dk, dv, stage, *sems,
+):
+    p = Place()
+    s_do, r_do, s_d, r_d = sems
+    z, d = p.z, p.d
+    p.greet()
+    mine = pl.ds(pl.multiple_of(z * CHUNK, CHUNK), CHUNK)
+
+    def do_copy(b, step):
+        m = p.peer(step)
+        return remote(
+            do_rows.at[b, m], do_head.at[b, mine, :], s_do.at[b, step - 1], r_do.at[b, z], (d, m)
+        )
+
+    def send_do(b):
+        for step in (1, 2, 3):
+            do_copy(b, step).start()
+        do_head[b, mine, :] = do_rows[b, z]
+
+    def take_do(b):
+        for step in (1, 2, 3):
+            m = p.peer(step)
+            dst = do_head.at[b, pl.ds(pl.multiple_of(m * CHUNK, CHUNK), CHUNK), :]
+            remote(do_rows.at[b, m], dst, s_do.at[b, 0], r_do.at[b, m], (d, m)).wait_recv()
+
+    def d_copy(b, i):
+        return remote(stage.at[b, i], d_rows.at[b, z], s_d.at[b, i], r_d.at[b, z], (d, i))
+
+    def back(b, i):
+        n = (i + 1) * CHUNK
+        rows = slice(i * CHUNK, n)
+        packed = seq[b]
+        head_of = lanes((CHUNK, CHUNK), 64)
+        lane = lax.broadcasted_iota(jnp.int32, (CHUNK, 128), 1)
+        q = qkv[b, 0, rows, :]
+        keys = qkv[b, 1, 0:n, :]
+        values = qkv[b, 2, 0:n, :]
+        grad = do_head[b, rows, :]
+        spread = grad.astype(F32) * o_head[b, rows, :].astype(F32)
+        stats = lse[b, rows, :]
+
+        def head(h, dq):
+            here = head_of == h
+            q_h = jnp.where(here, q, jnp.zeros_like(q))
+            g_h = jnp.where(here, grad, jnp.zeros_like(grad))
+            delta = jnp.sum(jnp.where(here, spread, 0.0), axis=1, keepdims=True)
+            level = jnp.sum(jnp.where(lane == h, stats, 0.0), axis=1, keepdims=True)
+            prob = jnp.exp(tile_scores(q_h, keys, i, packed) - level)
+            dp = dot_nt(g_h, values)
+            ds = (prob * (dp - delta)).astype(BF)
+            dv_part = dot_tn(prob.astype(BF), g_h)
+            dk_part = dot_tn(ds, q_h)
+            dv[0:n, :] += dv_part
+            dk[0:n, :] += dk_part
+            return jnp.where(here, dot(ds, keys), dq)
+
+        dq = lax.fori_loop(0, 4, head, jnp.zeros((CHUNK, CHUNK), F32))
+        cosine, sine = cos_t[rows, :], sin_t[rows, :]
+        if i >= 2:
+            early = slice((i - 2) * CHUNK, (i - 1) * CHUNK)
+            cosine = jnp.where(packed == 2, cos_t[early, :], cosine)
+            sine = jnp.where(packed == 2, sin_t[early, :], sine)
+        cosine, sine = wide(cosine), -wide(sine)
+        stage[b, i, :, 0:256] = turned(dq * 0.125, cosine, sine).astype(BF)
+        stage[b, i, :, 256:512] = turned(dk[rows, :] * 0.125, cosine, sine).astype(BF)
+        stage[b, i, :, 512:768] = dv[rows, :].astype(BF)
+
+        @pl.when(z == i)
+        def _():
+            d_rows[b, z] = stage[b, i]
+
+        @pl.when(z != i)
+        def _():
+            d_copy(b, i).start()
+
+    for b in range(3):
+        send_do(b)
+    for b in range(3):
+        take_do(b)
+        dk[...] = jnp.zeros_like(dk)
+        dv[...] = jnp.zeros_like(dv)
+        for i in (3, 2, 1, 0):
+            back(b, i)
+    for b in range(3):
+        for step in (1, 2, 3):
+            do_copy(b, step).wait_send()
+            m = p.peer(step)
+            remote(d_rows.at[b, m], d_rows.at[b, m], s_d.at[b, 0], r_d.at[b, m], (d, m)).wait_recv()
+        for i in range(4):
+
+            @pl.when(z != i)
+            def _():
+                d_copy(b, i).wait_send()
+
+
+def run_backward(seq, do_rows, qkv, o_head, lse, cos_t, sin_t):
+    vmem = pl.BlockSpec(memory_space=pltpu.VMEM)
+    dma = pltpu.SemaphoreType.DMA
+    return pl.pallas_call(
+        backward_kernel,
+        out_shape=jax.ShapeDtypeStruct((3, 4, CHUNK, 768), BF),
+        in_specs=[pl.BlockSpec(memory_space=pltpu.SMEM)] + [vmem] * 6,
+        out_specs=vmem,
+        scratch_shapes=[
+            pltpu.VMEM((3, 1024, CHUNK), BF),
+            pltpu.VMEM((1024, CHUNK), F32),
+            pltpu.VMEM((1024, CHUNK), F32),
+            pltpu.VMEM((3, 4, CHUNK, 768), BF),
+            dma((3, 3)),
+            dma((3, 4)),
+            dma((3, 4)),
+            dma((3, 4)),
+        ],
+        compiler_params=pltpu.CompilerParams(
+            collective_id=2, has_side_effects=True, vmem_limit_bytes=60 * 2**20
+        ),
+        cost_estimate=pl.CostEstimate(flops=3 * 10**10, bytes_accessed=2 * 10**7, transcendentals=8 * 10**6),
+        name="attend_back",
+    )(seq, do_rows, qkv, o_head, lse, cos_t, sin_t)
+
+
+ORDER = (3, 0, 1, 2)
+
+
+class Scatter:
+    def __init__(self, place, part, width, bufs, sems, out):
+        self.p, self.part, self.width, self.out = place, part, width, out
+        self.own, self.other, self.diag_buf, self.bx, self.by, self.br, self.bl = bufs
+        (self.l_own, self.s_core, self.r_core, self.s_diag, self.r_diag,
+         self.s_x, self.r_x, self.s_y, self.r_y, self.s_r, self.r_r, self.s_l, self.r_l) = sems
+
+    def core_copy(self, m, q):
+        p = self.p
+        return remote(
+            self.part(m, p.core_quads[q]), self.other.at[m, q],
+            self.s_core.at[m, q], self.r_core.at[m, q], p.core,
+        )
+
+    def own_copy(self, m, q):
+        return pltpu.make_async_copy(
+            self.part(m, self.p.quads[q]), self.own.at[m, q], self.l_own.at[m, q]
+        )
+
+    def begin(self, m):
+        for q in (3, 1, 2, 0):
+            self.core_copy(m, q).start()
+            self.own_copy(m, q).start()
+
+    def add(self, dst, *terms):
+        step = 16
+
+        def rows(r, carry):
+            at = pl.ds(pl.multiple_of(r * step, step), step)
+            total = dst[at, :].astype(F32)
+            for t in terms:
+                total = total + t[at, :].astype(F32)
+            dst[at, :] = total.astype(dst.dtype)
+            return carry
+
+        lax.fori_loop(0, 128 // step, rows, 0)
+
+    def joined(self, m, q, *more):
+        self.own_copy(m, q).wait()
+        self.core_copy(m, q).wait_recv()
+        self.add(self.own.at[m, q], self.other.at[m, q], *more)
+
+    def diag_copy(self, m):
+        to = self.p.x if m % 2 == 0 else self.p.y
+        return remote(self.own.at[m, 3], self.diag_buf.at[m], self.s_diag.at[m], self.r_diag.at[m], to)
+
+    def x_copy(self, m):
+        return remote(self.own.at[m, 1], self.bx.at[m], self.s_x.at[m], self.r_x.at[m], self.p.x)
+
+    def y_copy(self, m):
+        return remote(self.own.at[m, 2], self.by.at[m], self.s_y.at[m], self.r_y.at[m], self.p.y)
+
+    def r_copy(self, m):
+        return remote(
+            self.own.at[m, 0], self.br.at[m], self.s_r.at[m], self.r_r.at[m], (self.p.d, self.p.z + 1)
+        )
+
+    def l_copy(self, m):
+        return remote(
+            self.own.at[m, 0], self.bl.at[m], self.s_l.at[m], self.r_l.at[m], (self.p.d, self.p.z - 1)
+        )
+
+    def diag(self, m):
+        self.joined(m, 3)
+        self.diag_copy(m).start()
+
+    def direct(self, m):
+        self.joined(m, 1 if m % 2 == 0 else 2)
+        (self.x_copy if m % 2 == 0 else self.y_copy)(m).start()
+
+    def relay(self, m):
+        self.diag_copy(m).wait_recv()
+        self.joined(m, 2 if m % 2 == 0 else 1, self.diag_buf.at[m])
+        (self.y_copy if m % 2 == 0 else self.x_copy)(m).start()
+
+    def quad_sum(self, m):
+        self.own_copy(m, 0).wait()
+        self.core_copy(m, 0).wait_recv()
+        self.x_copy(m).wait_recv()
+        self.y_copy(m).wait_recv()
+        self.add(self.own.at[m, 0], self.other.at[m, 0], self.bx.at[m], self.by.at[m])
+
+    def along_z(self, m):
+        z = self.p.z
+
+        if m > 0:
+            @pl.when(z < m)
+            def _():
+                @pl.when(z > 0)
+                def _():
+                    self.r_copy(m).wait_recv()
+                    self.add(self.own.at[m, 0], self.br.at[m])
+
+                self.r_copy(m).start()
+
+        if m < 3:
+            @pl.when(z > m)
+            def _():
+                @pl.when(z < 3)
+                def _():
+                    self.l_copy(m).wait_recv()
+                    self.add(self.own.at[m, 0], self.bl.at[m])
+
+                self.l_copy(m).start()
+
+    def last(self):
+        z = self.p.z
+        step = 16
+
+        for m in range(4):
+            @pl.when(z == m)
+            def _():
+                terms = [self.own.at[m, 0]]
+                if m > 0:
+                    self.r_copy(m).wait_recv()
+                    terms.append(self.br.at[m])
+                if m < 3:
+                    self.l_copy(m).wait_recv()
+                    terms.append(self.bl.at[m])
+
+                def rows(r, carry):
+                    at = pl.ds(pl.multiple_of(r * step, step), step)
+                    total = terms[0][at, :].astype(F32)
+                    for t in terms[1:]:
+                        total = total + t[at, :].astype(F32)
+                    self.out[at, :] = total
+                    return carry
+
+                lax.fori_loop(0, 128 // step, rows, 0)
+
+    def finish(self):
+        z = self.p.z
+        for m in range(4):
+            for q in range(4):
+                self.core_copy(m, q).wait_send()
+            self.diag_copy(m).wait_send()
+            self.x_copy(m).wait_send()
+            self.y_copy(m).wait_send()
+            if m > 0:
+                @pl.when(z < m)
+                def _():
+                    self.r_copy(m).wait_send()
+            if m < 3:
+                @pl.when(z > m)
+                def _():
+                    self.l_copy(m).wait_send()
+
+    def steps(self):
+        a, b, c, e = ORDER
+        return [
+            lambda: self.begin(a), lambda: self.begin(b), lambda: self.diag(a), lambda: self.diag(b),
+            lambda: self.begin(c), lambda: self.direct(a), lambda: self.direct(b),
+            lambda: self.begin(e), lambda: self.diag(c), lambda: self.diag(e),
+            lambda: self.relay(a), lambda: self.relay(b), lambda: self.direct(c), lambda: self.direct(e),
+            lambda: self.quad_sum(a), lambda: self.along_z(a), lambda: self.quad_sum(b), lambda: self.along_z(b),
+            lambda: self.relay(c), lambda: self.relay(e),
+            lambda: self.quad_sum(c), lambda: self.along_z(c), lambda: self.quad_sum(e), lambda: self.along_z(e),
+            self.last,
+        ]
+
+
+def scatter_buffers(width):
+    def buf(*lead):
+        return pltpu.VMEM((*lead, 128, width), BF)
+
+    return [buf(4, 4), buf(4, 4), buf(4), buf(4), buf(4), buf(4), buf(4)]
+
+
+def scatter_sems():
+    dma = pltpu.SemaphoreType.DMA
+    return [dma((4, 4))] * 3 + [dma((4,))] * 10
+
+
+def scatter_kernel(part1, part2, out1, out2, *rest):
+    rest = list(rest)
+    bufs1, bufs2, sems1, sems2 = rest[:7], rest[7:14], rest[14:27], rest[27:40]
+    p = Place()
+    p.greet()
+    big = Scatter(p, lambda m, d: part2.at[m, d], PADW, bufs2, sems2, out2)
+    small = Scatter(p, lambda m, d: part1.at[m, d], 768, bufs1, sems1, out1)
+    for a, b in zip(big.steps(), small.steps()):
+        a()
+        b()
+    big.finish()
+    small.finish()
+
+
+def run_scatter(part1, part2):
+    vmem = pl.BlockSpec(memory_space=pltpu.VMEM)
+    hbm = pl.BlockSpec(memory_space=pl.ANY)
+    shape = jax.ShapeDtypeStruct
+    return pl.pallas_call(
+        scatter_kernel,
+        out_shape=(shape((128, 768), F32), shape((128, PADW), F32)),
+        in_specs=[hbm, hbm],
+        out_specs=(vmem, vmem),
+        scratch_shapes=scatter_buffers(768) + scatter_buffers(PADW) + scatter_sems() + scatter_sems(),
+        compiler_params=pltpu.CompilerParams(
+            collective_id=3, has_side_effects=True, vmem_limit_bytes=60 * 2**20
+        ),
+        cost_estimate=pl.CostEstimate(flops=10**7, bytes_accessed=5 * 10**7, transcendentals=0),
+        name="sum_grads",
+    )(part1, part2)
+
+
+def fast_body(
+    tokens, first_values, sequences, w_query, w_key, w_value, w_out, w_gate, w_up, w_down,
+    gain_attn, gain_mlp, cotangent,
+):
+    seq = sequences[:, 0]
+    gains = jnp.zeros((16, CHUNK), BF).at[0, :128].set(gain_attn).at[0, 128:].set(gain_mlp)
+    cos_t, sin_t = rope_tables()
+    f1, f2, qkv, o_head, lse, o_rows, a1, gain_out = run_forward(
+        seq, tokens, first_values, w_query, w_key, w_value, w_out, w_gate, w_up, w_down, gains, cos_t, sin_t
+    )
+    gain_two = gain_out[0]
+    dotf = lambda eq, a, b: jnp.einsum(eq, a, b, preferred_element_type=F32)
+    wo = f2[:, :, :, 0:256].reshape(4, 1024, 256)
+    wg = f2[:, :, :, 256:1024].reshape(4, 1024, HP)
+    wu = f2[:, :, :, 1024:1792].reshape(4, 1024, HP)
+    wd = f2[:, :, :, 1792:2560].reshape(4, 1024, HP)
+    x = tokens.reshape(768, 1024).astype(F32)
+    g16 = cotangent.reshape(768, 1024)
+    o_cols = o_rows.transpose(1, 0, 2, 3).reshape(4, 768, 256)
+    x2 = x + dotf("mrc,mdc->rd", o_cols, wo)
+    r2 = lax.rsqrt(jnp.mean(x2 * x2, axis=-1, keepdims=True) + EPSILON)
+    n2 = x2 * r2
+    a2 = (n2 * gain_two[None, :]).astype(BF)
+    gate = dotf("rd,mdc->mrc", a2, wg)
+    up = dotf("rd,mdc->mrc", a2, wu)
+    sg = jax.nn.sigmoid(gate)
+    h = (gate * sg * up).astype(BF)
+    layer_out = (x2 + dotf("mrc,mdc->rd", h, wd)).astype(BF).reshape(3, 256, 1024)
+    dh = dotf("rd,mdc->mrc", g16, wd)
+    dgate = (dh * up * sg * (1.0 + gate * (1.0 - sg))).astype(BF)
+    dup = (dh * gate * sg).astype(BF)
+    da2 = dotf("mrc,mdc->rd", dgate, wg) + dotf("mrc,mdc->rd", dup, wu)
+    part_gain2 = jnp.sum(da2 * n2, axis=0)
+    dn2 = da2 * gain_two[None, :]
+    dx2 = g16.astype(F32) + r2 * (dn2 - n2 * jnp.mean(dn2 * n2, axis=-1, keepdims=True))
+    dattn = dx2.astype(BF)
+    do_rows = dotf("rd,mdc->mrc", dattn, wo).astype(BF).reshape(4, 3, 256, 256).transpose(1, 0, 2, 3)
+    d_rows = run_backward(seq, do_rows, qkv, o_head, lse, cos_t, sin_t)
+    gw2 = jnp.concatenate(
+        [
+            dotf("rd,mrc->mdc", dattn, o_cols).astype(BF),
+            dotf("rd,mrc->mdc", a2, dgate).astype(BF),
+            dotf("rd,mrc->mdc", a2, dup).astype(BF),
+            dotf("rd,mrc->mdc", g16, h).astype(BF),
+        ],
+        axis=-1,
+    ).reshape(4, 8, 128, PADW)
+    dcols = d_rows.transpose(1, 0, 2, 3).reshape(4, 768, 768)
+    scale = jnp.concatenate([jnp.ones((512,), F32), jnp.full((256,), 0.5, F32)])
+    gw1 = (dotf("rd,mrc->mdc", a1, dcols) * scale).astype(BF).reshape(4, 8, 128, 768)
+    w1 = f1[:, :, 0:384, :].reshape(4, 8, 3, 128, 256)
+    dc = dcols.reshape(4, 768, 3, 256)
+    da1 = (
+        dotf("mrac,mdac->rd", dc[:, :, 0:2], w1[:, :, 0:2].transpose(0, 1, 3, 2, 4).reshape(4, 1024, 2, 256))
+        + 0.5 * dotf("mrc,mdc->rd", dc[:, :, 2], w1[:, :, 2].reshape(4, 1024, 256))
+    )
+    r1 = lax.rsqrt(jnp.mean(x * x, axis=-1, keepdims=True) + EPSILON)
+    n1 = x * r1
+    gain_one = f1[0, :, 384, 0:128].reshape(1024).astype(F32)
+    part_gain1 = jnp.sum(da1 * n1, axis=0)
+    dn1 = da1 * gain_one[None, :]
+    grad_tokens = dx2 + r1 * (dn1 - n1 * jnp.mean(dn1 * n1, axis=-1, keepdims=True))
+    grad_first = 0.5 * d_rows[:, :, :, 512:768].transpose(0, 2, 1, 3).reshape(3, 256, 1024).astype(F32)
+    s1, s2 = run_scatter(gw1, gw2)
+    gain_sums = lax.psum(jnp.stack([part_gain1, part_gain2]), ("dp", "mp"))
+    place = (lax.axis_index("dp") * 4 + lax.axis_index("mp")) * 32
+    gain_mine = lax.dynamic_slice(gain_sums, (0, place), (2, 32))
+    return (
+        layer_out,
+        grad_tokens.reshape(3, 256, 1024),
+        grad_first,
+        s1[:, 0:256],
+        s1[:, 256:512],
+        s1[:, 512:768],
+        s2[:, 0:256],
+        s2[:, 256:960],
+        s2[:, 1024:1728],
+        s2[:, 1792:2496],
+        gain_mine[0],
+        gain_mine[1],
+    )
+
+
+def is_small(mesh):
+    return mesh.axis_names == ("dp", "mp") and tuple(mesh.devices.shape) == (8, 4)
+
+
 def solution(mesh):
     return jax.shard_map(
-        body,
+        fast_body if is_small(mesh) else body,
         mesh=mesh,
         in_specs=(
             P(None, ("dp", "mp"), None),

time: 2020 us -> 871 us (0.43)
  the two profiles are of different devices: /device:TPU:0 before, /device:TPU:17 now
where the time goes in v1:
time: 871 us; the launch traced here: 861 us
  Pallas kernels  551 us (63%)
  matrix products  114 us (13%)
  local copies, waits for them, and re-layouts  109 us (13%)
  other arithmetic  46 us (5%)
  blocking collectives  39.6 us (5%)
    pallas_call x1, Pallas kernels, run_forward(): pl.pallas_call(forward_kernel, out_shape=(shape((4, 8, QROWS, CHUNK), BF)...  223 us
    pallas_call x1, Pallas kernels, run_scatter(): pl.pallas_call(scatter_kernel, out_shape=(shape((128, 768), F32), shape((...  181 us
    pallas_call x1, Pallas kernels, run_backward(): pl.pallas_call(backward_kernel, out_shape=jax.ShapeDtypeStruct((3, 4, CHU...  147 us
    dot_general x15, matrix products, fast_body(): dotf = lambda eq, a, b: jnp.einsum(eq, a, b, preferred_element_type=F32)  114 us
    psum x1, blocking collectives, fast_body(): gain_sums = lax.psum(jnp.stack([part_gain1, part_gain2]), ('dp', 'mp'))  39.6 us
    concatenate x1, local copies, waits for them, and re-layouts, fast_body(): jnp.concatenate([dotf('rd,mrc->mdc', dattn, o_cols).astype(BF), dotf('rd,...  25.9 us
    concatenate x1, other arithmetic, fast_body(): jnp.concatenate([dotf('rd,mrc->mdc', dattn, o_cols).astype(BF), dotf('rd,...  25.6 us
    unnamed x67, local copies, waits for them, and re-layouts  18.1 us

profile of v1, /device:TPU:17, one launch (start us, length us, event | category | flops | bytes accessed | tf_op | source)
XLA Modules:
  0.0 861.2 jit_solution(3288630963732545562)
XLA Ops:
  0.6 1.3 and_reduce_fusion
  2.0 0.6 fusion.39
  2.6 2.7 broadcast_select_fusion
  5.2 1.8 fusion.22
  7.0 0.6 rsqrt.21
  7.6 0.7 scatter.6
  8.3 1.4 scatter.9.gains
  9.8 1.7 copy.70.wg
  11.5 1.7 copy.71.wu
  13.2 1.7 copy.72.wd
  15.0 1.9 fusion.35
  16.9 1.9 pad_maximum_fusion.1
  18.7 223.5 %gather_attend.1 = (bf16[4,8,400,256]{3,2,1,0:T(8,128)(2,1)}, bf16[4,8,128,2560]{3,2,1,0:T(8,128)(2,1)}, bf16[3,3,1024,256]{3,2,1,0:T(8,128)(2,1)}, bf16[3,1024,...) custom-call(s32[3]{0:T(128)} %bitcast.208, ...), custom_call_target="tpu_custom_call" | custom-call | flops 20000000000 | bytes 60000000 | tf_op jit(solution)/shard_map/gather_attend/pallas_call | solution.py:777
  242.2 1.5 copy.73
  243.8 0.8 slice.105
  244.5 1.3 slice_convert_fusion
  245.9 3.2 slice.109
  249.1 1.5 slice.127
  250.8 2.2 copy.85
  253.0 1.8 slice.103
  254.9 11.1 %fusion.36 = (bf16[4,8,128,768]{3,2,1,0:T(8,128)(2,1)}, bf16[4,8,128,768]{3,2,1,0:T(8,128)(2,1)S(1)}, bf16[4,8,128,768]{3,2,1,0:T(8,128)(2,1)S(1)}) fusion(bf16[4,8,128,2560]{3,2,1,0:T(8,128)(2,1)} %get-tuple-element.47), kind=kLoop, calls=%fused_computation.80 | loop fusion | bytes 37748736 | tf_op jit(solution)/shard_map/slice | solution.py:1153
  266.0 1.9 multiply_reduce_fusion.2
  268.6 7.6 fusion.41
  276.2 7.7 fusion.40
  283.8 19.0 %fusion.4 = (bf16[4,768,768]{1,2,0:T(8,128)(2,1)}, bf16[4,768,768]{1,2,0:T(8,128)(2,1)}, bf16[4,768,768]{1,2,0:T(8,128)(2,1)}) fusion(f32[4,768,768]{2,1,0:T(8,128)} %fusion.40, f32[4,768,768]{2,1,0:T(8,128)} %fusion.41, bf16[4,1024,768]{2,1,0:T(8,128)(2,1)} %bitcast.185, bf16[768,1024,1]{1,0,2:T(8,128)(2,1)S(1)} %bitcast.197), kind=kOutput, calls=%fused_computation.8 | convolution fusion | flops 4869586944 | bytes 40894464 | tf_op jit(solution)/shard_map/rd,mdc->mrc/dot_general | solution.py:1149
  302.8 18.1 %fusion.13 = bf16[768,1024]{1,0:T(8,128)(2,1)} fusion(f32[768,1024]{1,0:T(8,128)S(1)} %get-tuple-element.116, bf16[4,768,768]{1,2,0:T(8,128)(2,1)} %get-tuple-element.101, bf16[4,1024,768]{2,1,0:T(8,128)(2,1)} %bitcast.186), kind=kOutput, calls=%fused_computation.29 | convolution fusion | flops 4833411072 | bytes 15728640 | tf_op jit(solution)/shard_map/mrc,mdc->rd/dot_general | solution.py:1149
  321.0 5.1 fusion.42
  326.2 6.1 multiply_reduce_fusion
  332.3 0.8 multiply_add_fusion
  333.1 0.7 copy-done.14
  333.9 3.2 fusion.30
  337.1 2.6 copy.81
  339.7 2.7 copy.118
  342.4 147.2 %attend_back.1 = bf16[3,4,256,768]{3,2,1,0:T(8,128)(2,1)} custom-call(s32[3]{0:T(128)} %bitcast.209, bf16[3,4,256,256]{3,2,1,0:T(8,128)(2,1)} %bitcast.196, bf16[3,3,1024,256]{3,2,1,0:T(8,128)(2,1)} %get-tuple-element.49.qkv, bf16[3,1024,256]{2,1,0:T(8,128)(2,1)} %get-tuple-element.50.o_head, f32[3,1024,128]{2,1,0:T(8,128)} %get-tuple-element.51.lse, ...), custom_call_target="tpu_custom_call" | custom-call | flops 30000001024 | bytes 20000000 | tf_op jit(solution)/shard_map/attend_back/pallas_call | solution.py:907
  489.6 4.8 convert_bitcast_fusion.3
  494.4 9.5 %convert_bitcast_fusion.1 = bf16[4,1024,768]{1,2,0:T(8,128)(2,1)} fusion(bf16[4,768,768]{1,2,0:T(8,128)(2,1)} %get-tuple-element.99, bf16[768,1024,1]{1,0,2:T(8,128)(2,1)S(1)} %copy-done.17), kind=kOutput, calls=%fused_computation.20 | convolution fusion | flops 4834983936 | bytes 12582912 | tf_op jit(solution)/shard_map/rd,mrc->mdc/dot_general | solution.py:1149
  503.9 7.0 convert_bitcast_fusion.2
  510.9 3.4 multiply_bitcast_fusion
  514.3 2.4 copy.87
  516.7 2.4 copy.93
  519.1 2.8 copy.83
  521.8 2.1 copy-done.1
  524.0 7.1 fusion.10
  531.1 8.6 %copy.90 = bf16[4,1024,768]{2,1,0:T(8,128)(2,1)} copy(bf16[4,1024,768]{1,2,0:T(8,128)(2,1)} %fusion.10) | data formatting | bytes 12582912 | tf_op jit(solution)/shard_map/convert_element_type | solution.py:1187
  539.7 11.5 %reshape_reshape.3 = bf16[4,768,3,256]{3,2,1,0:T(4,128)(2,1)} reshape(bf16[4,3,256,768]{3,2,1,0:T(8,128)(2,1)} %copy-done.1) | data formatting | bytes 9437184 | tf_op jit(solution)/shard_map/reshape;reshape | solution.py:1189
  551.2 2.8 copy-done
  553.9 3.4 slice.126
  557.4 1.8 fusion.26
  559.2 0.5 copy-done.9
  559.7 1.3 copy-done.10
  561.0 5.5 fusion.21
  566.5 39.6 %psum.7 = f32[2,1024]{1,0:T(2,128)S(1)} all-reduce(f32[2,1024]{1,0:T(2,128)S(1)} %pad_maximum_fusion.3), channel_id=1, replica_groups=mesh['dp'=8,'mp'=4] {'dp','mp'}, use_global_device_ids=true, to_apply=%region_7.0 | all-reduce | flops 2048 | bytes 16384 | tf_op jit(solution)/shard_map/psum | solution.py:1202
  606.2 0.5 slice_bitcast_fusion.1
  606.7 4.9 fusion.20
  611.6 9.5 %convert_bitcast_fusion = bf16[4,1024,768]{1,2,0:T(8,128)(2,1)} fusion(bf16[4,768,768]{1,2,0:T(8,128)(2,1)} %get-tuple-element.101, bf16[768,1024,1]{1,0,2:T(8,128)(2,1)S(1)} %bitcast.198), kind=kOutput, calls=%fused_computation.19 | convolution fusion | flops 4834983936 | bytes 12582912 | tf_op jit(solution)/shard_map/rd,mrc->mdc/dot_general | solution.py:1149
  621.1 25.6 %pad_maximum_fusion = bf16[4,1024,2560]{1,2,0:T(8,128)(2,1)} fusion(bf16[4,1024,768]{1,2,0:T(8,128)(2,1)} %convert_bitcast_fusion, bf16[4,1024,768]{1,2,0:T(8,128)(2,1)} %convert_bitcast_fusion.1, bf16[4,1024,768]{1,2,0:T(8,128)(2,1)} %convert_bitcast_fusion.2, bf16[4,1024,256]{1,2,0:T(8,128)(2,1)S(1)} %copy-done.11), kind=kLoop, calls=%fused_computation | loop fusion | flops 83886080 | bytes 41943040 | tf_op jit(solution)/shard_map/concatenate | solution.py:1176
  646.7 25.9 %copy.92 = bf16[4,1024,2560]{2,1,0:T(8,128)(2,1)} copy(bf16[4,1024,2560]{1,2,0:T(8,128)(2,1)} %pad_maximum_fusion) | data formatting | bytes 41943040 | tf_op jit(solution)/shard_map/concatenate | solution.py:1176
  672.6 180.8 %sum_grads.1 = (f32[128,768]{1,0:T(8,128)}, f32[128,2560]{1,0:T(8,128)}) custom-call(bf16[4,8,128,768]{3,2,1,0:T(8,128)(2,1)} %bitcast.177, bf16[4,8,128,2560]{3,2,1,0:T(8,128)(2,1)} %bitcast.174), custom_call_target="tpu_custom_call" | custom-call | flops 10000000 | bytes 50000000 | tf_op jit(solution)/shard_map/sum_grads/pallas_call | solution.py:1124
  853.4 1.8 fusion.38
  855.2 1.6 slice.118
  856.8 1.3 fusion.37
  858.1 0.9 copy.96
  859.0 0.9 copy.95
  859.9 0.9 copy.94
  (69 shorter events, 1.2 us)
Async XLA Ops:
  9.8 9.0 %copy-start.23 = (bf16[16,256]{1,0:T(8,128)(2,1)}, bf16[16,256]{1,0:T(8,128)(2,1)S(1)}, u32[]{:S(2)}) copy-start(bf16[16,256]{1,0:T(8,128)(2,1)S(1)} %scatter.9.gains) | copy-start | bytes 24580
  243.7 22.2 %copy-start.15 = (bf16[4,3,256,256]{3,2,1,0:T(8,128)(2,1)}, bf16[4,3,256,256]{3,2,1,0:T(8,128)(2,1)S(1)}, u32[]{:S(2)}) copy-start(bf16[4,3,256,256]{3,2,1,0:T(8,128)(2,1)S(1)} %copy.73) | copy-start | bytes 4718596
  254.8 11.1 %copy-start.13 = (bf16[4,8,128,256]{3,2,1,0:T(8,128)(2,1)}, bf16[4,8,128,256]{3,2,1,0:T(8,128)(2,1)S(1)}, u32[]{:S(2)}) copy-start(bf16[4,8,128,256]{3,2,1,0:T(8,128)(2,1)S(1)} %slice.103) | copy-start | bytes 6291460
  254.8 11.1 %copy-start.8 = (bf16[3,256,1024]{2,1,0:T(8,128)(2,1)S(1)}, bf16[3,256,1024]{2,1,0:T(8,128)(2,1)}, u32[]{:S(2)}) copy-start(bf16[3,256,1024]{2,1,0:T(8,128)(2,1)} %tok.1) | copy-start | bytes 4718596
  266.0 2.6 copy-start.4
  266.0 10.2 %copy-start.6 = (bf16[4,8,128,768]{3,2,1,0:T(8,128)(2,1)}, bf16[4,8,128,768]{3,2,1,0:T(8,128)(2,1)S(1)}, u32[]{:S(2)}) copy-start(bf16[4,8,128,768]{3,2,1,0:T(8,128)(2,1)S(1)} %get-tuple-element.98) | copy-start | bytes 18874372
  268.6 7.6 copy-start.16
  276.2 7.7 copy-start.18
  302.8 18.2 %copy-start.7 = (bf16[4,8,128,768]{3,2,1,0:T(8,128)(2,1)S(1)}, bf16[4,8,128,768]{3,2,1,0:T(8,128)(2,1)}, u32[]{:S(2)}) copy-start(bf16[4,8,128,768]{3,2,1,0:T(8,128)(2,1)} %copy-done.6) | copy-start | bytes 18874372
  302.8 18.2 %copy-start.26 = (bf16[4,768,768]{1,2,0:T(8,128)(2,1)S(1)}, bf16[4,768,768]{1,2,0:T(8,128)(2,1)}, u32[]{:S(2)}) copy-start(bf16[4,768,768]{1,2,0:T(8,128)(2,1)} %get-tuple-element.100) | copy-start | bytes 14155780
  321.0 5.1 copy-start.5
  321.0 5.1 copy-start.25
  326.2 6.1 copy-start.19
  332.3 1.6 copy-start.14
  333.9 155.7 %copy-start.2 = (f32[768,1024]{1,0:T(8,128)}, f32[768,1024]{1,0:T(8,128)S(1)}, u32[]{:S(2)}) copy-start(f32[768,1024]{1,0:T(8,128)S(1)} %multiply_add_fusion) | copy-start | bytes 9437188
  489.6 4.8 copy-start.17
  489.6 14.3 %slice-start.1 = ((s8[4718592]{0:T(1024)(128)(4,1)}), s8[4194304]{0:T(1024)(128)(4,1)S(1)}, s32[]{:S(2)}) async-start(s8[4718592]{0:T(1024)(128)(4,1)} %bitcast.211), calls=%async_computation.1 | async-start | bytes 8388608
  494.4 9.5 %slice-start.2 = ((s8[4718592]{0:T(1024)(128)(4,1)}), s8[524288]{0:T(1024)(128)(4,1)S(1)}, s32[]{:S(2)}) async-start(s8[4718592]{0:T(1024)(128)(4,1)} %bitcast.211), calls=%async_computation.2 | async-start | bytes 1048576
  519.1 4.9 copy-start.24
  519.1 4.9 copy-start.27
  521.8 2.1 copy-start.1
  551.2 2.8 copy-start
  553.9 3.4 copy-start.12
  557.3 1.9 slice-start
  557.3 2.3 copy-start.9
  557.3 3.6 copy-start.10
  557.4 3.6 copy-start.21
  557.4 3.6 copy-start.22
  561.0 45.7 %copy-start.3 = (f32[768,1024]{1,0:T(8,128)S(1)}, f32[768,1024]{1,0:T(8,128)}, u32[]{:S(2)}) copy-start(f32[768,1024]{1,0:T(8,128)} %copy-done.2) | copy-start | bytes 9437188
  606.7 4.9 copy-start.20
  611.6 9.5 %copy-start.11 = (bf16[4,1024,256]{1,2,0:T(8,128)(2,1)S(1)}, bf16[4,1024,256]{1,2,0:T(8,128)(2,1)}, u32[]{:S(2)}) copy-start(bf16[4,1024,256]{1,2,0:T(8,128)(2,1)} %convert_bitcast_fusion.3) | copy-start | bytes 6291460

commit v2 on v1

--- a/solution.py
+++ b/solution.py
@@ -367,12 +367,12 @@
 
 def rope_tables():
     half = HEAD_DIM // 2
-    inverse = THETA ** (-2.0 * jnp.arange(half, dtype=jnp.float32) / HEAD_DIM)
-    angles = jnp.arange(1024, dtype=jnp.int32).astype(jnp.float32)[:, None] * inverse[None, :]
-    cosine, sine = jnp.cos(angles), jnp.sin(angles)
+    inverse = (THETA ** (-2.0 * np.arange(half) / HEAD_DIM)).astype(np.float32)
+    angles = np.arange(1024, dtype=np.float32)[:, None] * inverse[None, :]
+    cosine, sine = np.cos(angles), np.sin(angles)
     return (
-        jnp.concatenate([cosine] * 4, axis=1),
-        jnp.concatenate([-sine, sine, -sine, sine], axis=1),
+        jnp.asarray(np.concatenate([cosine] * 4, axis=1), jnp.float32),
+        jnp.asarray(np.concatenate([-sine, sine, -sine, sine], axis=1), jnp.float32),
     )
 
 
@@ -380,8 +380,8 @@
 F32 = jnp.float32
 MESH = pl.DeviceIdType.MESH
 CHUNK = 256
-HP = 768
-PADW = 2560
+FFC = 704
+PIECE = 3 * FFC + 256
 QROWS = 400
 
 
@@ -559,9 +559,9 @@
 
 
 def forward_kernel(
-    seq, tok, fv, wq, wk, wv, wo, wg, wu, wd, gains, cos_t, sin_t,
-    f1, f2, qkv, o_head, lse, o_rows, a1, gain_out,
-    stage, p2, *sems,
+    seq, tok, fv, wq, wk, wv, wo, wg_t, wu_t, wd_t, gain_attn, gain_mlp, cos_t, sin_t,
+    f1, f2, qkv, o_head, lse, o_rows, a1_t, gain_out,
+    a1, stage, p2, *sems,
 ):
     p = Place()
     sems = list(sems)
@@ -573,16 +573,15 @@
     f1[z, d, 0:128] = wq[...]
     f1[z, d, 128:256] = wk[...]
     f1[z, d, 256:384] = wv[...]
-    f1[z, d, 384:400] = gains[...]
+    f1[z, d, 384:400, 0:128] = jnp.broadcast_to(gain_attn[...], (16, 128))
+    f1[z, d, 384:400, 128:256] = jnp.broadcast_to(gain_mlp[...], (16, 128))
     g1 = Gather(p, lambda m, e: f1.at[m, e], f1.at[0, 0], g1s)
     g2 = Gather(p, lambda m, e: f2.at[m, e], p2, g2s)
     g1.along_z(z)
     g1.spread(z)
-    p2[...] = jnp.zeros_like(p2)
-    p2[:, 0:256] = wo[...]
-    p2[:, 256:960] = wg[...]
-    p2[:, 1024:1728] = wu[...]
-    p2[:, 1792:2496] = wd[...]
+    for i, source in enumerate((wg_t, wu_t, wd_t)):
+        p2[i * FFC : (i + 1) * FFC, :] = source[...]
+    p2[3 * FFC :, :] = wo[...].T
     own_copy = pltpu.make_async_copy(p2, f2.at[z, d], s_local)
     own_copy.start()
 
@@ -718,6 +717,7 @@
         project(b)
         if b == 0:
             send_qkv(0)
+    a1_t[...] = a1[...].T
     p.hop(1, g2.z_in)
     sent_qkv(0)
     send_qkv(1)
@@ -769,7 +769,7 @@
     own_copy.wait()
 
 
-def run_forward(seq, tok, fv, wq, wk, wv, wo, wg, wu, wd, gains, cos_t, sin_t):
+def run_forward(*args):
     vmem = pl.BlockSpec(memory_space=pltpu.VMEM)
     hbm = pl.BlockSpec(memory_space=pl.ANY)
     dma = pltpu.SemaphoreType.DMA
@@ -778,19 +778,20 @@
         forward_kernel,
         out_shape=(
             shape((4, 8, QROWS, CHUNK), BF),
-            shape((4, 8, 128, PADW), BF),
+            shape((4, 8, PIECE, 128), BF),
             shape((3, 3, 1024, CHUNK), BF),
             shape((3, 1024, CHUNK), BF),
             shape((3, 1024, 128), F32),
             shape((3, 4, CHUNK, CHUNK), BF),
-            shape((768, 1024), BF),
+            shape((1024, 768), BF),
             shape((8, 1024), F32),
         ),
-        in_specs=[pl.BlockSpec(memory_space=pltpu.SMEM)] + [vmem] * 12,
+        in_specs=[pl.BlockSpec(memory_space=pltpu.SMEM)] + [vmem] * (len(args) - 1),
         out_specs=(vmem, hbm, vmem, vmem, vmem, vmem, vmem, vmem),
         scratch_shapes=[
+            pltpu.VMEM((768, 1024), BF),
             pltpu.VMEM((3, 4, 3, CHUNK, CHUNK), BF),
-            pltpu.VMEM((128, PADW), BF),
+            pltpu.VMEM((PIECE, 128), BF),
         ]
         + gather_sems()
         + gather_sems()
@@ -800,16 +801,180 @@
         ),
         cost_estimate=pl.CostEstimate(flops=2 * 10**10, bytes_accessed=6 * 10**7, transcendentals=8 * 10**6),
         name="gather_attend",
-    )(seq, tok, fv, wq, wk, wv, wo, wg, wu, wd, gains, cos_t, sin_t)
+    )(*args)
+
+
+def spans(n, step):
+    return [(at, min(step, n - at)) for at in range(0, n, step)]
+
+
+def mlp_kernel(
+    tok, cot, o_rows, f2, gain,
+    layer_out, dx2, do_rows, part, gain_part,
+    w, wo, a2, hid, dga, dup, acc, back, stage, wo_stage, in_sems, wo_sems, out_sems, wo_out,
+):
+    def w_copy(m, slot, d):
+        return pltpu.make_async_copy(
+            f2.at[m, d, 0 : 3 * FFC, :], w.at[slot, :, d * 128 : (d + 1) * 128], in_sems.at[slot, d]
+        )
+
+    def wo_copy(m, d):
+        return pltpu.make_async_copy(
+            f2.at[m, d, 3 * FFC :, :], wo.at[m, :, d * 128 : (d + 1) * 128], wo_sems.at[m, d]
+        )
+
+    def out_copy(m, slot):
+        return pltpu.make_async_copy(stage.at[slot], part.at[m, :, 0 : 3 * FFC, :], out_sems.at[slot])
+
+    def wo_out_copy(m):
+        return pltpu.make_async_copy(wo_stage.at[m], part.at[m, :, 3 * FFC :, :], wo_out.at[m])
+
+    for m in range(4):
+        for d in range(8):
+            wo_copy(m, d).start()
+    for d in range(8):
+        w_copy(0, 0, d).start()
+    for m in range(4):
+        for d in range(8):
+            wo_copy(m, d).wait()
+
+    def row_block(b):
+        return pl.ds(pl.multiple_of(b * CHUNK, CHUNK), CHUNK)
+
+    def enter(b, carry):
+        x2 = tok[b].astype(F32)
+        for m in range(4):
+            x2 = x2 + dot(o_rows[b, m], wo[m])
+        dx2[b] = x2
+        factor = lax.rsqrt(jnp.mean(x2 * x2, axis=1, keepdims=True) + EPSILON)
+        a2[row_block(b), :] = (x2 * factor * gain[0:1, :]).astype(BF)
+        return carry
+
+    lax.fori_loop(0, 3, enter, 0)
+    grad = cot[...].reshape(768, 1024)
+
+    def chunk(m, carry):
+        slot = lax.rem(m, 2)
+        for d in range(8):
+            w_copy(m, slot, d).wait()
+
+        @pl.when(m < 3)
+        def _():
+            for d in range(8):
+                w_copy(m + 1, 1 - slot, d).start()
+
+        @pl.when(m >= 2)
+        def _():
+            out_copy(m - 2, slot).wait()
+
+        for at, size in spans(FFC, 256):
+            cols = slice(at, at + size)
+            gate = dot_nt(a2[...], w[slot, at : at + size, :])
+            up = dot_nt(a2[...], w[slot, FFC + at : FFC + at + size, :])
+            dh = dot_nt(grad, w[slot, 2 * FFC + at : 2 * FFC + at + size, :])
+            sg = jax.nn.sigmoid(gate)
+            act = gate * sg
+            hid[:, cols] = (act * up).astype(BF)
+            dga[:, cols] = (dh * up * (sg + act * (1.0 - sg))).astype(BF)
+            dup[:, cols] = (dh * act).astype(BF)
+            for i, (left, right) in enumerate(((dga, a2[...]), (dup, a2[...]), (hid, grad))):
+                out = dot_tn(left[:, cols], right).astype(BF)
+                for d in range(8):
+                    stage[slot, d, i * FFC + at : i * FFC + at + size, :] = out[:, d * 128 : (d + 1) * 128]
+
+        for at, size in spans(1024, 256):
+            cols = slice(at, at + size)
+            y = dot(hid[...], w[slot, 2 * FFC : 3 * FFC, cols])
+            u = dot(dga[...], w[slot, 0:FFC, cols]) + dot(dup[...], w[slot, FFC : 2 * FFC, cols])
+            acc[:, cols] = jnp.where(m == 0, y, acc[:, cols] + y)
+            back[:, cols] = jnp.where(m == 0, u, back[:, cols] + u)
+
+        out_copy(m, slot).start()
+        return carry
+
+    lax.fori_loop(0, 4, chunk, 0)
+
+    def leave(b, total):
+        x2 = dx2[b]
+        rows = row_block(b)
+        layer_out[b] = (x2 + acc[rows, :]).astype(BF)
+        factor = lax.rsqrt(jnp.mean(x2 * x2, axis=1, keepdims=True) + EPSILON)
+        n2 = x2 * factor
+        da2 = back[rows, :]
+        total = total + jnp.sum(da2 * n2, axis=0, keepdims=True)
+        dn2 = da2 * gain[0:1, :]
+        grad_mid = cot[b].astype(F32) + factor * (
+            dn2 - n2 * jnp.mean(dn2 * n2, axis=1, keepdims=True)
+        )
+        dx2[b] = grad_mid
+        a2[rows, :] = grad_mid.astype(BF)
+        return total
+
+    total = lax.fori_loop(0, 3, leave, jnp.zeros((1, 1024), F32))
+    gain_part[...] = jnp.broadcast_to(total, (8, 1024))
+
+    def heads(m, carry):
+        own = jnp.concatenate([o_rows[b, m] for b in range(3)], axis=0)
+        dw = dot_tn(own, a2[...]).astype(BF)
+        for d in range(8):
+            wo_stage[m, d] = dw[:, d * 128 : (d + 1) * 128]
+        wo_out_copy(m).start()
+        for b in range(3):
+            do_rows[b, m] = dot_nt(a2[b * CHUNK : (b + 1) * CHUNK, :], wo[m]).astype(BF)
+        return carry
+
+    lax.fori_loop(0, 4, heads, 0)
+    out_copy(2, 0).wait()
+    out_copy(3, 1).wait()
+    for m in range(4):
+        wo_out_copy(m).wait()
+
+
+def run_mlp(tok, cot, o_rows, f2, gain):
+    vmem = pl.BlockSpec(memory_space=pltpu.VMEM)
+    hbm = pl.BlockSpec(memory_space=pl.ANY)
+    shape = jax.ShapeDtypeStruct
+    dma = pltpu.SemaphoreType.DMA
+    return pl.pallas_call(
+        mlp_kernel,
+        out_shape=(
+            shape((3, CHUNK, 1024), BF),
+            shape((3, CHUNK, 1024), F32),
+            shape((3, 4, CHUNK, CHUNK), BF),
+            shape((4, 8, PIECE, 128), BF),
+            shape((8, 1024), F32),
+        ),
+        in_specs=[vmem, vmem, vmem, hbm, vmem],
+        out_specs=(vmem, vmem, vmem, hbm, vmem),
+        scratch_shapes=[
+            pltpu.VMEM((2, 3 * FFC, 1024), BF),
+            pltpu.VMEM((4, CHUNK, 1024), BF),
+            pltpu.VMEM((768, 1024), BF),
+            pltpu.VMEM((768, FFC), BF),
+            pltpu.VMEM((768, FFC), BF),
+            pltpu.VMEM((768, FFC), BF),
+            pltpu.VMEM((768, 1024), F32),
+            pltpu.VMEM((768, 1024), F32),
+            pltpu.VMEM((2, 8, 3 * FFC, 128), BF),
+            pltpu.VMEM((4, 8, CHUNK, 128), BF),
+            dma((2, 8)),
+            dma((4, 8)),
+            dma((2,)),
+            dma((4,)),
+        ],
+        compiler_params=pltpu.CompilerParams(vmem_limit_bytes=60 * 2**20),
+        cost_estimate=pl.CostEstimate(flops=5 * 10**10, bytes_accessed=6 * 10**7, transcendentals=2 * 10**6),
+        name="mlp",
+    )(tok, cot, o_rows, f2, gain)
 
 
 def backward_kernel(
-    seq, do_rows, qkv, o_head, lse, cos_t, sin_t,
-    d_rows,
-    do_head, dk, dv, stage, *sems,
+    seq, do_rows, qkv, o_head, lse, cos_t, sin_t, part,
+    d_rows, summed,
+    do_head, dk, dv, stage, *rest,
 ):
     p = Place()
-    s_do, r_do, s_d, r_d = sems
+    s_do, r_do, s_d, r_d = rest[:4]
     z, d = p.z, p.d
     p.greet()
     mine = pl.ds(pl.multiple_of(z * CHUNK, CHUNK), CHUNK)
@@ -871,7 +1036,7 @@
         cosine, sine = wide(cosine), -wide(sine)
         stage[b, i, :, 0:256] = turned(dq * 0.125, cosine, sine).astype(BF)
         stage[b, i, :, 256:512] = turned(dk[rows, :] * 0.125, cosine, sine).astype(BF)
-        stage[b, i, :, 512:768] = dv[rows, :].astype(BF)
+        stage[b, i, :, 512:768] = (dv[rows, :] * 0.5).astype(BF)
 
         @pl.when(z == i)
         def _():
@@ -881,14 +1046,22 @@
         def _():
             d_copy(b, i).start()
 
+    crossing = Crossing(p, lambda m, e: part.at[m, e], rest[4:9], rest[9:], summed, 592)
     for b in range(3):
         send_do(b)
+    plan = crossing.steps()
     for b in range(3):
         take_do(b)
         dk[...] = jnp.zeros_like(dk)
         dv[...] = jnp.zeros_like(dv)
         for i in (3, 2, 1, 0):
             back(b, i)
+            for step in plan[:2]:
+                step()
+            plan = plan[2:]
+    for step in plan:
+        step()
+    crossing.finish()
     for b in range(3):
         for step in (1, 2, 3):
             do_copy(b, step).wait_send()
@@ -901,14 +1074,16 @@
                 d_copy(b, i).wait_send()
 
 
-def run_backward(seq, do_rows, qkv, o_head, lse, cos_t, sin_t):
+def run_backward(*args):
     vmem = pl.BlockSpec(memory_space=pltpu.VMEM)
+    hbm = pl.BlockSpec(memory_space=pl.ANY)
     dma = pltpu.SemaphoreType.DMA
+    shape = jax.ShapeDtypeStruct
     return pl.pallas_call(
         backward_kernel,
-        out_shape=jax.ShapeDtypeStruct((3, 4, CHUNK, 768), BF),
-        in_specs=[pl.BlockSpec(memory_space=pltpu.SMEM)] + [vmem] * 6,
-        out_specs=vmem,
+        out_shape=(shape((3, 4, CHUNK, 768), BF), shape((4, PIECE, 128), BF)),
+        in_specs=[pl.BlockSpec(memory_space=pltpu.SMEM)] + [vmem] * 6 + [hbm],
+        out_specs=(vmem, vmem),
         scratch_shapes=[
             pltpu.VMEM((3, 1024, CHUNK), BF),
             pltpu.VMEM((1024, CHUNK), F32),
@@ -918,221 +1093,379 @@
             dma((3, 4)),
             dma((3, 4)),
             dma((3, 4)),
-        ],
+        ]
+        + crossing_scratch(PIECE, 128),
         compiler_params=pltpu.CompilerParams(
             collective_id=2, has_side_effects=True, vmem_limit_bytes=60 * 2**20
         ),
         cost_estimate=pl.CostEstimate(flops=3 * 10**10, bytes_accessed=2 * 10**7, transcendentals=8 * 10**6),
         name="attend_back",
-    )(seq, do_rows, qkv, o_head, lse, cos_t, sin_t)
+    )(*args)
 
 
 ORDER = (3, 0, 1, 2)
 
 
-class Scatter:
-    def __init__(self, place, part, width, bufs, sems, out):
-        self.p, self.part, self.width, self.out = place, part, width, out
-        self.own, self.other, self.diag_buf, self.bx, self.by, self.br, self.bl = bufs
-        (self.l_own, self.s_core, self.r_core, self.s_diag, self.r_diag,
-         self.s_x, self.r_x, self.s_y, self.r_y, self.s_r, self.r_r, self.s_l, self.r_l) = sems
+def add_rows(dst, terms, step):
+    def rows(r, carry):
+        at = pl.ds(pl.multiple_of(r * step, step), step)
+        total = terms[0][at, :].astype(F32)
+        for term in terms[1:]:
+            total = total + term[at, :].astype(F32)
+        dst[at, :] = total.astype(dst.dtype)
+        return carry
+
+    lax.fori_loop(0, dst.shape[0] // step, rows, 0)
+
+
+class Crossing:
+    def __init__(self, place, part, bufs, sems, out, step):
+        self.p, self.part, self.out, self.step = place, part, out, step
+        self.own, self.acc, self.corner, self.bx, self.by = bufs
+        (self.l_own, self.s_core, self.r_core, self.s_corner, self.r_corner,
+         self.s_x, self.r_x, self.s_y, self.r_y) = sems
 
     def core_copy(self, m, q):
         p = self.p
         return remote(
-            self.part(m, p.core_quads[q]), self.other.at[m, q],
+            self.part(m, p.core_quads[q]), self.acc.at[m, q],
             self.s_core.at[m, q], self.r_core.at[m, q], p.core,
         )
 
     def own_copy(self, m, q):
+        slot = ORDER.index(m) % 2
         return pltpu.make_async_copy(
-            self.part(m, self.p.quads[q]), self.own.at[m, q], self.l_own.at[m, q]
+            self.part(m, self.p.quads[q]), self.own.at[slot, q], self.l_own.at[slot, q]
         )
 
     def begin(self, m):
         for q in (3, 1, 2, 0):
             self.core_copy(m, q).start()
+
+    def load(self, m):
+        for q in (3, 1, 2, 0):
             self.own_copy(m, q).start()
 
-    def add(self, dst, *terms):
-        step = 16
-
-        def rows(r, carry):
-            at = pl.ds(pl.multiple_of(r * step, step), step)
-            total = dst[at, :].astype(F32)
-            for t in terms:
-                total = total + t[at, :].astype(F32)
-            dst[at, :] = total.astype(dst.dtype)
-            return carry
-
-        lax.fori_loop(0, 128 // step, rows, 0)
-
-    def joined(self, m, q, *more):
-        self.own_copy(m, q).wait()
-        self.core_copy(m, q).wait_recv()
-        self.add(self.own.at[m, q], self.other.at[m, q], *more)
-
-    def diag_copy(self, m):
+    def corner_copy(self, m):
         to = self.p.x if m % 2 == 0 else self.p.y
-        return remote(self.own.at[m, 3], self.diag_buf.at[m], self.s_diag.at[m], self.r_diag.at[m], to)
+        return remote(self.acc.at[m, 3], self.corner.at[m], self.s_corner.at[m], self.r_corner.at[m], to)
 
     def x_copy(self, m):
-        return remote(self.own.at[m, 1], self.bx.at[m], self.s_x.at[m], self.r_x.at[m], self.p.x)
+        return remote(self.acc.at[m, 1], self.bx.at[m], self.s_x.at[m], self.r_x.at[m], self.p.x)
 
     def y_copy(self, m):
-        return remote(self.own.at[m, 2], self.by.at[m], self.s_y.at[m], self.r_y.at[m], self.p.y)
-
-    def r_copy(self, m):
-        return remote(
-            self.own.at[m, 0], self.br.at[m], self.s_r.at[m], self.r_r.at[m], (self.p.d, self.p.z + 1)
-        )
-
-    def l_copy(self, m):
-        return remote(
-            self.own.at[m, 0], self.bl.at[m], self.s_l.at[m], self.r_l.at[m], (self.p.d, self.p.z - 1)
-        )
-
-    def diag(self, m):
-        self.joined(m, 3)
-        self.diag_copy(m).start()
-
-    def direct(self, m):
-        self.joined(m, 1 if m % 2 == 0 else 2)
-        (self.x_copy if m % 2 == 0 else self.y_copy)(m).start()
+        return remote(self.acc.at[m, 2], self.by.at[m], self.s_y.at[m], self.r_y.at[m], self.p.y)
+
+    def join(self, m):
+        slot = ORDER.index(m) % 2
+        first = 1 if m % 2 == 0 else 2
+        for q in (3, first, 3 - first, 0):
+            self.own_copy(m, q).wait()
+            self.core_copy(m, q).wait_recv()
+            add_rows(self.acc.at[m, q], [self.acc.at[m, q], self.own.at[slot, q]], self.step)
+            if q == 3:
+                self.corner_copy(m).start()
+            if q == first:
+                (self.x_copy if m % 2 == 0 else self.y_copy)(m).start()
 
     def relay(self, m):
-        self.diag_copy(m).wait_recv()
-        self.joined(m, 2 if m % 2 == 0 else 1, self.diag_buf.at[m])
+        q = 2 if m % 2 == 0 else 1
+        self.corner_copy(m).wait_recv()
+        add_rows(self.acc.at[m, q], [self.acc.at[m, q], self.corner.at[m]], self.step)
         (self.y_copy if m % 2 == 0 else self.x_copy)(m).start()
 
-    def quad_sum(self, m):
-        self.own_copy(m, 0).wait()
-        self.core_copy(m, 0).wait_recv()
+    def total(self, m):
         self.x_copy(m).wait_recv()
         self.y_copy(m).wait_recv()
-        self.add(self.own.at[m, 0], self.other.at[m, 0], self.bx.at[m], self.by.at[m])
-
-    def along_z(self, m):
+        add_rows(self.out.at[m], [self.acc.at[m, 0], self.bx.at[m], self.by.at[m]], self.step)
+
+    def finish(self):
+        for m in range(4):
+            for q in range(4):
+                self.core_copy(m, q).wait_send()
+            self.corner_copy(m).wait_send()
+            self.x_copy(m).wait_send()
+            self.y_copy(m).wait_send()
+
+    def steps(self):
+        a, b, c, e = ORDER
+
+        def start():
+            for m in ORDER:
+                self.begin(m)
+            self.load(a)
+            self.load(b)
+
+        def join_then_load(m, after):
+            self.join(m)
+            self.load(after)
+
+        return [
+            start,
+            lambda: join_then_load(a, c),
+            lambda: join_then_load(b, e),
+            lambda: self.relay(a),
+            lambda: self.relay(b),
+            lambda: self.join(c),
+            lambda: self.join(e),
+            lambda: self.total(a),
+            lambda: self.total(b),
+            lambda: self.relay(c),
+            lambda: self.relay(e),
+            lambda: self.total(c),
+            lambda: self.total(e),
+        ]
+
+
+def crossing_scratch(rows, width):
+    def buf(*lead):
+        return pltpu.VMEM((*lead, rows, width), BF)
+
+    dma = pltpu.SemaphoreType.DMA
+    return [buf(2, 4), buf(4, 4), buf(4), buf(4), buf(4), dma((2, 4)), dma((4, 4)), dma((4, 4))] + [dma((4,))] * 6
+
+
+class Chain:
+    def __init__(self, place, part, bufs, sems, out, step):
+        self.p, self.part, self.out, self.step = place, part, out, step
+        self.br, self.bl = bufs
+        self.s_r, self.r_r, self.s_l, self.r_l = sems
+
+    def r_copy(self, m):
+        p = self.p
+        return remote(self.part.at[m], self.br.at[m], self.s_r.at[m], self.r_r.at[m], (p.d, p.z + 1))
+
+    def l_copy(self, m):
+        p = self.p
+        return remote(self.part.at[m], self.bl.at[m], self.s_l.at[m], self.r_l.at[m], (p.d, p.z - 1))
+
+    def along(self, m):
         z = self.p.z
 
         if m > 0:
+
             @pl.when(z < m)
             def _():
                 @pl.when(z > 0)
                 def _():
                     self.r_copy(m).wait_recv()
-                    self.add(self.own.at[m, 0], self.br.at[m])
+                    add_rows(self.part.at[m], [self.part.at[m], self.br.at[m]], self.step)
 
                 self.r_copy(m).start()
 
         if m < 3:
+
             @pl.when(z > m)
             def _():
                 @pl.when(z < 3)
                 def _():
                     self.l_copy(m).wait_recv()
-                    self.add(self.own.at[m, 0], self.bl.at[m])
+                    add_rows(self.part.at[m], [self.part.at[m], self.bl.at[m]], self.step)
 
                 self.l_copy(m).start()
 
     def last(self):
-        z = self.p.z
-        step = 16
-
         for m in range(4):
-            @pl.when(z == m)
+
+            @pl.when(self.p.z == m)
             def _():
-                terms = [self.own.at[m, 0]]
+                terms = [self.part.at[m]]
                 if m > 0:
                     self.r_copy(m).wait_recv()
                     terms.append(self.br.at[m])
                 if m < 3:
                     self.l_copy(m).wait_recv()
                     terms.append(self.bl.at[m])
-
-                def rows(r, carry):
-                    at = pl.ds(pl.multiple_of(r * step, step), step)
-                    total = terms[0][at, :].astype(F32)
-                    for t in terms[1:]:
-                        total = total + t[at, :].astype(F32)
-                    self.out[at, :] = total
-                    return carry
-
-                lax.fori_loop(0, 128 // step, rows, 0)
+                add_rows(self.out, terms, self.step)
 
     def finish(self):
-        z = self.p.z
         for m in range(4):
-            for q in range(4):
-                self.core_copy(m, q).wait_send()
-            self.diag_copy(m).wait_send()
-            self.x_copy(m).wait_send()
-            self.y_copy(m).wait_send()
             if m > 0:
-                @pl.when(z < m)
+
+                @pl.when(self.p.z < m)
                 def _():
                     self.r_copy(m).wait_send()
+
             if m < 3:
-                @pl.when(z > m)
+
+                @pl.when(self.p.z > m)
                 def _():
                     self.l_copy(m).wait_send()
 
-    def steps(self):
-        a, b, c, e = ORDER
-        return [
-            lambda: self.begin(a), lambda: self.begin(b), lambda: self.diag(a), lambda: self.diag(b),
-            lambda: self.begin(c), lambda: self.direct(a), lambda: self.direct(b),
-            lambda: self.begin(e), lambda: self.diag(c), lambda: self.diag(e),
-            lambda: self.relay(a), lambda: self.relay(b), lambda: self.direct(c), lambda: self.direct(e),
-            lambda: self.quad_sum(a), lambda: self.along_z(a), lambda: self.quad_sum(b), lambda: self.along_z(b),
-            lambda: self.relay(c), lambda: self.relay(e),
-            lambda: self.quad_sum(c), lambda: self.along_z(c), lambda: self.quad_sum(e), lambda: self.along_z(e),
-            self.last,
-        ]
-
-
-def scatter_buffers(width):
-    def buf(*lead):
-        return pltpu.VMEM((*lead, 128, width), BF)
-
-    return [buf(4, 4), buf(4, 4), buf(4), buf(4), buf(4), buf(4), buf(4)]
-
-
-def scatter_sems():
+
+def chain_scratch(rows, width):
     dma = pltpu.SemaphoreType.DMA
-    return [dma((4, 4))] * 3 + [dma((4,))] * 10
-
-
-def scatter_kernel(part1, part2, out1, out2, *rest):
-    rest = list(rest)
-    bufs1, bufs2, sems1, sems2 = rest[:7], rest[7:14], rest[14:27], rest[27:40]
+    return [pltpu.VMEM((4, rows, width), BF)] * 2 + [dma((4,))] * 4
+
+
+def finish_kernel(
+    tok, mid, d_rows, a1_t, f1, gain_part, summed,
+    grad_tokens, grad_first, dw1, dw2, gain_sum,
+    part, acc, total1, total2, gbuf, *rest,
+):
     p = Place()
     p.greet()
-    big = Scatter(p, lambda m, d: part2.at[m, d], PADW, bufs2, sems2, out2)
-    small = Scatter(p, lambda m, d: part1.at[m, d], 768, bufs1, sems1, out1)
-    for a, b in zip(big.steps(), small.steps()):
-        a()
-        b()
-    big.finish()
-    small.finish()
-
-
-def run_scatter(part1, part2):
+    rest = list(rest)
+    cross = Crossing(p, lambda m, e: part.at[m, e], rest[:5], rest[5:14], total1, 16)
+    chain1 = Chain(p, total1, rest[14:16], rest[16:20], dw1, 16)
+    chain2 = Chain(p, total2, rest[20:22], rest[22:26], dw2, 592)
+    s_gain, r_gain, l_total = rest[26:29]
+
+    def total_copy(m):
+        return pltpu.make_async_copy(summed.at[m], total2.at[m], l_total.at[m])
+
+    def along2(m):
+        total_copy(m).wait()
+        chain2.along(m)
+
+    for m in ORDER:
+        total_copy(m).start()
+
+    def weight_grad(m):
+        cols = jnp.concatenate([d_rows[b, m] for b in range(3)], axis=0)
+
+        def rows(k, carry):
+            at = pl.ds(pl.multiple_of(k * CHUNK, CHUNK), CHUNK)
+            part[m, pl.ds(2 * k, 2)] = dot(a1_t[at, :], cols).astype(BF).reshape(2, 128, 768)
+            return carry
+
+        lax.fori_loop(0, 4, rows, 0)
+
+    def input_grad(m):
+        cols = jnp.concatenate([d_rows[b, m] for b in range(3)], axis=0)
+
+        def tile(k, carry):
+            w = jnp.concatenate(
+                [f1[m, pl.ds(2 * k, 2), i * 128 : (i + 1) * 128, :].reshape(CHUNK, CHUNK) for i in range(3)],
+                axis=1,
+            )
+            at = pl.ds(pl.multiple_of(k * CHUNK, CHUNK), CHUNK)
+            y = dot_nt(cols, w)
+            if m == 0:
+                acc[:, at] = y
+            else:
+                acc[:, at] += y
+            return carry
+
+        lax.fori_loop(0, 4, tile, 0)
+
+    def leave(b, total):
+        x = tok[b].astype(F32)
+        factor = lax.rsqrt(jnp.mean(x * x, axis=1, keepdims=True) + EPSILON)
+        n1 = x * factor
+        da1 = acc[pl.ds(pl.multiple_of(b * CHUNK, CHUNK), CHUNK), :]
+        total = total + jnp.sum(da1 * n1, axis=0, keepdims=True)
+        gain = jnp.concatenate([f1[0, e, 384:400, 0:128].astype(F32)[0:1] for e in range(8)], axis=1)
+        dn1 = da1 * gain
+        grad_tokens[b] = mid[b] + factor * (dn1 - n1 * jnp.mean(dn1 * n1, axis=1, keepdims=True))
+        for m in range(4):
+            grad_first[b, :, m * CHUNK : (m + 1) * CHUNK] = d_rows[b, m, :, 512:768].astype(F32)
+        return total
+
+    def gain_copy(i, device):
+        return remote(gbuf.at[0] if i == 0 else gbuf.at[4 + i], gbuf.at[1 + i], s_gain.at[i], r_gain.at[i], device)
+
+    a, b, c, e = ORDER
+    weight_grad(a)
+    cross.begin(a)
+    cross.load(a)
+    along2(a)
+    weight_grad(b)
+    cross.begin(b)
+    cross.load(b)
+    along2(b)
+    cross.join(a)
+    weight_grad(c)
+    cross.begin(c)
+    cross.load(c)
+    along2(c)
+    cross.join(b)
+    weight_grad(e)
+    cross.begin(e)
+    cross.load(e)
+    along2(e)
+    cross.relay(a)
+    cross.relay(b)
+    cross.join(c)
+    cross.join(e)
+    input_grad(0)
+    cross.relay(c)
+    cross.relay(e)
+    cross.total(a)
+    chain1.along(a)
+    input_grad(1)
+    cross.total(b)
+    chain1.along(b)
+    input_grad(2)
+    input_grad(3)
+    cross.total(c)
+    chain1.along(c)
+    cross.total(e)
+    chain1.along(e)
+    total = lax.fori_loop(0, 3, leave, jnp.zeros((1, 1024), F32))
+    row = lax.broadcasted_iota(jnp.int32, (8, 1024), 0)
+    gbuf[0] = jnp.where(row == 0, total, gain_part[...])
+    gain_copy(0, p.core).start()
+    chain2.last()
+    gain_copy(0, p.core).wait_recv()
+    gbuf[5] = gbuf[0] + gbuf[1]
+    gain_copy(1, p.x).start()
+    chain1.last()
+    gain_copy(1, p.x).wait_recv()
+    gbuf[6] = gbuf[5] + gbuf[2]
+    gain_copy(2, p.y).start()
+    gain_copy(2, p.y).wait_recv()
+    gbuf[7] = gbuf[6] + gbuf[3]
+    for step in (1, 2, 3):
+        m = p.peer(step)
+        remote(gbuf.at[7], gbuf.at[8 + p.z], s_gain.at[2 + step], r_gain.at[3 + p.z], (p.d, m)).start()
+    gbuf[8 + p.z] = gbuf[7]
+    for step in (1, 2, 3):
+        m = p.peer(step)
+        remote(gbuf.at[7], gbuf.at[8 + m], s_gain.at[2 + step], r_gain.at[3 + m], (p.d, m)).wait_recv()
+    gain_sum[...] = (gbuf[8] + gbuf[9]) + (gbuf[10] + gbuf[11])
+    for i, device in enumerate((p.core, p.x, p.y)):
+        gain_copy(i, device).wait_send()
+    for step in (1, 2, 3):
+        m = p.peer(step)
+        remote(gbuf.at[7], gbuf.at[8 + m], s_gain.at[2 + step], r_gain.at[3 + m], (p.d, m)).wait_send()
+    cross.finish()
+    chain1.finish()
+    chain2.finish()
+
+
+def run_finish(*args):
     vmem = pl.BlockSpec(memory_space=pltpu.VMEM)
-    hbm = pl.BlockSpec(memory_space=pl.ANY)
+    dma = pltpu.SemaphoreType.DMA
     shape = jax.ShapeDtypeStruct
     return pl.pallas_call(
-        scatter_kernel,
-        out_shape=(shape((128, 768), F32), shape((128, PADW), F32)),
-        in_specs=[hbm, hbm],
-        out_specs=(vmem, vmem),
-        scratch_shapes=scatter_buffers(768) + scatter_buffers(PADW) + scatter_sems() + scatter_sems(),
+        finish_kernel,
+        out_shape=(
+            shape((3, CHUNK, 1024), F32),
+            shape((3, CHUNK, 1024), F32),
+            shape((128, 768), F32),
+            shape((PIECE, 128), F32),
+            shape((8, 1024), F32),
+        ),
+        in_specs=[vmem] * (len(args) - 1) + [pl.BlockSpec(memory_space=pl.ANY)],
+        out_specs=(vmem,) * 5,
+        scratch_shapes=[
+            pltpu.VMEM((4, 8, 128, 768), BF),
+            pltpu.VMEM((768, 1024), F32),
+            pltpu.VMEM((4, 128, 768), BF),
+            pltpu.VMEM((4, PIECE, 128), BF),
+            pltpu.VMEM((12, 8, 1024), F32),
+        ]
+        + crossing_scratch(128, 768)
+        + chain_scratch(128, 768)
+        + chain_scratch(PIECE, 128)
+        + [dma((6,)), dma((7,)), dma((4,))],
         compiler_params=pltpu.CompilerParams(
             collective_id=3, has_side_effects=True, vmem_limit_bytes=60 * 2**20
         ),
-        cost_estimate=pl.CostEstimate(flops=10**7, bytes_accessed=5 * 10**7, transcendentals=0),
+        cost_estimate=pl.CostEstimate(flops=10**10, bytes_accessed=5 * 10**7, transcendentals=0),
         name="sum_grads",
-    )(part1, part2)
+    )(*args)
 
 
 def fast_body(
@@ -1140,79 +1473,27 @@
     gain_attn, gain_mlp, cotangent,
 ):
     seq = sequences[:, 0]
-    gains = jnp.zeros((16, CHUNK), BF).at[0, :128].set(gain_attn).at[0, 128:].set(gain_mlp)
     cos_t, sin_t = rope_tables()
-    f1, f2, qkv, o_head, lse, o_rows, a1, gain_out = run_forward(
-        seq, tokens, first_values, w_query, w_key, w_value, w_out, w_gate, w_up, w_down, gains, cos_t, sin_t
+    f1, f2, qkv, o_head, lse, o_rows, a1_t, gain_out = run_forward(
+        seq, tokens, first_values, w_query, w_key, w_value, w_out, w_gate.T, w_up.T, w_down.T,
+        gain_attn[None, :], gain_mlp[None, :], cos_t, sin_t,
     )
-    gain_two = gain_out[0]
-    dotf = lambda eq, a, b: jnp.einsum(eq, a, b, preferred_element_type=F32)
-    wo = f2[:, :, :, 0:256].reshape(4, 1024, 256)
-    wg = f2[:, :, :, 256:1024].reshape(4, 1024, HP)
-    wu = f2[:, :, :, 1024:1792].reshape(4, 1024, HP)
-    wd = f2[:, :, :, 1792:2560].reshape(4, 1024, HP)
-    x = tokens.reshape(768, 1024).astype(F32)
-    g16 = cotangent.reshape(768, 1024)
-    o_cols = o_rows.transpose(1, 0, 2, 3).reshape(4, 768, 256)
-    x2 = x + dotf("mrc,mdc->rd", o_cols, wo)
-    r2 = lax.rsqrt(jnp.mean(x2 * x2, axis=-1, keepdims=True) + EPSILON)
-    n2 = x2 * r2
-    a2 = (n2 * gain_two[None, :]).astype(BF)
-    gate = dotf("rd,mdc->mrc", a2, wg)
-    up = dotf("rd,mdc->mrc", a2, wu)
-    sg = jax.nn.sigmoid(gate)
-    h = (gate * sg * up).astype(BF)
-    layer_out = (x2 + dotf("mrc,mdc->rd", h, wd)).astype(BF).reshape(3, 256, 1024)
-    dh = dotf("rd,mdc->mrc", g16, wd)
-    dgate = (dh * up * sg * (1.0 + gate * (1.0 - sg))).astype(BF)
-    dup = (dh * gate * sg).astype(BF)
-    da2 = dotf("mrc,mdc->rd", dgate, wg) + dotf("mrc,mdc->rd", dup, wu)
-    part_gain2 = jnp.sum(da2 * n2, axis=0)
-    dn2 = da2 * gain_two[None, :]
-    dx2 = g16.astype(F32) + r2 * (dn2 - n2 * jnp.mean(dn2 * n2, axis=-1, keepdims=True))
-    dattn = dx2.astype(BF)
-    do_rows = dotf("rd,mdc->mrc", dattn, wo).astype(BF).reshape(4, 3, 256, 256).transpose(1, 0, 2, 3)
-    d_rows = run_backward(seq, do_rows, qkv, o_head, lse, cos_t, sin_t)
-    gw2 = jnp.concatenate(
-        [
-            dotf("rd,mrc->mdc", dattn, o_cols).astype(BF),
-            dotf("rd,mrc->mdc", a2, dgate).astype(BF),
-            dotf("rd,mrc->mdc", a2, dup).astype(BF),
-            dotf("rd,mrc->mdc", g16, h).astype(BF),
-        ],
-        axis=-1,
-    ).reshape(4, 8, 128, PADW)
-    dcols = d_rows.transpose(1, 0, 2, 3).reshape(4, 768, 768)
-    scale = jnp.concatenate([jnp.ones((512,), F32), jnp.full((256,), 0.5, F32)])
-    gw1 = (dotf("rd,mrc->mdc", a1, dcols) * scale).astype(BF).reshape(4, 8, 128, 768)
-    w1 = f1[:, :, 0:384, :].reshape(4, 8, 3, 128, 256)
-    dc = dcols.reshape(4, 768, 3, 256)
-    da1 = (
-        dotf("mrac,mdac->rd", dc[:, :, 0:2], w1[:, :, 0:2].transpose(0, 1, 3, 2, 4).reshape(4, 1024, 2, 256))
-        + 0.5 * dotf("mrc,mdc->rd", dc[:, :, 2], w1[:, :, 2].reshape(4, 1024, 256))
-    )
-    r1 = lax.rsqrt(jnp.mean(x * x, axis=-1, keepdims=True) + EPSILON)
-    n1 = x * r1
-    gain_one = f1[0, :, 384, 0:128].reshape(1024).astype(F32)
-    part_gain1 = jnp.sum(da1 * n1, axis=0)
-    dn1 = da1 * gain_one[None, :]
-    grad_tokens = dx2 + r1 * (dn1 - n1 * jnp.mean(dn1 * n1, axis=-1, keepdims=True))
-    grad_first = 0.5 * d_rows[:, :, :, 512:768].transpose(0, 2, 1, 3).reshape(3, 256, 1024).astype(F32)
-    s1, s2 = run_scatter(gw1, gw2)
-    gain_sums = lax.psum(jnp.stack([part_gain1, part_gain2]), ("dp", "mp"))
+    layer_out, mid, do_rows, part, gain_part = run_mlp(tokens, cotangent, o_rows, f2, gain_out)
+    d_rows, summed = run_backward(seq, do_rows, qkv, o_head, lse, cos_t, sin_t, part)
+    grad_tokens, grad_first, dw1, dw2, gain_sum = run_finish(tokens, mid, d_rows, a1_t, f1, gain_part, summed)
     place = (lax.axis_index("dp") * 4 + lax.axis_index("mp")) * 32
-    gain_mine = lax.dynamic_slice(gain_sums, (0, place), (2, 32))
+    gain_mine = lax.dynamic_slice(gain_sum, (0, place), (2, 32))
     return (
         layer_out,
-        grad_tokens.reshape(3, 256, 1024),
+        grad_tokens,
         grad_first,
-        s1[:, 0:256],
-        s1[:, 256:512],
-        s1[:, 512:768],
-        s2[:, 0:256],
-        s2[:, 256:960],
-        s2[:, 1024:1728],
-        s2[:, 1792:2496],
+        dw1[:, 0:256],
+        dw1[:, 256:512],
+        dw1[:, 512:768],
+        dw2[3 * FFC :].T,
+        dw2[0:FFC].T,
+        dw2[FFC : 2 * FFC].T,
+        dw2[2 * FFC : 3 * FFC].T,
         gain_mine[0],
         gain_mine[1],
     )

time: 871 us -> 613 us (0.70)
  the two profiles are of different devices: /device:TPU:17 before, /device:TPU:0 now
where the time goes in v2:
time: 613 us; the launch traced here: 609 us
  Pallas kernels  597 us (97%)
  local copies, waits for them, and re-layouts  11.8 us (2%)
    pallas_call x1, Pallas kernels, run_forward(): pl.pallas_call(forward_kernel, out_shape=(shape((4, 8, QROWS, CHUNK), BF)...  231 us
    pallas_call x1, Pallas kernels, run_backward(): pl.pallas_call(backward_kernel, out_shape=(shape((3, 4, CHUNK, 768), BF),...  184 us
    pallas_call x1, Pallas kernels, run_finish(): pl.pallas_call(finish_kernel, out_shape=(shape((3, CHUNK, 1024), F32), sh...  118 us
    pallas_call x1, Pallas kernels, run_mlp(): pl.pallas_call(mlp_kernel, out_shape=(shape((3, CHUNK, 1024), BF), shape(...  64 us

profile of v2, /device:TPU:0, one launch (start us, length us, event | category | flops | bytes accessed | tf_op | source)
XLA Modules:
  0.0 609.4 jit_solution(14979596882236161952)
XLA Ops:
  0.6 231.0 %gather_attend.1 = (bf16[4,8,400,256]{3,2,1,0:T(8,128)(2,1)}, bf16[4,8,2368,128]{3,2,1,0:T(8,128)(2,1)}, bf16[3,3,1024,256]{3,2,1,0:T(8,128)(2,1)}, bf16[3,1024,...) custom-call(s32[3]{0:T(128)} %bitcast.23, ...), custom_call_target="tpu_custom_call" | custom-call | flops 20000000000 | bytes 60000000 | tf_op jit(solution)/shard_map/gather_attend/pallas_call | solution.py:777
  231.7 64.0 %mlp.1 = (bf16[3,256,1024]{2,1,0:T(8,128)(2,1)}, f32[3,256,1024]{2,1,0:T(8,128)}, bf16[3,4,256,256]{3,2,1,0:T(8,128)(2,1)}, bf16[4,8,2368,128]{3,2,1,0:T(8,128)(2,1)}, f32[8,1024]{1,0:T(8,128)}) custom-call(bf16[3,256,1024]{2,1,0:T(8,128)(2,1)} %tok.5, bf16[3,256,1024]{2,1,0:T(8,128)(2,1)} %cot.1, bf16[3,4,256,256]{3,2,1,0:T(8,128)(2,1)} %get-tuple-element.32.o_rows, ...), custom_call_target="tpu_custom_call" | custom-call | flops 49999998976 | bytes 60000000 | tf_op jit(solution)/shard_map/mlp/pallas_call | solution.py:938
  295.7 184.2 %attend_back.1 = (bf16[3,4,256,768]{3,2,1,0:T(8,128)(2,1)}, bf16[4,2368,128]{2,1,0:T(8,128)(2,1)}) custom-call(s32[3]{0:T(128)} %bitcast.24, bf16[3,4,256,256]{3,2,1,0:T(8,128)(2,1)} %get-tuple-element.37.do_rows, bf16[3,3,1024,256]{3,2,1,0:T(8,128)(2,1)} %get-tuple-element.38.qkv, bf16[3,1024,256]{2,1,0:T(8,128)(2,1)} %get-tuple-element.39.o_head, ...), custom_call_target="tpu_custom_call" | custom-call | flops 30000001024 | bytes 20000000 | tf_op jit(solution)/shard_map/attend_back/pallas_call | solution.py:1082
  479.9 117.5 %sum_grads.1 = (f32[3,256,1024]{2,1,0:T(8,128)}, f32[3,256,1024]{2,1,0:T(8,128)}, f32[128,768]{1,0:T(8,128)}, f32[2368,128]{1,0:T(8,128)}, f32[8,1024]{1,0:T(8,128)}) custom-call(bf16[3,256,1024]{2,1,0:T(8,128)(2,1)} %tok.5, f32[3,256,1024]{2,1,0:T(8,128)} %get-tuple-element.36.mid, bf16[3,4,256,768]{3,2,1,0:T(8,128)(2,1)} %get-tuple-element.42.d_rows, ...), custom_call_target="tpu_custom_call" | custom-call | flops 10000000000 | bytes 50000000 | tf_op jit(solution)/shard_map/sum_grads/pallas_call | solution.py:1441
  597.5 0.0 copy-start.1
  597.5 2.3 slice_bitcast_fusion
  599.8 1.8 fusion
  601.6 0.9 slice_bitcast_fusion.3
  602.5 0.8 copy.27
  603.3 0.7 constant_dynamic-slice_fusion
  604.0 0.5 slice_bitcast_fusion.4
  604.5 0.0 copy-done.1
  604.5 0.0 copy-start
  604.5 1.7 copy.30
  606.2 1.4 copy-done
  607.6 1.7 copy.31
Async XLA Ops:
  597.5 7.1 %copy-start.1 = (f32[3,256,1024]{2,1,0:T(8,128)S(1)}, f32[3,256,1024]{2,1,0:T(8,128)}, u32[]{:S(2)}) copy-start(f32[3,256,1024]{2,1,0:T(8,128)} %get-tuple-element.85) | copy-start | bytes 9437188
  604.5 3.0 copy-start

commit v3 on v2

--- a/solution.py
+++ b/solution.py
@@ -558,16 +558,196 @@
     return jnp.where(allowed, s, -1e30)
 
 
+ORDER = (3, 0, 1, 2)
+
+
+def add_rows(dst, terms, step):
+    def rows(r, carry):
+        at = pl.ds(pl.multiple_of(r * step, step), step)
+        total = terms[0][at, :].astype(F32)
+        for term in terms[1:]:
+            total = total + term[at, :].astype(F32)
+        dst[at, :] = total.astype(dst.dtype)
+        return carry
+
+    lax.fori_loop(0, dst.shape[0] // step, rows, 0)
+
+
+def spans(n, step):
+    return [(at, min(step, n - at)) for at in range(0, n, step)]
+
+
+def block(i):
+    return pl.ds(pl.multiple_of(i * CHUNK, CHUNK), CHUNK)
+
+
+class Moves:
+    def __init__(self, sems):
+        self.sems, self.made = sems, []
+
+    def start(self, src, dst):
+        copy = pltpu.make_async_copy(src, dst, self.sems.at[len(self.made)])
+        copy.start()
+        self.made.append(copy)
+        return len(self.made) - 1
+
+    def wait(self, i):
+        self.made[i].wait()
+        self.made[i] = self.made[i], True
+
+    def rest(self):
+        for copy in self.made:
+            if not isinstance(copy, tuple):
+                copy.wait()
+
+
+class Crossing:
+    def __init__(self, place, part, bufs, sems, out, step):
+        self.p, self.part, self.out, self.step = place, part, out, step
+        self.acc, self.corner, self.bx, self.by = bufs
+        (self.s_core, self.r_core, self.s_corner, self.r_corner,
+         self.s_x, self.r_x, self.s_y, self.r_y) = sems
+
+    def core_copy(self, m, q):
+        p = self.p
+        return remote(
+            self.part(m, p.core_quads[q]), self.acc.at[m, q],
+            self.s_core.at[m, q], self.r_core.at[m, q], p.core,
+        )
+
+    def begin(self, m):
+        for q in (3, 1, 2, 0):
+            self.core_copy(m, q).start()
+
+    def corner_copy(self, m):
+        to = self.p.x if m % 2 == 0 else self.p.y
+        return remote(self.acc.at[m, 3], self.corner.at[m], self.s_corner.at[m], self.r_corner.at[m], to)
+
+    def x_copy(self, m):
+        return remote(self.acc.at[m, 1], self.bx.at[m], self.s_x.at[m], self.r_x.at[m], self.p.x)
+
+    def y_copy(self, m):
+        return remote(self.acc.at[m, 2], self.by.at[m], self.s_y.at[m], self.r_y.at[m], self.p.y)
+
+    def join(self, m):
+        first = 1 if m % 2 == 0 else 2
+        for q in (3, first, 3 - first, 0):
+            self.core_copy(m, q).wait_recv()
+            add_rows(self.acc.at[m, q], [self.acc.at[m, q], self.part(m, self.p.quads[q])], self.step)
+            if q == 3:
+                self.corner_copy(m).start()
+            if q == first:
+                (self.x_copy if m % 2 == 0 else self.y_copy)(m).start()
+
+    def relay(self, m):
+        q = 2 if m % 2 == 0 else 1
+        self.corner_copy(m).wait_recv()
+        add_rows(self.acc.at[m, q], [self.acc.at[m, q], self.corner.at[m]], self.step)
+        (self.y_copy if m % 2 == 0 else self.x_copy)(m).start()
+
+    def total(self, m):
+        self.x_copy(m).wait_recv()
+        self.y_copy(m).wait_recv()
+        add_rows(self.out.at[m], [self.acc.at[m, 0], self.bx.at[m], self.by.at[m]], self.step)
+
+    def core_sent(self, m):
+        for q in range(4):
+            self.core_copy(m, q).wait_send()
+
+    def finish(self):
+        for m in range(4):
+            self.corner_copy(m).wait_send()
+            self.x_copy(m).wait_send()
+            self.y_copy(m).wait_send()
+
+
+def crossing_scratch(rows, width):
+    def buf(*lead):
+        return pltpu.VMEM((*lead, rows, width), BF)
+
+    dma = pltpu.SemaphoreType.DMA
+    return [buf(4, 4), buf(4), buf(4), buf(4), dma((4, 4)), dma((4, 4))] + [dma((4,))] * 6
+
+
+class Chain:
+    def __init__(self, place, part, bufs, sems, out, step):
+        self.p, self.part, self.out, self.step = place, part, out, step
+        self.br, self.bl = bufs
+        self.s_r, self.r_r, self.s_l, self.r_l = sems
+
+    def r_copy(self, m):
+        p = self.p
+        return remote(self.part.at[m], self.br.at[m], self.s_r.at[m], self.r_r.at[m], (p.d, p.z + 1))
+
+    def l_copy(self, m):
+        p = self.p
+        return remote(self.part.at[m], self.bl.at[m], self.s_l.at[m], self.r_l.at[m], (p.d, p.z - 1))
+
+    def level(self, k):
+        @pl.when(self.p.z == k)
+        def _():
+            for m in range(3, k, -1):
+                if k > 0:
+                    self.r_copy(m).wait_recv()
+                    add_rows(self.part.at[m], [self.part.at[m], self.br.at[m]], self.step)
+                self.r_copy(m).start()
+
+        @pl.when(self.p.z == 3 - k)
+        def _():
+            for m in range(0, 3 - k):
+                if k > 0:
+                    self.l_copy(m).wait_recv()
+                    add_rows(self.part.at[m], [self.part.at[m], self.bl.at[m]], self.step)
+                self.l_copy(m).start()
+
+    def last(self):
+        for m in range(4):
+
+            @pl.when(self.p.z == m)
+            def _():
+                terms = [self.part.at[m]]
+                if m > 0:
+                    self.r_copy(m).wait_recv()
+                    terms.append(self.br.at[m])
+                if m < 3:
+                    self.l_copy(m).wait_recv()
+                    terms.append(self.bl.at[m])
+                add_rows(self.out, terms, self.step)
+
+    def finish(self):
+        for m in range(4):
+            if m > 0:
+
+                @pl.when(self.p.z < m)
+                def _():
+                    self.r_copy(m).wait_send()
+
+            if m < 3:
+
+                @pl.when(self.p.z > m)
+                def _():
+                    self.l_copy(m).wait_send()
+
+
+def chain_scratch(rows, width):
+    dma = pltpu.SemaphoreType.DMA
+    return [pltpu.VMEM((4, rows, width), BF)] * 2 + [dma((4,))] * 4
+
+
 def forward_kernel(
-    seq, tok, fv, wq, wk, wv, wo, wg_t, wu_t, wd_t, gain_attn, gain_mlp, cos_t, sin_t,
-    f1, f2, qkv, o_head, lse, o_rows, a1_t, gain_out,
-    a1, stage, p2, *sems,
+    seq, wq, wk, wv, wo_own, wg_t, wu_t, wd_t, gain_attn, gain_mlp, cos_t, sin_t, tok_in, fv_in, cot_in,
+    f2, acts, f1_out, qkv_out, o_out, lse_out, rows_out, a1t_out, a2_out, dattn_out, mid_out, layer_out, do_out, do_last, gain_part,
+    tok, fv, cot, f1, qkv, o_head, lse, o_rows, a1_t, a1, stage, p2, w, wo, a2, mid, y_out, acc, back, act, dattn, do_rows, do_head, *sems,
 ):
     p = Place()
     sems = list(sems)
     g1s, g2s = sems[:6], sems[6:12]
-    s_qkv, r_qkv, s_o, r_o, s_local = sems[12:]
+    s_qkv, r_qkv, s_o, r_o, s_local, s_do, r_do, w_sems, wo_sems, act_sems, move_sems = sems[12:]
+    moves = Moves(move_sems)
     z, d = p.z, p.d
+    got_tok = moves.start(tok_in, tok)
+    got_fv = moves.start(fv_in, fv)
+    got_cot = moves.start(cot_in, cot)
     p.greet()
 
     f1[z, d, 0:128] = wq[...]
@@ -581,7 +761,7 @@
     g1.spread(z)
     for i, source in enumerate((wg_t, wu_t, wd_t)):
         p2[i * FFC : (i + 1) * FFC, :] = source[...]
-    p2[3 * FFC :, :] = wo[...].T
+    p2[3 * FFC :, :] = wo_own[...].T
     own_copy = pltpu.make_async_copy(p2, f2.at[z, d], s_local)
     own_copy.start()
 
@@ -609,8 +789,8 @@
     g1.core_in(z)
 
     gain_row = jnp.concatenate([f1[z, e, 384:400, :].astype(F32)[0:8] for e in range(8)], axis=1)
-    for e in range(8):
-        gain_out[:, e * 128 : (e + 1) * 128] = gain_row[:, e * 256 + 128 : e * 256 + 256]
+    gain_two = jnp.concatenate([gain_row[0:1, e * 256 + 128 : e * 256 + 256] for e in range(8)], axis=1)
+    moves.wait(got_tok)
 
     def norm_body(b, carry):
         x = tok[b].astype(F32)
@@ -631,6 +811,8 @@
     p.hop(2, g1.core_in)
     p.hop(3, g1.core_in)
     g2.spread(z, p2)
+    moves.start(f1, f1_out)
+    moves.wait(got_fv)
 
     def project(b):
         pos_full = pl.ds(pl.multiple_of(z * CHUNK, CHUNK), CHUNK)
@@ -652,7 +834,7 @@
 
         lax.fori_loop(0, 4, one, 0)
         for i in range(3):
-            qkv[b, i, pl.ds(pl.multiple_of(z * CHUNK, CHUNK), CHUNK), :] = stage[b, z, i]
+            qkv[b, i, block(z), :] = stage[b, z, i]
 
     def qkv_copy(b, step):
         m = p.peer(step)
@@ -713,51 +895,173 @@
         def _():
             o_copy(b, i).start()
 
+    def take_o(b):
+        for step in (1, 2, 3):
+            m = p.peer(step)
+            remote(o_rows.at[b, m], o_rows.at[b, m], s_o.at[b, 0], r_o.at[b, m], (d, m)).wait_recv()
+
+    def w_copy(t, e):
+        m, slot = lax.rem(t, 4), lax.rem(t, 2)
+        return pltpu.make_async_copy(
+            f2.at[m, e, 0 : 3 * FFC, :], w.at[slot, :, e * 128 : (e + 1) * 128], w_sems.at[slot, e]
+        )
+
+    def wo_copy(m, e):
+        return pltpu.make_async_copy(
+            f2.at[m, e, 3 * FFC :, :], wo.at[m, :, e * 128 : (e + 1) * 128], wo_sems.at[m, e]
+        )
+
+    def act_copy(b, m, slot):
+        return pltpu.make_async_copy(
+            act.at[slot], acts.at[:, m, b * CHUNK : (b + 1) * CHUNK, :], act_sems.at[slot]
+        )
+
+    def load_mlp():
+        for m in range(4):
+            for e in range(8):
+                wo_copy(m, e).start()
+        for e in range(8):
+            w_copy(0, e).start()
+        for m in range(4):
+            for e in range(8):
+                wo_copy(m, e).wait()
+
+    def do_copy(b, step):
+        m = p.peer(step)
+        return remote(
+            do_rows.at[b, m], do_head.at[b, block(z), :], s_do.at[b, step - 1], r_do.at[b, z], (d, m)
+        )
+
+    def mlp_rows(b):
+        rows = slice(b * CHUNK, (b + 1) * CHUNK)
+        x2 = tok[b].astype(F32)
+        for m in range(4):
+            x2 = x2 + dot(o_rows[b, m], wo[m])
+        factor = lax.rsqrt(jnp.mean(x2 * x2, axis=1, keepdims=True) + EPSILON)
+        mid[b] = x2
+        a2[rows, :] = (x2 * factor * gain_two).astype(BF)
+
+        def chunk(m, carry):
+            t = b * 4 + m
+            slot = lax.rem(m, 2)
+            for e in range(8):
+                w_copy(t, e).wait()
+
+            @pl.when(t < 11)
+            def _():
+                for e in range(8):
+                    w_copy(t + 1, e).start()
+
+            @pl.when(t >= 2)
+            def _():
+                act_copy(b, m, slot).wait()
+
+            for at, size in spans(FFC, 256):
+                cols = slice(at, at + size)
+                gate = dot_nt(a2[rows, :], w[slot, at : at + size, :])
+                up = dot_nt(a2[rows, :], w[slot, FFC + at : FFC + at + size, :])
+                dh = dot_nt(cot[b], w[slot, 2 * FFC + at : 2 * FFC + at + size, :])
+                sg = jax.nn.sigmoid(gate)
+                silu = gate * sg
+                act[slot, 0, :, cols] = (dh * up * (sg + silu * (1.0 - sg))).astype(BF)
+                act[slot, 1, :, cols] = (dh * silu).astype(BF)
+                act[slot, 2, :, cols] = (silu * up).astype(BF)
+            for at, size in spans(1024, 256):
+                cols = slice(at, at + size)
+                y = dot(act[slot, 2], w[slot, 2 * FFC : 3 * FFC, cols])
+                u = dot(act[slot, 0], w[slot, 0:FFC, cols]) + dot(act[slot, 1], w[slot, FFC : 2 * FFC, cols])
+                acc[:, cols] = jnp.where(m == 0, y, acc[:, cols] + y)
+                back[:, cols] = jnp.where(m == 0, u, back[:, cols] + u)
+            act_copy(b, m, slot).start()
+            return carry
+
+        lax.fori_loop(0, 4, chunk, 0)
+        x2 = mid[b]
+        y_out[b] = (x2 + acc[...]).astype(BF)
+        factor = lax.rsqrt(jnp.mean(x2 * x2, axis=1, keepdims=True) + EPSILON)
+        n2 = x2 * factor
+        da2 = back[...]
+        sums = jnp.broadcast_to(jnp.sum(da2 * n2, axis=0, keepdims=True), (8, 1024))
+        gain_part[...] = sums if b == 0 else gain_part[...] + sums
+        dn2 = da2 * gain_two
+        grad_mid = cot[b].astype(F32) + factor * (dn2 - n2 * jnp.mean(dn2 * n2, axis=1, keepdims=True))
+        mid[b] = grad_mid
+        dattn[rows, :] = grad_mid.astype(BF)
+
+        def heads(m, carry):
+            do_rows[b, m] = dot_nt(dattn[rows, :], wo[m]).astype(BF)
+            return carry
+
+        lax.fori_loop(0, 4, heads, 0)
+        if b < 2:
+            for step in (1, 2, 3):
+                do_copy(b, step).start()
+            do_head[b, block(z), :] = do_rows[b, z]
+        moves.start(mid.at[b], mid_out.at[b])
+        moves.start(y_out.at[b], layer_out.at[b])
+
+    def attend_all(b):
+        for i in range(4):
+            attend(b, i)
+        moves.start(o_head.at[b], o_out.at[b])
+        moves.start(lse.at[b], lse_out.at[b])
+
     for b in range(3):
         project(b)
         if b == 0:
             send_qkv(0)
     a1_t[...] = a1[...].T
-    p.hop(1, g2.z_in)
+    moves.start(a1_t, a1t_out)
+    p.hop(1, arrive(g2))
+    p.hop(2, arrive(g2))
+    side(g2)(z)
     sent_qkv(0)
     send_qkv(1)
-    p.hop(2, g2.z_in)
-    p.hop(3, g2.z_in)
-    p.hop(1, g2.spread)
-    side(g2)(z)
-    p.hop(2, g2.spread)
+    p.hop(3, arrive(g2))
+    p.hop(1, side(g2))
+    g2.diag_in(z)
     take_qkv(0)
-    attend(0, 0)
-    attend(0, 1)
-    p.hop(1, side(g2))
+    moves.start(qkv.at[0], qkv_out.at[0])
+    attend_all(0)
+    p.hop(2, side(g2))
+    p.hop(1, g2.diag_in)
     sent_qkv(1)
     send_qkv(2)
-    attend(0, 2)
-    attend(0, 3)
-    p.hop(3, g2.spread)
-    p.hop(2, side(g2))
     take_qkv(1)
-    attend(1, 0)
-    attend(1, 1)
-    g2.diag_in(z)
-    p.hop(1, g2.diag_in)
-    attend(1, 2)
-    attend(1, 3)
+    moves.start(qkv.at[1], qkv_out.at[1])
+    attend_all(1)
     p.hop(3, side(g2))
     p.hop(2, g2.diag_in)
-    take_qkv(2)
-    attend(2, 0)
-    attend(2, 1)
     p.hop(3, g2.diag_in)
-    attend(2, 2)
-    attend(2, 3)
-    sent_qkv(2)
     for m in range(4):
         g2.core_in(m)
-    for b in range(3):
+    own_copy.wait()
+    load_mlp()
+    moves.wait(got_cot)
+    take_o(0)
+    mlp_rows(0)
+    take_qkv(2)
+    moves.start(qkv.at[2], qkv_out.at[2])
+    attend_all(2)
+    take_o(1)
+    mlp_rows(1)
+    take_o(2)
+    moves.start(o_rows, rows_out)
+    mlp_rows(2)
+    moves.start(a2, a2_out)
+    moves.start(dattn, dattn_out)
+    moves.start(do_rows.at[2], do_last)
+    for b in range(2):
         for step in (1, 2, 3):
             m = p.peer(step)
-            remote(o_rows.at[b, m], o_rows.at[b, m], s_o.at[b, 0], r_o.at[b, m], (d, m)).wait_recv()
+            dst = do_head.at[b, block(m), :]
+            remote(do_rows.at[b, m], dst, s_do.at[b, 0], r_do.at[b, m], (d, m)).wait_recv()
+            do_copy(b, step).wait_send()
+        moves.start(do_head.at[b], do_out.at[b])
+    act_copy(2, 2, 0).wait()
+    act_copy(2, 3, 1).wait()
+    sent_qkv(2)
+    for b in range(3):
         for i in range(4):
 
             @pl.when(z != i)
@@ -766,7 +1070,7 @@
 
     g1.finish()
     g2.finish()
-    own_copy.wait()
+    moves.rest()
 
 
 def run_forward(*args):
@@ -777,227 +1081,109 @@
     return pl.pallas_call(
         forward_kernel,
         out_shape=(
+            shape((4, 8, PIECE, 128), BF),
+            shape((3, 4, 768, FFC), BF),
             shape((4, 8, QROWS, CHUNK), BF),
-            shape((4, 8, PIECE, 128), BF),
             shape((3, 3, 1024, CHUNK), BF),
             shape((3, 1024, CHUNK), BF),
             shape((3, 1024, 128), F32),
             shape((3, 4, CHUNK, CHUNK), BF),
             shape((1024, 768), BF),
+            shape((768, 1024), BF),
+            shape((768, 1024), BF),
+            shape((3, CHUNK, 1024), F32),
+            shape((3, CHUNK, 1024), BF),
+            shape((2, 1024, CHUNK), BF),
+            shape((4, CHUNK, CHUNK), BF),
             shape((8, 1024), F32),
         ),
-        in_specs=[pl.BlockSpec(memory_space=pltpu.SMEM)] + [vmem] * (len(args) - 1),
-        out_specs=(vmem, hbm, vmem, vmem, vmem, vmem, vmem, vmem),
+        in_specs=[pl.BlockSpec(memory_space=pltpu.SMEM)] + [vmem] * 11 + [hbm] * 3,
+        out_specs=(hbm,) * 14 + (vmem,),
         scratch_shapes=[
+            pltpu.VMEM((3, CHUNK, 1024), BF),
+            pltpu.VMEM((3, CHUNK, 1024), BF),
+            pltpu.VMEM((3, CHUNK, 1024), BF),
+            pltpu.VMEM((4, 8, QROWS, CHUNK), BF),
+            pltpu.VMEM((3, 3, 1024, CHUNK), BF),
+            pltpu.VMEM((3, 1024, CHUNK), BF),
+            pltpu.VMEM((3, 1024, 128), F32),
+            pltpu.VMEM((3, 4, CHUNK, CHUNK), BF),
+            pltpu.VMEM((1024, 768), BF),
             pltpu.VMEM((768, 1024), BF),
             pltpu.VMEM((3, 4, 3, CHUNK, CHUNK), BF),
             pltpu.VMEM((PIECE, 128), BF),
+            pltpu.VMEM((2, 3 * FFC, 1024), BF),
+            pltpu.VMEM((4, CHUNK, 1024), BF),
+            pltpu.VMEM((768, 1024), BF),
+            pltpu.VMEM((3, CHUNK, 1024), F32),
+            pltpu.VMEM((3, CHUNK, 1024), BF),
+            pltpu.VMEM((CHUNK, 1024), F32),
+            pltpu.VMEM((CHUNK, 1024), F32),
+            pltpu.VMEM((2, 3, CHUNK, FFC), BF),
+            pltpu.VMEM((768, 1024), BF),
+            pltpu.VMEM((3, 4, CHUNK, CHUNK), BF),
+            pltpu.VMEM((2, 1024, CHUNK), BF),
         ]
         + gather_sems()
         + gather_sems()
-        + [dma((3, 3)), dma((3, 4)), dma((3, 4)), dma((3, 4)), dma],
+        + [dma((3, 3)), dma((3, 4)), dma((3, 4)), dma((3, 4)), dma, dma((3, 3)), dma((3, 4))]
+        + [dma((2, 8)), dma((4, 8)), dma((2,)), dma((32,))],
         compiler_params=pltpu.CompilerParams(
-            collective_id=1, has_side_effects=True, vmem_limit_bytes=60 * 2**20
+            collective_id=1, has_side_effects=True, vmem_limit_bytes=62 * 2**20
         ),
-        cost_estimate=pl.CostEstimate(flops=2 * 10**10, bytes_accessed=6 * 10**7, transcendentals=8 * 10**6),
-        name="gather_attend",
+        cost_estimate=pl.CostEstimate(flops=5 * 10**10, bytes_accessed=6 * 10**7, transcendentals=8 * 10**6),
+        name="gather_forward",
     )(*args)
 
 
-def spans(n, step):
-    return [(at, min(step, n - at)) for at in range(0, n, step)]
-
-
-def mlp_kernel(
-    tok, cot, o_rows, f2, gain,
-    layer_out, dx2, do_rows, part, gain_part,
-    w, wo, a2, hid, dga, dup, acc, back, stage, wo_stage, in_sems, wo_sems, out_sems, wo_out,
-):
-    def w_copy(m, slot, d):
-        return pltpu.make_async_copy(
-            f2.at[m, d, 0 : 3 * FFC, :], w.at[slot, :, d * 128 : (d + 1) * 128], in_sems.at[slot, d]
-        )
-
-    def wo_copy(m, d):
-        return pltpu.make_async_copy(
-            f2.at[m, d, 3 * FFC :, :], wo.at[m, :, d * 128 : (d + 1) * 128], wo_sems.at[m, d]
-        )
-
-    def out_copy(m, slot):
-        return pltpu.make_async_copy(stage.at[slot], part.at[m, :, 0 : 3 * FFC, :], out_sems.at[slot])
-
-    def wo_out_copy(m):
-        return pltpu.make_async_copy(wo_stage.at[m], part.at[m, :, 3 * FFC :, :], wo_out.at[m])
-
-    for m in range(4):
-        for d in range(8):
-            wo_copy(m, d).start()
-    for d in range(8):
-        w_copy(0, 0, d).start()
-    for m in range(4):
-        for d in range(8):
-            wo_copy(m, d).wait()
-
-    def row_block(b):
-        return pl.ds(pl.multiple_of(b * CHUNK, CHUNK), CHUNK)
-
-    def enter(b, carry):
-        x2 = tok[b].astype(F32)
-        for m in range(4):
-            x2 = x2 + dot(o_rows[b, m], wo[m])
-        dx2[b] = x2
-        factor = lax.rsqrt(jnp.mean(x2 * x2, axis=1, keepdims=True) + EPSILON)
-        a2[row_block(b), :] = (x2 * factor * gain[0:1, :]).astype(BF)
-        return carry
-
-    lax.fori_loop(0, 3, enter, 0)
-    grad = cot[...].reshape(768, 1024)
-
-    def chunk(m, carry):
-        slot = lax.rem(m, 2)
-        for d in range(8):
-            w_copy(m, slot, d).wait()
-
-        @pl.when(m < 3)
-        def _():
-            for d in range(8):
-                w_copy(m + 1, 1 - slot, d).start()
-
-        @pl.when(m >= 2)
-        def _():
-            out_copy(m - 2, slot).wait()
-
-        for at, size in spans(FFC, 256):
-            cols = slice(at, at + size)
-            gate = dot_nt(a2[...], w[slot, at : at + size, :])
-            up = dot_nt(a2[...], w[slot, FFC + at : FFC + at + size, :])
-            dh = dot_nt(grad, w[slot, 2 * FFC + at : 2 * FFC + at + size, :])
-            sg = jax.nn.sigmoid(gate)
-            act = gate * sg
-            hid[:, cols] = (act * up).astype(BF)
-            dga[:, cols] = (dh * up * (sg + act * (1.0 - sg))).astype(BF)
-            dup[:, cols] = (dh * act).astype(BF)
-            for i, (left, right) in enumerate(((dga, a2[...]), (dup, a2[...]), (hid, grad))):
-                out = dot_tn(left[:, cols], right).astype(BF)
-                for d in range(8):
-                    stage[slot, d, i * FFC + at : i * FFC + at + size, :] = out[:, d * 128 : (d + 1) * 128]
-
-        for at, size in spans(1024, 256):
-            cols = slice(at, at + size)
-            y = dot(hid[...], w[slot, 2 * FFC : 3 * FFC, cols])
-            u = dot(dga[...], w[slot, 0:FFC, cols]) + dot(dup[...], w[slot, FFC : 2 * FFC, cols])
-            acc[:, cols] = jnp.where(m == 0, y, acc[:, cols] + y)
-            back[:, cols] = jnp.where(m == 0, u, back[:, cols] + u)
-
-        out_copy(m, slot).start()
-        return carry
-
-    lax.fori_loop(0, 4, chunk, 0)
-
-    def leave(b, total):
-        x2 = dx2[b]
-        rows = row_block(b)
-        layer_out[b] = (x2 + acc[rows, :]).astype(BF)
-        factor = lax.rsqrt(jnp.mean(x2 * x2, axis=1, keepdims=True) + EPSILON)
-        n2 = x2 * factor
-        da2 = back[rows, :]
-        total = total + jnp.sum(da2 * n2, axis=0, keepdims=True)
-        dn2 = da2 * gain[0:1, :]
-        grad_mid = cot[b].astype(F32) + factor * (
-            dn2 - n2 * jnp.mean(dn2 * n2, axis=1, keepdims=True)
-        )
-        dx2[b] = grad_mid
-        a2[rows, :] = grad_mid.astype(BF)
-        return total
-
-    total = lax.fori_loop(0, 3, leave, jnp.zeros((1, 1024), F32))
-    gain_part[...] = jnp.broadcast_to(total, (8, 1024))
-
-    def heads(m, carry):
-        own = jnp.concatenate([o_rows[b, m] for b in range(3)], axis=0)
-        dw = dot_tn(own, a2[...]).astype(BF)
-        for d in range(8):
-            wo_stage[m, d] = dw[:, d * 128 : (d + 1) * 128]
-        wo_out_copy(m).start()
-        for b in range(3):
-            do_rows[b, m] = dot_nt(a2[b * CHUNK : (b + 1) * CHUNK, :], wo[m]).astype(BF)
-        return carry
-
-    lax.fori_loop(0, 4, heads, 0)
-    out_copy(2, 0).wait()
-    out_copy(3, 1).wait()
-    for m in range(4):
-        wo_out_copy(m).wait()
-
-
-def run_mlp(tok, cot, o_rows, f2, gain):
-    vmem = pl.BlockSpec(memory_space=pltpu.VMEM)
-    hbm = pl.BlockSpec(memory_space=pl.ANY)
-    shape = jax.ShapeDtypeStruct
-    dma = pltpu.SemaphoreType.DMA
-    return pl.pallas_call(
-        mlp_kernel,
-        out_shape=(
-            shape((3, CHUNK, 1024), BF),
-            shape((3, CHUNK, 1024), F32),
-            shape((3, 4, CHUNK, CHUNK), BF),
-            shape((4, 8, PIECE, 128), BF),
-            shape((8, 1024), F32),
-        ),
-        in_specs=[vmem, vmem, vmem, hbm, vmem],
-        out_specs=(vmem, vmem, vmem, hbm, vmem),
-        scratch_shapes=[
-            pltpu.VMEM((2, 3 * FFC, 1024), BF),
-            pltpu.VMEM((4, CHUNK, 1024), BF),
-            pltpu.VMEM((768, 1024), BF),
-            pltpu.VMEM((768, FFC), BF),
-            pltpu.VMEM((768, FFC), BF),
-            pltpu.VMEM((768, FFC), BF),
-            pltpu.VMEM((768, 1024), F32),
-            pltpu.VMEM((768, 1024), F32),
-            pltpu.VMEM((2, 8, 3 * FFC, 128), BF),
-            pltpu.VMEM((4, 8, CHUNK, 128), BF),
-            dma((2, 8)),
-            dma((4, 8)),
-            dma((2,)),
-            dma((4,)),
-        ],
-        compiler_params=pltpu.CompilerParams(vmem_limit_bytes=60 * 2**20),
-        cost_estimate=pl.CostEstimate(flops=5 * 10**10, bytes_accessed=6 * 10**7, transcendentals=2 * 10**6),
-        name="mlp",
-    )(tok, cot, o_rows, f2, gain)
-
-
 def backward_kernel(
-    seq, do_rows, qkv, o_head, lse, cos_t, sin_t, part,
+    seq, cos_t, sin_t, do_last, do_in, qkv_in, o_in, lse_in, rows_in, a2_in, dattn_in, cot_in, acts,
     d_rows, summed,
-    do_head, dk, dv, stage, *rest,
+    do_mine, do_head, qkv, o_head, lse, o_rows, a2, dattn, cot, act, part, total, dk, dv, stage, *rest,
 ):
     p = Place()
-    s_do, r_do, s_d, r_d = rest[:4]
+    s_do, r_do, s_d, r_d, act_sems, move_sems = rest[:6]
     z, d = p.z, p.d
+    moves = Moves(move_sems)
+    got = []
+    for b in range(3):
+        got.append(
+            [moves.start(qkv_in.at[b], qkv.at[b]), moves.start(o_in.at[b], o_head.at[b]), moves.start(lse_in.at[b], lse.at[b])]
+            + ([moves.start(do_in.at[b], do_head.at[b])] if b < 2 else [])
+        )
+        if b == 0:
+            got_do = moves.start(do_last, do_mine)
+            got_w = [
+                moves.start(a2_in, a2), moves.start(dattn_in, dattn), moves.start(cot_in, cot),
+                moves.start(rows_in, o_rows),
+            ]
     p.greet()
-    mine = pl.ds(pl.multiple_of(z * CHUNK, CHUNK), CHUNK)
-
-    def do_copy(b, step):
+
+    def act_copy(m, slot):
+        return pltpu.make_async_copy(acts.at[:, m], act.at[slot], act_sems.at[slot])
+
+    act_copy(ORDER[0], 0).start()
+    moves.wait(got_do)
+
+    def do_copy(step):
         m = p.peer(step)
-        return remote(
-            do_rows.at[b, m], do_head.at[b, mine, :], s_do.at[b, step - 1], r_do.at[b, z], (d, m)
-        )
-
-    def send_do(b):
-        for step in (1, 2, 3):
-            do_copy(b, step).start()
-        do_head[b, mine, :] = do_rows[b, z]
-
-    def take_do(b):
+        return remote(do_mine.at[m], do_head.at[2, block(z), :], s_do.at[step - 1], r_do.at[z], (d, m))
+
+    for step in (1, 2, 3):
+        do_copy(step).start()
+    do_head[2, block(z), :] = do_mine[z]
+
+    def take_do():
         for step in (1, 2, 3):
             m = p.peer(step)
-            dst = do_head.at[b, pl.ds(pl.multiple_of(m * CHUNK, CHUNK), CHUNK), :]
-            remote(do_rows.at[b, m], dst, s_do.at[b, 0], r_do.at[b, m], (d, m)).wait_recv()
+            dst = do_head.at[2, block(m), :]
+            remote(do_mine.at[m], dst, s_do.at[0], r_do.at[m], (d, m)).wait_recv()
 
     def d_copy(b, i):
         return remote(stage.at[b, i], d_rows.at[b, z], s_d.at[b, i], r_d.at[b, z], (d, i))
+
+    def own_copy(b, i):
+        return pltpu.make_async_copy(stage.at[b, i], d_rows.at[b, i], s_d.at[b, i])
 
     def back(b, i):
         n = (i + 1) * CHUNK
@@ -1040,38 +1226,86 @@
 
         @pl.when(z == i)
         def _():
-            d_rows[b, z] = stage[b, i]
+            own_copy(b, i).start()
 
         @pl.when(z != i)
         def _():
             d_copy(b, i).start()
 
-    crossing = Crossing(p, lambda m, e: part.at[m, e], rest[4:9], rest[9:], summed, 592)
-    for b in range(3):
-        send_do(b)
-    plan = crossing.steps()
-    for b in range(3):
-        take_do(b)
+    def back_all(b):
+        for i in got[b]:
+            moves.wait(i)
         dk[...] = jnp.zeros_like(dk)
         dv[...] = jnp.zeros_like(dv)
         for i in (3, 2, 1, 0):
             back(b, i)
-            for step in plan[:2]:
-                step()
-            plan = plan[2:]
-    for step in plan:
-        step()
+
+    crossing = Crossing(p, lambda m, e: part.at[ORDER.index(m) % 2, e], rest[6:10], rest[10:], total, 592)
+
+    def weight_grad(k):
+        m, slot = ORDER[k], k % 2
+        act_copy(m, slot).wait()
+        if k < 3:
+            act_copy(ORDER[k + 1], 1 - slot).start()
+        if k >= 2:
+            crossing.core_sent(ORDER[k - 2])
+
+        for i in range(3):
+            right = cot[...].reshape(768, 1024) if i == 2 else a2[...]
+            for at, size in spans(FFC, 256):
+                out = dot_tn(act[slot, i, :, at : at + size], right).astype(BF)
+                for e in range(8):
+                    part[slot, e, i * FFC + at : i * FFC + at + size, :] = out[:, e * 128 : (e + 1) * 128]
+        own = jnp.concatenate([o_rows[b, m] for b in range(3)], axis=0)
+        out = dot_tn(own, dattn[...]).astype(BF)
+        for e in range(8):
+            part[slot, e, 3 * FFC :, :] = out[:, e * 128 : (e + 1) * 128]
+        crossing.begin(m)
+
+    a, b_, c, e_ = ORDER
+    back_all(0)
+    for i in got_w:
+        moves.wait(i)
+    weight_grad(0)
+    weight_grad(1)
+    crossing.join(a)
+    crossing.join(b_)
+    back_all(1)
+    weight_grad(2)
+    weight_grad(3)
+    crossing.relay(a)
+    crossing.relay(b_)
+    take_do()
+    back_all(2)
+    crossing.join(c)
+    crossing.join(e_)
+    crossing.total(a)
+    crossing.total(b_)
+    crossing.relay(c)
+    crossing.relay(e_)
+    crossing.total(c)
+    crossing.total(e_)
+    moves.start(total, summed)
+    crossing.core_sent(c)
+    crossing.core_sent(e_)
     crossing.finish()
+    for step in (1, 2, 3):
+        do_copy(step).wait_send()
     for b in range(3):
         for step in (1, 2, 3):
-            do_copy(b, step).wait_send()
             m = p.peer(step)
-            remote(d_rows.at[b, m], d_rows.at[b, m], s_d.at[b, 0], r_d.at[b, m], (d, m)).wait_recv()
+            remote(stage.at[b, m], d_rows.at[b, m], s_d.at[b, 0], r_d.at[b, m], (d, m)).wait_recv()
         for i in range(4):
+
+            @pl.when(z == i)
+            def _():
+                own_copy(b, i).wait()
 
             @pl.when(z != i)
             def _():
                 d_copy(b, i).wait_send()
+
+    moves.rest()
 
 
 def run_backward(*args):
@@ -1082,244 +1316,57 @@
     return pl.pallas_call(
         backward_kernel,
         out_shape=(shape((3, 4, CHUNK, 768), BF), shape((4, PIECE, 128), BF)),
-        in_specs=[pl.BlockSpec(memory_space=pltpu.SMEM)] + [vmem] * 6 + [hbm],
-        out_specs=(vmem, vmem),
+        in_specs=[pl.BlockSpec(memory_space=pltpu.SMEM)] + [vmem] * 2 + [hbm] * (len(args) - 3),
+        out_specs=(hbm, hbm),
         scratch_shapes=[
+            pltpu.VMEM((4, CHUNK, CHUNK), BF),
             pltpu.VMEM((3, 1024, CHUNK), BF),
+            pltpu.VMEM((3, 3, 1024, CHUNK), BF),
+            pltpu.VMEM((3, 1024, CHUNK), BF),
+            pltpu.VMEM((3, 1024, 128), F32),
+            pltpu.VMEM((3, 4, CHUNK, CHUNK), BF),
+            pltpu.VMEM((768, 1024), BF),
+            pltpu.VMEM((768, 1024), BF),
+            pltpu.VMEM((3, CHUNK, 1024), BF),
+            pltpu.VMEM((2, 3, 768, FFC), BF),
+            pltpu.VMEM((2, 8, PIECE, 128), BF),
+            pltpu.VMEM((4, PIECE, 128), BF),
             pltpu.VMEM((1024, CHUNK), F32),
             pltpu.VMEM((1024, CHUNK), F32),
             pltpu.VMEM((3, 4, CHUNK, 768), BF),
-            dma((3, 3)),
+            dma((3,)),
+            dma((4,)),
             dma((3, 4)),
             dma((3, 4)),
-            dma((3, 4)),
+            dma((2,)),
+            dma((32,)),
         ]
         + crossing_scratch(PIECE, 128),
         compiler_params=pltpu.CompilerParams(
-            collective_id=2, has_side_effects=True, vmem_limit_bytes=60 * 2**20
+            collective_id=2, has_side_effects=True, vmem_limit_bytes=63 * 2**20
         ),
-        cost_estimate=pl.CostEstimate(flops=3 * 10**10, bytes_accessed=2 * 10**7, transcendentals=8 * 10**6),
+        cost_estimate=pl.CostEstimate(flops=4 * 10**10, bytes_accessed=4 * 10**7, transcendentals=8 * 10**6),
         name="attend_back",
     )(*args)
 
 
-ORDER = (3, 0, 1, 2)
-
-
-def add_rows(dst, terms, step):
-    def rows(r, carry):
-        at = pl.ds(pl.multiple_of(r * step, step), step)
-        total = terms[0][at, :].astype(F32)
-        for term in terms[1:]:
-            total = total + term[at, :].astype(F32)
-        dst[at, :] = total.astype(dst.dtype)
-        return carry
-
-    lax.fori_loop(0, dst.shape[0] // step, rows, 0)
-
-
-class Crossing:
-    def __init__(self, place, part, bufs, sems, out, step):
-        self.p, self.part, self.out, self.step = place, part, out, step
-        self.own, self.acc, self.corner, self.bx, self.by = bufs
-        (self.l_own, self.s_core, self.r_core, self.s_corner, self.r_corner,
-         self.s_x, self.r_x, self.s_y, self.r_y) = sems
-
-    def core_copy(self, m, q):
-        p = self.p
-        return remote(
-            self.part(m, p.core_quads[q]), self.acc.at[m, q],
-            self.s_core.at[m, q], self.r_core.at[m, q], p.core,
-        )
-
-    def own_copy(self, m, q):
-        slot = ORDER.index(m) % 2
-        return pltpu.make_async_copy(
-            self.part(m, self.p.quads[q]), self.own.at[slot, q], self.l_own.at[slot, q]
-        )
-
-    def begin(self, m):
-        for q in (3, 1, 2, 0):
-            self.core_copy(m, q).start()
-
-    def load(self, m):
-        for q in (3, 1, 2, 0):
-            self.own_copy(m, q).start()
-
-    def corner_copy(self, m):
-        to = self.p.x if m % 2 == 0 else self.p.y
-        return remote(self.acc.at[m, 3], self.corner.at[m], self.s_corner.at[m], self.r_corner.at[m], to)
-
-    def x_copy(self, m):
-        return remote(self.acc.at[m, 1], self.bx.at[m], self.s_x.at[m], self.r_x.at[m], self.p.x)
-
-    def y_copy(self, m):
-        return remote(self.acc.at[m, 2], self.by.at[m], self.s_y.at[m], self.r_y.at[m], self.p.y)
-
-    def join(self, m):
-        slot = ORDER.index(m) % 2
-        first = 1 if m % 2 == 0 else 2
-        for q in (3, first, 3 - first, 0):
-            self.own_copy(m, q).wait()
-            self.core_copy(m, q).wait_recv()
-            add_rows(self.acc.at[m, q], [self.acc.at[m, q], self.own.at[slot, q]], self.step)
-            if q == 3:
-                self.corner_copy(m).start()
-            if q == first:
-                (self.x_copy if m % 2 == 0 else self.y_copy)(m).start()
-
-    def relay(self, m):
-        q = 2 if m % 2 == 0 else 1
-        self.corner_copy(m).wait_recv()
-        add_rows(self.acc.at[m, q], [self.acc.at[m, q], self.corner.at[m]], self.step)
-        (self.y_copy if m % 2 == 0 else self.x_copy)(m).start()
-
-    def total(self, m):
-        self.x_copy(m).wait_recv()
-        self.y_copy(m).wait_recv()
-        add_rows(self.out.at[m], [self.acc.at[m, 0], self.bx.at[m], self.by.at[m]], self.step)
-
-    def finish(self):
-        for m in range(4):
-            for q in range(4):
-                self.core_copy(m, q).wait_send()
-            self.corner_copy(m).wait_send()
-            self.x_copy(m).wait_send()
-            self.y_copy(m).wait_send()
-
-    def steps(self):
-        a, b, c, e = ORDER
-
-        def start():
-            for m in ORDER:
-                self.begin(m)
-            self.load(a)
-            self.load(b)
-
-        def join_then_load(m, after):
-            self.join(m)
-            self.load(after)
-
-        return [
-            start,
-            lambda: join_then_load(a, c),
-            lambda: join_then_load(b, e),
-            lambda: self.relay(a),
-            lambda: self.relay(b),
-            lambda: self.join(c),
-            lambda: self.join(e),
-            lambda: self.total(a),
-            lambda: self.total(b),
-            lambda: self.relay(c),
-            lambda: self.relay(e),
-            lambda: self.total(c),
-            lambda: self.total(e),
-        ]
-
-
-def crossing_scratch(rows, width):
-    def buf(*lead):
-        return pltpu.VMEM((*lead, rows, width), BF)
-
-    dma = pltpu.SemaphoreType.DMA
-    return [buf(2, 4), buf(4, 4), buf(4), buf(4), buf(4), dma((2, 4)), dma((4, 4)), dma((4, 4))] + [dma((4,))] * 6
-
-
-class Chain:
-    def __init__(self, place, part, bufs, sems, out, step):
-        self.p, self.part, self.out, self.step = place, part, out, step
-        self.br, self.bl = bufs
-        self.s_r, self.r_r, self.s_l, self.r_l = sems
-
-    def r_copy(self, m):
-        p = self.p
-        return remote(self.part.at[m], self.br.at[m], self.s_r.at[m], self.r_r.at[m], (p.d, p.z + 1))
-
-    def l_copy(self, m):
-        p = self.p
-        return remote(self.part.at[m], self.bl.at[m], self.s_l.at[m], self.r_l.at[m], (p.d, p.z - 1))
-
-    def along(self, m):
-        z = self.p.z
-
-        if m > 0:
-
-            @pl.when(z < m)
-            def _():
-                @pl.when(z > 0)
-                def _():
-                    self.r_copy(m).wait_recv()
-                    add_rows(self.part.at[m], [self.part.at[m], self.br.at[m]], self.step)
-
-                self.r_copy(m).start()
-
-        if m < 3:
-
-            @pl.when(z > m)
-            def _():
-                @pl.when(z < 3)
-                def _():
-                    self.l_copy(m).wait_recv()
-                    add_rows(self.part.at[m], [self.part.at[m], self.bl.at[m]], self.step)
-
-                self.l_copy(m).start()
-
-    def last(self):
-        for m in range(4):
-
-            @pl.when(self.p.z == m)
-            def _():
-                terms = [self.part.at[m]]
-                if m > 0:
-                    self.r_copy(m).wait_recv()
-                    terms.append(self.br.at[m])
-                if m < 3:
-                    self.l_copy(m).wait_recv()
-                    terms.append(self.bl.at[m])
-                add_rows(self.out, terms, self.step)
-
-    def finish(self):
-        for m in range(4):
-            if m > 0:
-
-                @pl.when(self.p.z < m)
-                def _():
-                    self.r_copy(m).wait_send()
-
-            if m < 3:
-
-                @pl.when(self.p.z > m)
-                def _():
-                    self.l_copy(m).wait_send()
-
-
-def chain_scratch(rows, width):
-    dma = pltpu.SemaphoreType.DMA
-    return [pltpu.VMEM((4, rows, width), BF)] * 2 + [dma((4,))] * 4
-
-
 def finish_kernel(
-    tok, mid, d_rows, a1_t, f1, gain_part, summed,
+    gain_part, tok_in, mid_in, d_rows_in, a1t_in, f1_in, summed,
     grad_tokens, grad_first, dw1, dw2, gain_sum,
-    part, acc, total1, total2, gbuf, *rest,
+    tok, mid, d_rows, a1_t, f1, grad, first, part, acc, total1, total2, gbuf, *rest,
 ):
     p = Place()
+    rest = list(rest)
+    cross = Crossing(p, lambda m, e: part.at[m, e], rest[:4], rest[4:12], total1, 16)
+    chain1 = Chain(p, total1, rest[12:14], rest[14:18], dw1, 16)
+    chain2 = Chain(p, total2, rest[18:20], rest[20:24], dw2, 592)
+    s_gain, r_gain, move_sems = rest[24:27]
+    moves = Moves(move_sems)
+    got_total = moves.start(summed, total2)
+    got_d = [moves.start(d_rows_in, d_rows), moves.start(a1t_in, a1_t)]
+    got_f1 = moves.start(f1_in, f1)
+    got_x = [moves.start(tok_in, tok), moves.start(mid_in, mid)]
     p.greet()
-    rest = list(rest)
-    cross = Crossing(p, lambda m, e: part.at[m, e], rest[:5], rest[5:14], total1, 16)
-    chain1 = Chain(p, total1, rest[14:16], rest[16:20], dw1, 16)
-    chain2 = Chain(p, total2, rest[20:22], rest[22:26], dw2, 592)
-    s_gain, r_gain, l_total = rest[26:29]
-
-    def total_copy(m):
-        return pltpu.make_async_copy(summed.at[m], total2.at[m], l_total.at[m])
-
-    def along2(m):
-        total_copy(m).wait()
-        chain2.along(m)
-
-    for m in ORDER:
-        total_copy(m).start()
 
     def weight_grad(m):
         cols = jnp.concatenate([d_rows[b, m] for b in range(3)], axis=0)
@@ -1357,69 +1404,66 @@
         total = total + jnp.sum(da1 * n1, axis=0, keepdims=True)
         gain = jnp.concatenate([f1[0, e, 384:400, 0:128].astype(F32)[0:1] for e in range(8)], axis=1)
         dn1 = da1 * gain
-        grad_tokens[b] = mid[b] + factor * (dn1 - n1 * jnp.mean(dn1 * n1, axis=1, keepdims=True))
+        grad[b] = mid[b] + factor * (dn1 - n1 * jnp.mean(dn1 * n1, axis=1, keepdims=True))
         for m in range(4):
-            grad_first[b, :, m * CHUNK : (m + 1) * CHUNK] = d_rows[b, m, :, 512:768].astype(F32)
+            first[b, :, m * CHUNK : (m + 1) * CHUNK] = d_rows[b, m, :, 512:768].astype(F32)
         return total
 
     def gain_copy(i, device):
         return remote(gbuf.at[0] if i == 0 else gbuf.at[4 + i], gbuf.at[1 + i], s_gain.at[i], r_gain.at[i], device)
 
     a, b, c, e = ORDER
-    weight_grad(a)
-    cross.begin(a)
-    cross.load(a)
-    along2(a)
-    weight_grad(b)
-    cross.begin(b)
-    cross.load(b)
-    along2(b)
+    moves.wait(got_total)
+    chain2.level(0)
+    for i in got_d:
+        moves.wait(i)
+    for m in ORDER:
+        weight_grad(m)
+        cross.begin(m)
     cross.join(a)
-    weight_grad(c)
-    cross.begin(c)
-    cross.load(c)
-    along2(c)
     cross.join(b)
-    weight_grad(e)
-    cross.begin(e)
-    cross.load(e)
-    along2(e)
+    cross.join(c)
+    cross.join(e)
+    chain2.level(1)
     cross.relay(a)
     cross.relay(b)
-    cross.join(c)
-    cross.join(e)
+    moves.wait(got_f1)
     input_grad(0)
     cross.relay(c)
     cross.relay(e)
+    input_grad(1)
     cross.total(a)
-    chain1.along(a)
-    input_grad(1)
     cross.total(b)
-    chain1.along(b)
     input_grad(2)
+    chain2.level(2)
     input_grad(3)
     cross.total(c)
-    chain1.along(c)
     cross.total(e)
-    chain1.along(e)
+    chain1.level(0)
+    for i in got_x:
+        moves.wait(i)
     total = lax.fori_loop(0, 3, leave, jnp.zeros((1, 1024), F32))
+    moves.start(grad, grad_tokens)
+    moves.start(first, grad_first)
     row = lax.broadcasted_iota(jnp.int32, (8, 1024), 0)
     gbuf[0] = jnp.where(row == 0, total, gain_part[...])
     gain_copy(0, p.core).start()
-    chain2.last()
+    chain1.level(1)
     gain_copy(0, p.core).wait_recv()
     gbuf[5] = gbuf[0] + gbuf[1]
     gain_copy(1, p.x).start()
-    chain1.last()
+    chain2.last()
     gain_copy(1, p.x).wait_recv()
     gbuf[6] = gbuf[5] + gbuf[2]
     gain_copy(2, p.y).start()
+    chain1.level(2)
     gain_copy(2, p.y).wait_recv()
     gbuf[7] = gbuf[6] + gbuf[3]
     for step in (1, 2, 3):
         m = p.peer(step)
         remote(gbuf.at[7], gbuf.at[8 + p.z], s_gain.at[2 + step], r_gain.at[3 + p.z], (p.d, m)).start()
     gbuf[8 + p.z] = gbuf[7]
+    chain1.last()
     for step in (1, 2, 3):
         m = p.peer(step)
         remote(gbuf.at[7], gbuf.at[8 + m], s_gain.at[2 + step], r_gain.at[3 + m], (p.d, m)).wait_recv()
@@ -1429,13 +1473,17 @@
     for step in (1, 2, 3):
         m = p.peer(step)
         remote(gbuf.at[7], gbuf.at[8 + m], s_gain.at[2 + step], r_gain.at[3 + m], (p.d, m)).wait_send()
+    for m in range(4):
+        cross.core_sent(m)
     cross.finish()
     chain1.finish()
     chain2.finish()
+    moves.rest()
 
 
 def run_finish(*args):
     vmem = pl.BlockSpec(memory_space=pltpu.VMEM)
+    hbm = pl.BlockSpec(memory_space=pl.ANY)
     dma = pltpu.SemaphoreType.DMA
     shape = jax.ShapeDtypeStruct
     return pl.pallas_call(
@@ -1447,9 +1495,16 @@
             shape((PIECE, 128), F32),
             shape((8, 1024), F32),
         ),
-        in_specs=[vmem] * (len(args) - 1) + [pl.BlockSpec(memory_space=pl.ANY)],
-        out_specs=(vmem,) * 5,
+        in_specs=[vmem] + [hbm] * (len(args) - 1),
+        out_specs=(hbm, hbm, vmem, vmem, vmem),
         scratch_shapes=[
+            pltpu.VMEM((3, CHUNK, 1024), BF),
+            pltpu.VMEM((3, CHUNK, 1024), F32),
+            pltpu.VMEM((3, 4, CHUNK, 768), BF),
+            pltpu.VMEM((1024, 768), BF),
+            pltpu.VMEM((4, 8, QROWS, CHUNK), BF),
+            pltpu.VMEM((3, CHUNK, 1024), F32),
+            pltpu.VMEM((3, CHUNK, 1024), F32),
             pltpu.VMEM((4, 8, 128, 768), BF),
             pltpu.VMEM((768, 1024), F32),
             pltpu.VMEM((4, 128, 768), BF),
@@ -1459,9 +1514,9 @@
         + crossing_scratch(128, 768)
         + chain_scratch(128, 768)
         + chain_scratch(PIECE, 128)
-        + [dma((6,)), dma((7,)), dma((4,))],
+        + [dma((6,)), dma((7,)), dma((8,))],
         compiler_params=pltpu.CompilerParams(
-            collective_id=3, has_side_effects=True, vmem_limit_bytes=60 * 2**20
+            collective_id=3, has_side_effects=True, vmem_limit_bytes=62 * 2**20
         ),
         cost_estimate=pl.CostEstimate(flops=10**10, bytes_accessed=5 * 10**7, transcendentals=0),
         name="sum_grads",
@@ -1474,13 +1529,14 @@
 ):
     seq = sequences[:, 0]
     cos_t, sin_t = rope_tables()
-    f1, f2, qkv, o_head, lse, o_rows, a1_t, gain_out = run_forward(
-        seq, tokens, first_values, w_query, w_key, w_value, w_out, w_gate.T, w_up.T, w_down.T,
-        gain_attn[None, :], gain_mlp[None, :], cos_t, sin_t,
+    (_, acts, f1, qkv, o_head, lse, o_rows, a1_t, a2, dattn, mid, layer_out, do_head, do_last, gain_part) = run_forward(
+        seq, w_query, w_key, w_value, w_out, w_gate.T, w_up.T, w_down.T,
+        gain_attn[None, :], gain_mlp[None, :], cos_t, sin_t, tokens, first_values, cotangent,
     )
-    layer_out, mid, do_rows, part, gain_part = run_mlp(tokens, cotangent, o_rows, f2, gain_out)
-    d_rows, summed = run_backward(seq, do_rows, qkv, o_head, lse, cos_t, sin_t, part)
-    grad_tokens, grad_first, dw1, dw2, gain_sum = run_finish(tokens, mid, d_rows, a1_t, f1, gain_part, summed)
+    d_rows, summed = run_backward(
+        seq, cos_t, sin_t, do_last, do_head, qkv, o_head, lse, o_rows, a2, dattn, cotangent, acts
+    )
+    grad_tokens, grad_first, dw1, dw2, gain_sum = run_finish(gain_part, tokens, mid, d_rows, a1_t, f1, summed)
     place = (lax.axis_index("dp") * 4 + lax.axis_index("mp")) * 32
     gain_mine = lax.dynamic_slice(gain_sum, (0, place), (2, 32))
     return (

time: 613 us -> 456 us (0.74)
  Pallas kernels: 597 us -> 435 us
    pallas_call x1, Pallas kernels: 184 us -> 120 us  [run_backward(): pl.pallas_call(backward_kernel, out_shape=(shape((3, 4, CHUNK, 768), BF),...]
    pallas_call x1, Pallas kernels: 118 us -> 64.4 us  [run_finish(): pl.pallas_call(finish_kernel, out_shape=(shape((3, CHUNK, 1024), F32), sh...]
    pallas_call x2 -> x1, Pallas kernels: 295 us -> 250 us  [run_forward(): pl.pallas_call(forward_kernel, out_shape=(shape((4, 8, PIECE, 128), BF),...]
where the time goes in v3:
time: 456 us; the launch traced here: 449 us
  Pallas kernels  435 us (95%)
  local copies, waits for them, and re-layouts  13.2 us (3%)
    pallas_call x1, Pallas kernels, run_forward(): pl.pallas_call(forward_kernel, out_shape=(shape((4, 8, PIECE, 128), BF),...  250 us
    pallas_call x1, Pallas kernels, run_backward(): pl.pallas_call(backward_kernel, out_shape=(shape((3, 4, CHUNK, 768), BF),...  120 us
    pallas_call x1, Pallas kernels, run_finish(): pl.pallas_call(finish_kernel, out_shape=(shape((3, CHUNK, 1024), F32), sh...  64.4 us

profile of v3, /device:TPU:0, one launch (start us, length us, event | category | flops | bytes accessed | tf_op | source)
XLA Modules:
  0.0 449.0 jit_solution(12047998569049036006)
XLA Ops:
  0.6 250.4 %gather_forward.1 = (bf16[4,8,2368,128]{3,2,1,0:T(8,128)(2,1)}, bf16[3,4,768,704]{3,2,1,0:T(8,128)(2,1)}, bf16[4,8,400,256]{3,2,1,0:T(8,128)(2,1)}, bf16[3,3,102...) custom-call(s32[3]{0:T(128)} %bitcast.23, ...), custom_call_target="tpu_custom_call" | custom-call | flops 49999998976 | bytes 60000000 | tf_op jit(solution)/shard_map/gather_forward/pallas_call | solution.py:1081
  251.0 119.9 %attend_back.1 = (bf16[3,4,256,768]{3,2,1,0:T(8,128)(2,1)}, bf16[4,2368,128]{2,1,0:T(8,128)(2,1)}) custom-call(s32[3]{0:T(128)} %bitcast.24, f32[1024,128]{1,0:T(8,128)} %constant.21.clone.cos_t, f32[1024,128]{1,0:T(8,128)} %constant.22.clone.sin_t, bf16[4,256,256]{2,1,0:T(8,128)(2,1)} %get-tuple-element.36.do_last, ...), custom_call_target="tpu_custom_call" | custom-call | flops 40000000000 | bytes 40000000 | tf_op jit(solution)/shard_map/attend_back/pallas_call | solution.py:1316
  371.0 64.4 %sum_grads.1 = (f32[3,256,1024]{2,1,0:T(8,128)}, f32[3,256,1024]{2,1,0:T(8,128)}, f32[128,768]{1,0:T(8,128)}, f32[2368,128]{1,0:T(8,128)}, f32[8,1024]{1,0:T(8,128)}) custom-call(f32[8,1024]{1,0:T(8,128)} %get-tuple-element.34.gain_part, bf16[3,256,1024]{2,1,0:T(8,128)(2,1)} %tok_in.3, f32[3,256,1024]{2,1,0:T(8,128)} %get-tuple-element.35.mid_in, ...), custom_call_target="tpu_custom_call" | custom-call | flops 10000000000 | bytes 50000000 | tf_op jit(solution)/shard_map/sum_grads/pallas_call | solution.py:1489
  435.4 0.0 copy-start.3
  435.4 0.0 copy-start.2
  435.4 2.3 slice_bitcast_fusion
  437.8 0.0 copy-done.3
  437.8 0.8 fusion
  438.5 0.9 slice_bitcast_fusion.3
  439.4 0.8 copy.27
  440.2 0.7 constant_dynamic-slice_fusion
  440.9 0.5 slice_bitcast_fusion.4
  441.5 0.0 copy-done.2
  441.5 0.0 copy-start.1
  441.5 1.1 copy.31
  442.6 1.3 copy-done.1
  443.9 0.0 copy-start
  443.9 1.7 copy.32
  445.6 1.4 copy-done
  446.9 1.7 copy.33
Async XLA Ops:
  435.4 2.4 copy-start.3
  435.4 6.0 %copy-start.2 = (bf16[3,256,1024]{2,1,0:T(8,128)(2,1)S(1)}, bf16[3,256,1024]{2,1,0:T(8,128)(2,1)}, u32[]{:S(2)}) copy-start(bf16[3,256,1024]{2,1,0:T(8,128)(2,1)} %get-tuple-element.86) | copy-start | bytes 4718596
  441.5 2.5 copy-start.1
  443.9 3.0 copy-start

commit v4 on v3

--- a/solution.py
+++ b/solution.py
@@ -780,12 +780,10 @@
     p.hop(1, arrive(g1))
     side(g1)(z)
     p.hop(2, arrive(g1))
+    g2.along_z(z, p2)
     p.hop(1, side(g1))
     g1.diag_in(z)
     p.hop(3, arrive(g1))
-    g2.along_z(z, p2)
-    p.hop(2, side(g1))
-    p.hop(1, g1.diag_in)
     g1.core_in(z)
 
     gain_row = jnp.concatenate([f1[z, e, 384:400, :].astype(F32)[0:8] for e in range(8)], axis=1)
@@ -804,13 +802,17 @@
 
     lax.fori_loop(0, 3, norm_body, 0)
 
+    p.hop(2, side(g1))
+    p.hop(1, g1.diag_in)
     p.hop(3, side(g1))
     p.hop(2, g1.diag_in)
+    p.hop(1, g2.z_in)
     p.hop(1, g1.core_in)
     p.hop(3, g1.diag_in)
     p.hop(2, g1.core_in)
     p.hop(3, g1.core_in)
     g2.spread(z, p2)
+    p.hop(1, g2.spread)
     moves.start(f1, f1_out)
     moves.wait(got_fv)
 
@@ -931,6 +933,11 @@
         return remote(
             do_rows.at[b, m], do_head.at[b, block(z), :], s_do.at[b, step - 1], r_do.at[b, z], (d, m)
         )
+
+    def send_do(b):
+        for step in (1, 2, 3):
+            do_copy(b, step).start()
+        do_head[b, block(z), :] = do_rows[b, z]
 
     def mlp_rows(b):
         rows = slice(b * CHUNK, (b + 1) * CHUNK)
@@ -993,10 +1000,6 @@
             return carry
 
         lax.fori_loop(0, 4, heads, 0)
-        if b < 2:
-            for step in (1, 2, 3):
-                do_copy(b, step).start()
-            do_head[b, block(z), :] = do_rows[b, z]
         moves.start(mid.at[b], mid_out.at[b])
         moves.start(y_out.at[b], layer_out.at[b])
 
@@ -1006,18 +1009,17 @@
         moves.start(o_head.at[b], o_out.at[b])
         moves.start(lse.at[b], lse_out.at[b])
 
-    for b in range(3):
-        project(b)
-        if b == 0:
-            send_qkv(0)
+    project(0)
+    send_qkv(0)
+    p.hop(2, arrive(g2))
+    project(1)
+    project(2)
     a1_t[...] = a1[...].T
     moves.start(a1_t, a1t_out)
-    p.hop(1, arrive(g2))
-    p.hop(2, arrive(g2))
+    p.hop(3, arrive(g2))
     side(g2)(z)
     sent_qkv(0)
     send_qkv(1)
-    p.hop(3, arrive(g2))
     p.hop(1, side(g2))
     g2.diag_in(z)
     take_qkv(0)
@@ -1040,11 +1042,13 @@
     moves.wait(got_cot)
     take_o(0)
     mlp_rows(0)
+    take_o(1)
+    mlp_rows(1)
     take_qkv(2)
     moves.start(qkv.at[2], qkv_out.at[2])
     attend_all(2)
-    take_o(1)
-    mlp_rows(1)
+    send_do(0)
+    send_do(1)
     take_o(2)
     moves.start(o_rows, rows_out)
     mlp_rows(2)

time: 456 us -> 446 us (0.978)
  Pallas kernels: 435 us -> 424 us
    pallas_call x1, Pallas kernels: 250 us -> 237 us  [run_forward(): pl.pallas_call(forward_kernel, out_shape=(shape((4, 8, PIECE, 128), BF),...]
where the time goes in v4:
time: 446 us; the launch traced here: 439 us
  Pallas kernels  424 us (95%)
  local copies, waits for them, and re-layouts  13.2 us (3%)
    pallas_call x1, Pallas kernels, run_forward(): pl.pallas_call(forward_kernel, out_shape=(shape((4, 8, PIECE, 128), BF),...  237 us
    pallas_call x1, Pallas kernels, run_backward(): pl.pallas_call(backward_kernel, out_shape=(shape((3, 4, CHUNK, 768), BF),...  121 us
    pallas_call x1, Pallas kernels, run_finish(): pl.pallas_call(finish_kernel, out_shape=(shape((3, CHUNK, 1024), F32), sh...  65.9 us

profile of v4, /device:TPU:0, one launch (start us, length us, event | category | flops | bytes accessed | tf_op | source)
XLA Modules:
  0.0 438.5 jit_solution(8336764882986063534)
XLA Ops:
  0.6 237.4 %gather_forward.1 = (bf16[4,8,2368,128]{3,2,1,0:T(8,128)(2,1)}, bf16[3,4,768,704]{3,2,1,0:T(8,128)(2,1)}, bf16[4,8,400,256]{3,2,1,0:T(8,128)(2,1)}, bf16[3,3,102...) custom-call(s32[3]{0:T(128)} %bitcast.23, ...), custom_call_target="tpu_custom_call" | custom-call | flops 49999998976 | bytes 60000000 | tf_op jit(solution)/shard_map/gather_forward/pallas_call | solution.py:1085
  238.0 120.9 %attend_back.1 = (bf16[3,4,256,768]{3,2,1,0:T(8,128)(2,1)}, bf16[4,2368,128]{2,1,0:T(8,128)(2,1)}) custom-call(s32[3]{0:T(128)} %bitcast.24, f32[1024,128]{1,0:T(8,128)} %constant.21.clone.cos_t, f32[1024,128]{1,0:T(8,128)} %constant.22.clone.sin_t, bf16[4,256,256]{2,1,0:T(8,128)(2,1)} %get-tuple-element.36.do_last, ...), custom_call_target="tpu_custom_call" | custom-call | flops 40000000000 | bytes 40000000 | tf_op jit(solution)/shard_map/attend_back/pallas_call | solution.py:1320
  359.0 65.9 %sum_grads.1 = (f32[3,256,1024]{2,1,0:T(8,128)}, f32[3,256,1024]{2,1,0:T(8,128)}, f32[128,768]{1,0:T(8,128)}, f32[2368,128]{1,0:T(8,128)}, f32[8,1024]{1,0:T(8,128)}) custom-call(f32[8,1024]{1,0:T(8,128)} %get-tuple-element.34.gain_part, bf16[3,256,1024]{2,1,0:T(8,128)(2,1)} %tok_in.3, f32[3,256,1024]{2,1,0:T(8,128)} %get-tuple-element.35.mid_in, ...), custom_call_target="tpu_custom_call" | custom-call | flops 10000000000 | bytes 50000000 | tf_op jit(solution)/shard_map/sum_grads/pallas_call | solution.py:1493
  424.9 0.0 copy-start.3
  424.9 0.0 copy-start.2
  424.9 2.3 slice_bitcast_fusion
  427.2 0.0 copy-done.3
  427.2 0.8 fusion
  428.0 0.9 slice_bitcast_fusion.3
  428.9 0.8 copy.27
  429.6 0.7 constant_dynamic-slice_fusion
  430.4 0.5 slice_bitcast_fusion.4
  430.9 0.0 copy-done.2
  430.9 0.0 copy-start.1
  430.9 1.1 copy.31
  432.1 1.3 copy-done.1
  433.4 0.0 copy-start
  433.4 1.7 copy.32
  435.0 1.4 copy-done
  436.4 1.7 copy.33
Async XLA Ops:
  424.9 2.4 copy-start.3
  424.9 6.0 %copy-start.2 = (bf16[3,256,1024]{2,1,0:T(8,128)(2,1)S(1)}, bf16[3,256,1024]{2,1,0:T(8,128)(2,1)}, u32[]{:S(2)}) copy-start(bf16[3,256,1024]{2,1,0:T(8,128)(2,1)} %get-tuple-element.86) | copy-start | bytes 4718596
  430.9 2.5 copy-start.1
  433.4 3.0 copy-start

commit v5 on v4

--- a/solution.py
+++ b/solution.py
@@ -413,7 +413,7 @@
 
     def greet(self):
         barrier = pltpu.get_barrier_semaphore()
-        others = [self.core, self.x, self.y] + [(self.d, self.peer(s)) for s in (1, 2, 3)]
+        others = [self.core, self.x, self.y, (self.dxy, self.z)] + [(self.d, self.peer(s)) for s in (1, 2, 3)]
         for other in others:
             pl.semaphore_signal(barrier, inc=1, device_id=other, device_id_type=MESH)
         pl.semaphore_wait(barrier, len(others))
@@ -492,6 +492,9 @@
         for d in self.p.core_quads:
             self.take(m, d)
 
+    def second(self, m):
+        return (self.sx if m % 2 else self.sy).at[4 + m]
+
     def finish(self):
         p = self.p
 
@@ -510,9 +513,28 @@
 
             sent(self.sx.at[m], p.core)
             sent(self.sy.at[m], p.core)
-            sent((self.sx if m % 2 else self.sy).at[4 + m], p.core)
+            sent(self.second(m), p.core)
             for q in range(4):
                 sent(self.sc.at[4 * q + m], p.core)
+
+
+class Direct(Gather):
+    def spread(self, m, src=None):
+        p = self.p
+        src = self.at(m, p.d) if src is None else src
+        super().spread(m, src)
+        self.send(src, m, p.d, self.sx.at[4 + m], (p.dxy, p.z))
+
+    def x_in(self, m):
+        self.take(m, self.p.dx)
+        self.send(self.at(m, self.p.dx), m, self.p.dx, self.sc.at[4 + m], self.p.core)
+
+    def y_in(self, m):
+        self.take(m, self.p.dy)
+        self.send(self.at(m, self.p.dy), m, self.p.dy, self.sc.at[8 + m], self.p.core)
+
+    def second(self, m):
+        return self.sx.at[4 + m]
 
 
 def gather_sems():
@@ -756,7 +778,7 @@
     f1[z, d, 384:400, 0:128] = jnp.broadcast_to(gain_attn[...], (16, 128))
     f1[z, d, 384:400, 128:256] = jnp.broadcast_to(gain_mlp[...], (16, 128))
     g1 = Gather(p, lambda m, e: f1.at[m, e], f1.at[0, 0], g1s)
-    g2 = Gather(p, lambda m, e: f2.at[m, e], p2, g2s)
+    g2 = Direct(p, lambda m, e: f2.at[m, e], p2, g2s)
     g1.along_z(z)
     g1.spread(z)
     for i, source in enumerate((wg_t, wu_t, wd_t)):
@@ -1017,23 +1039,39 @@
     a1_t[...] = a1[...].T
     moves.start(a1_t, a1t_out)
     p.hop(3, arrive(g2))
-    side(g2)(z)
-    sent_qkv(0)
     send_qkv(1)
-    p.hop(1, side(g2))
-    g2.diag_in(z)
     take_qkv(0)
     moves.start(qkv.at[0], qkv_out.at[0])
-    attend_all(0)
-    p.hop(2, side(g2))
-    p.hop(1, g2.diag_in)
-    sent_qkv(1)
     send_qkv(2)
+    attend(0, 0)
+    attend(0, 1)
+    attend(0, 2)
+    attend(0, 3)
+    moves.start(o_head.at[0], o_out.at[0])
+    moves.start(lse.at[0], lse_out.at[0])
+    side(g2)(z)
+    p.hop(1, side(g2))
     take_qkv(1)
     moves.start(qkv.at[1], qkv_out.at[1])
-    attend_all(1)
+    attend(1, 0)
+    attend(1, 1)
+    g2.diag_in(z)
+    attend(1, 2)
+    attend(1, 3)
+    p.hop(2, side(g2))
+    moves.start(o_head.at[1], o_out.at[1])
+    moves.start(lse.at[1], lse_out.at[1])
+    p.hop(1, g2.diag_in)
+    take_qkv(2)
+    moves.start(qkv.at[2], qkv_out.at[2])
+    attend(2, 0)
+    attend(2, 1)
+    p.hop(2, g2.diag_in)
+    attend(2, 2)
+    attend(2, 3)
     p.hop(3, side(g2))
-    p.hop(2, g2.diag_in)
+    moves.start(o_head.at[2], o_out.at[2])
+    moves.start(lse.at[2], lse_out.at[2])
     p.hop(3, g2.diag_in)
     for m in range(4):
         g2.core_in(m)
@@ -1042,12 +1080,9 @@
     moves.wait(got_cot)
     take_o(0)
     mlp_rows(0)
+    send_do(0)
     take_o(1)
     mlp_rows(1)
-    take_qkv(2)
-    moves.start(qkv.at[2], qkv_out.at[2])
-    attend_all(2)
-    send_do(0)
     send_do(1)
     take_o(2)
     moves.start(o_rows, rows_out)
@@ -1064,6 +1099,8 @@
         moves.start(do_head.at[b], do_out.at[b])
     act_copy(2, 2, 0).wait()
     act_copy(2, 3, 1).wait()
+    sent_qkv(0)
+    sent_qkv(1)
     sent_qkv(2)
     for b in range(3):
         for i in range(4):

time: 446 us -> 437 us (0.980)
  Pallas kernels: 424 us -> 414 us
    pallas_call x1, Pallas kernels: 237 us -> 221 us  [run_forward(): pl.pallas_call(forward_kernel, out_shape=(shape((4, 8, PIECE, 128), BF),...]
    pallas_call x1, Pallas kernels: 121 us -> 130 us  [run_backward(): pl.pallas_call(backward_kernel, out_shape=(shape((3, 4, CHUNK, 768), BF),...]
where the time goes in v5:
time: 437 us; the launch traced here: 429 us
  Pallas kernels  414 us (95%)
  local copies, waits for them, and re-layouts  13.2 us (3%)
    pallas_call x1, Pallas kernels, run_forward(): pl.pallas_call(forward_kernel, out_shape=(shape((4, 8, PIECE, 128), BF),...  221 us
    pallas_call x1, Pallas kernels, run_backward(): pl.pallas_call(backward_kernel, out_shape=(shape((3, 4, CHUNK, 768), BF),...  130 us
    pallas_call x1, Pallas kernels, run_finish(): pl.pallas_call(finish_kernel, out_shape=(shape((3, CHUNK, 1024), F32), sh...  63.7 us

profile of v5, /device:TPU:0, one launch (start us, length us, event | category | flops | bytes accessed | tf_op | source)
XLA Modules:
  0.0 428.6 jit_solution(13891567073431647214)
XLA Ops:
  0.6 220.9 %gather_forward.1 = (bf16[4,8,2368,128]{3,2,1,0:T(8,128)(2,1)}, bf16[3,4,768,704]{3,2,1,0:T(8,128)(2,1)}, bf16[4,8,400,256]{3,2,1,0:T(8,128)(2,1)}, bf16[3,3,102...) custom-call(s32[3]{0:T(128)} %bitcast.23, ...), custom_call_target="tpu_custom_call" | custom-call | flops 49999998976 | bytes 60000000 | tf_op jit(solution)/shard_map/gather_forward/pallas_call | solution.py:1122
  221.6 129.7 %attend_back.1 = (bf16[3,4,256,768]{3,2,1,0:T(8,128)(2,1)}, bf16[4,2368,128]{2,1,0:T(8,128)(2,1)}) custom-call(s32[3]{0:T(128)} %bitcast.24, f32[1024,128]{1,0:T(8,128)} %constant.21.clone.cos_t, f32[1024,128]{1,0:T(8,128)} %constant.22.clone.sin_t, bf16[4,256,256]{2,1,0:T(8,128)(2,1)} %get-tuple-element.36.do_last, ...), custom_call_target="tpu_custom_call" | custom-call | flops 40000000000 | bytes 40000000 | tf_op jit(solution)/shard_map/attend_back/pallas_call | solution.py:1357
  351.3 63.7 %sum_grads.1 = (f32[3,256,1024]{2,1,0:T(8,128)}, f32[3,256,1024]{2,1,0:T(8,128)}, f32[128,768]{1,0:T(8,128)}, f32[2368,128]{1,0:T(8,128)}, f32[8,1024]{1,0:T(8,128)}) custom-call(f32[8,1024]{1,0:T(8,128)} %get-tuple-element.34.gain_part, bf16[3,256,1024]{2,1,0:T(8,128)(2,1)} %tok_in.3, f32[3,256,1024]{2,1,0:T(8,128)} %get-tuple-element.35.mid_in, ...), custom_call_target="tpu_custom_call" | custom-call | flops 10000000000 | bytes 50000000 | tf_op jit(solution)/shard_map/sum_grads/pallas_call | solution.py:1530
  415.0 0.0 copy-start.3
  415.0 0.0 copy-start.2
  415.0 2.3 slice_bitcast_fusion
  417.3 0.0 copy-done.3
  417.3 0.8 fusion
  418.1 0.9 slice_bitcast_fusion.3
  419.0 0.8 copy.27
  419.7 0.7 constant_dynamic-slice_fusion
  420.5 0.5 slice_bitcast_fusion.4
  421.0 0.0 copy-done.2
  421.0 0.0 copy-start.1
  421.0 1.1 copy.31
  422.2 1.3 copy-done.1
  423.5 0.0 copy-start
  423.5 1.7 copy.32
  425.1 1.4 copy-done
  426.5 1.7 copy.33
Async XLA Ops:
  415.0 2.4 copy-start.3
  415.0 6.0 %copy-start.2 = (bf16[3,256,1024]{2,1,0:T(8,128)(2,1)S(1)}, bf16[3,256,1024]{2,1,0:T(8,128)(2,1)}, u32[]{:S(2)}) copy-start(bf16[3,256,1024]{2,1,0:T(8,128)(2,1)} %get-tuple-element.86) | copy-start | bytes 4718596
  421.0 2.5 copy-start.1
  423.5 3.0 copy-start

commit v6 on v5

--- a/solution.py
+++ b/solution.py
@@ -827,13 +827,13 @@
     p.hop(2, side(g1))
     p.hop(1, g1.diag_in)
     p.hop(3, side(g1))
+    g2.spread(z, p2)
     p.hop(2, g1.diag_in)
     p.hop(1, g2.z_in)
     p.hop(1, g1.core_in)
     p.hop(3, g1.diag_in)
     p.hop(2, g1.core_in)
     p.hop(3, g1.core_in)
-    g2.spread(z, p2)
     p.hop(1, g2.spread)
     moves.start(f1, f1_out)
     moves.wait(got_fv)
@@ -1040,17 +1040,17 @@
     moves.start(a1_t, a1t_out)
     p.hop(3, arrive(g2))
     send_qkv(1)
+    side(g2)(z)
     take_qkv(0)
     moves.start(qkv.at[0], qkv_out.at[0])
     send_qkv(2)
+    p.hop(1, side(g2))
     attend(0, 0)
     attend(0, 1)
     attend(0, 2)
     attend(0, 3)
     moves.start(o_head.at[0], o_out.at[0])
     moves.start(lse.at[0], lse_out.at[0])
-    side(g2)(z)
-    p.hop(1, side(g2))
     take_qkv(1)
     moves.start(qkv.at[1], qkv_out.at[1])
     attend(1, 0)

time: 437 us -> 437 us (level)
  no operation moved by 1% of the time
where the time goes in v6:
time: 437 us; the launch traced here: 429 us
  Pallas kernels  414 us (95%)
  local copies, waits for them, and re-layouts  13.2 us (3%)
    pallas_call x1, Pallas kernels, run_forward(): pl.pallas_call(forward_kernel, out_shape=(shape((4, 8, PIECE, 128), BF),...  221 us
    pallas_call x1, Pallas kernels, run_backward(): pl.pallas_call(backward_kernel, out_shape=(shape((3, 4, CHUNK, 768), BF),...  130 us
    pallas_call x1, Pallas kernels, run_finish(): pl.pallas_call(finish_kernel, out_shape=(shape((3, CHUNK, 1024), F32), sh...  63.7 us

profile of v6, /device:TPU:0, one launch (start us, length us, event | category | flops | bytes accessed | tf_op | source)
XLA Modules:
  0.0 428.6 jit_solution(3956625087720927478)
XLA Ops:
  0.6 220.9 %gather_forward.1 = (bf16[4,8,2368,128]{3,2,1,0:T(8,128)(2,1)}, bf16[3,4,768,704]{3,2,1,0:T(8,128)(2,1)}, bf16[4,8,400,256]{3,2,1,0:T(8,128)(2,1)}, bf16[3,3,102...) custom-call(s32[3]{0:T(128)} %bitcast.23, ...), custom_call_target="tpu_custom_call" | custom-call | flops 49999998976 | bytes 60000000 | tf_op jit(solution)/shard_map/gather_forward/pallas_call | solution.py:1122
  221.6 129.7 %attend_back.1 = (bf16[3,4,256,768]{3,2,1,0:T(8,128)(2,1)}, bf16[4,2368,128]{2,1,0:T(8,128)(2,1)}) custom-call(s32[3]{0:T(128)} %bitcast.24, f32[1024,128]{1,0:T(8,128)} %constant.21.clone.cos_t, f32[1024,128]{1,0:T(8,128)} %constant.22.clone.sin_t, bf16[4,256,256]{2,1,0:T(8,128)(2,1)} %get-tuple-element.36.do_last, ...), custom_call_target="tpu_custom_call" | custom-call | flops 40000000000 | bytes 40000000 | tf_op jit(solution)/shard_map/attend_back/pallas_call | solution.py:1357
  351.3 63.7 %sum_grads.1 = (f32[3,256,1024]{2,1,0:T(8,128)}, f32[3,256,1024]{2,1,0:T(8,128)}, f32[128,768]{1,0:T(8,128)}, f32[2368,128]{1,0:T(8,128)}, f32[8,1024]{1,0:T(8,128)}) custom-call(f32[8,1024]{1,0:T(8,128)} %get-tuple-element.34.gain_part, bf16[3,256,1024]{2,1,0:T(8,128)(2,1)} %tok_in.3, f32[3,256,1024]{2,1,0:T(8,128)} %get-tuple-element.35.mid_in, ...), custom_call_target="tpu_custom_call" | custom-call | flops 10000000000 | bytes 50000000 | tf_op jit(solution)/shard_map/sum_grads/pallas_call | solution.py:1530
  415.0 0.0 copy-start.3
  415.0 0.0 copy-start.2
  415.0 2.3 slice_bitcast_fusion
  417.3 0.0 copy-done.3
  417.3 0.8 fusion
  418.1 0.9 slice_bitcast_fusion.3
  419.0 0.8 copy.27
  419.7 0.7 constant_dynamic-slice_fusion
  420.5 0.5 slice_bitcast_fusion.4
  421.0 0.0 copy-done.2
  421.0 0.0 copy-start.1
  421.0 1.1 copy.31
  422.2 1.3 copy-done.1
  423.5 0.0 copy-start
  423.5 1.7 copy.32
  425.1 1.4 copy-done
  426.5 1.7 copy.33
Async XLA Ops:
  415.0 2.4 copy-start.3
  415.0 6.0 %copy-start.2 = (bf16[3,256,1024]{2,1,0:T(8,128)(2,1)S(1)}, bf16[3,256,1024]{2,1,0:T(8,128)(2,1)}, u32[]{:S(2)}) copy-start(bf16[3,256,1024]{2,1,0:T(8,128)(2,1)} %get-tuple-element.86) | copy-start | bytes 4718596
  421.0 2.5 copy-start.1
  423.5 3.0 copy-start
